TPU v7x, 32 devices: a whole 2x2x4 slice. The times are simulated.
32 devices in a mesh: band: 4 (over x, core), pw: 8 (over z, y).
Axes of the slice: x: 2, y: 2, z: 4, core: 2. Of those that a mesh axis runs over, the one named last changes fastest.
Arguments:
- coeffs: bfloat16 [2, 64, 256, 256], P(None, None, ('band', 'pw')), may hold values from -6 to 6
- rotation_matrix: bfloat16 [2, 64, 8], replicated, may hold values from -0.5 to 0.5
- stick_length: int32 [256], replicated, may hold values from 64 to 256
- stick_column: int32 [256], replicated, may hold values from 0 to 65535, as said below
- plane_index: int32 [16], replicated, may hold values from 0 to 255, as said below
- occupation: int32 [8], P('band'), may hold values from 0 to 2
Outputs:
- density: float32 [16, 256, 256], P('pw')
Inputs may be any that keep to these rules, and one draw needn't show every extreme that they name: `stick_column`: distinct column numbers. `plane_index`: distinct plane numbers.
All inputs are finite; a program needn't handle non-finite values.
Results may differ from a plain program's by a relative error of at most 0.003.
Values may be sent and summed in bfloat16 or wider, within the bound.
No kernel may reach another device: no remote copies, remote signals or barrier semaphores. Data moves between devices by JAX's collectives and lax.ppermute only.
A program may use at most 64 MiB of HBM per device.

v0:
```python
import math

import jax
import jax.numpy as jnp
from jax import lax
from jax.sharding import PartitionSpec as P


def tables(grid_len, indices):
    product = jnp.arange(grid_len, dtype=jnp.int32)[:, None] * indices[None, :] % grid_len
    angles = 2.0 * math.pi / grid_len * product.astype(jnp.float32)
    return (jnp.cos(angles).astype(jnp.bfloat16), jnp.sin(angles).astype(jnp.bfloat16))


def contract(form, left, right):
    return jnp.einsum(form, left, right, preferred_element_type=jnp.float32)


def rotate(coeff_part, rotation_matrix):
    in_count = rotation_matrix.shape[1]
    out_count = rotation_matrix.shape[2]
    rotation = jnp.concatenate(
        [
            jnp.concatenate([rotation_matrix[0], rotation_matrix[1]], 1),
            jnp.concatenate([-rotation_matrix[1], rotation_matrix[0]], 1),
        ],
        0,
    )
    flattened = coeff_part.reshape(2 * in_count, -1)
    result = jnp.dot(rotation.T, flattened, preferred_element_type=jnp.float32)
    return result.reshape((2, out_count) + coeff_part.shape[2:]).astype(jnp.bfloat16)


def z_transform(rotated, lengths, plane_index):
    grid_len = rotated.shape[3]
    count = plane_index.shape[0]
    live_mask = (jnp.arange(grid_len, dtype=jnp.int32)[None, :] < lengths[:, None]).astype(
        jnp.bfloat16
    )
    masked = rotated * live_mask
    cos_table, sin_table = tables(grid_len, plane_index)
    weight = jnp.concatenate(
        [jnp.concatenate([cos_table, sin_table], 1), jnp.concatenate([-sin_table, cos_table], 1)], 0
    )
    stacked = jnp.concatenate([masked[0], masked[1]], axis=-1)
    amplitude = contract("bsj,jk->bsk", stacked, weight)
    amp_real = amplitude[..., :count]
    amp_imag = amplitude[..., count:]
    shift = (lengths // 2)[:, None] * plane_index[None, :] % grid_len
    phase = -2.0 * math.pi / grid_len * shift.astype(jnp.float32)
    phase_cos = jnp.cos(phase)
    phase_sin = jnp.sin(phase)
    out_real = amp_real * phase_cos - amp_imag * phase_sin
    out_imag = amp_real * phase_sin + amp_imag * phase_cos
    result = jnp.stack([out_real, out_imag])
    return jnp.swapaxes(result, 2, 3).astype(jnp.bfloat16)


def plane_power(values, columns, grid_len):
    shape = values.shape
    pairs = jnp.moveaxis(values.reshape(2, shape[1] * shape[2], shape[3]), 1, 0)
    cos_table, sin_table = tables(grid_len, jnp.arange(grid_len, dtype=jnp.int32))

    def one_plane(stick_values):
        flattened = (
            jnp.zeros((2, grid_len * grid_len), jnp.bfloat16).at[:, columns].set(stick_values)
        )
        planes = flattened.reshape(2, grid_len, grid_len)
        half_real = (
            contract("xy,yk->xk", planes[0], cos_table)
            - contract("xy,yk->xk", planes[1], sin_table)
        ).astype(jnp.bfloat16)
        half_imag = (
            contract("xy,yk->xk", planes[0], sin_table)
            + contract("xy,yk->xk", planes[1], cos_table)
        ).astype(jnp.bfloat16)
        wave_real = contract("xq,xk->qk", cos_table, half_real) - contract(
            "xq,xk->qk", sin_table, half_imag
        )
        wave_imag = contract("xq,xk->qk", sin_table, half_real) + contract(
            "xq,xk->qk", cos_table, half_imag
        )
        return wave_real * wave_real + wave_imag * wave_imag

    powers = lax.map(one_plane, pairs)
    return powers.reshape(shape[1], shape[2], grid_len, grid_len)


def shards(coeffs, rotation_matrix, stick_length, stick_column, plane_index, occupation):
    band_count = lax.axis_size("band")
    pw_count = lax.axis_size("pw")
    pw_index = lax.axis_index("pw")
    local_sticks = coeffs.shape[2]
    grid_len = coeffs.shape[3]
    length_table = stick_length.reshape(band_count, pw_count, local_sticks)
    columns = jnp.transpose(
        stick_column.reshape(band_count, pw_count, local_sticks), (1, 0, 2)
    ).reshape(-1)
    rotated = rotate(coeffs, rotation_matrix)
    norm_factor = 1.0 / float(occupation.shape[0] * band_count * stick_column.shape[0] * grid_len)
    grouped = lax.all_to_all(rotated, "band", split_axis=1, concat_axis=2, tiled=True)
    group_lengths = lax.dynamic_index_in_dim(length_table, pw_index, 1, False).reshape(-1)
    z_values = z_transform(grouped, group_lengths, plane_index)
    magnitudes = plane_power(
        lax.all_to_all(z_values, "pw", split_axis=2, concat_axis=3, tiled=True), columns, grid_len
    )
    local_sum = jnp.einsum("b,bzxy->zxy", occupation.astype(jnp.float32), magnitudes) * norm_factor
    return lax.psum(local_sum, "band")


def solution(mesh):
    return jax.shard_map(
        shards,
        mesh=mesh,
        in_specs=(P(None, None, ("band", "pw"), None), P(), P(), P(), P(), P("band")),
        out_specs=P("pw", None, None),
        check_vma=False,
    )
```

profile of v0, /device:TPU:0, one launch (start us, length us, event | category | flops | bytes accessed | tf_op | source)
XLA Modules:
  0.0 239.2 jit_solution(6038612665508422848)
XLA Ops:
  7.9 1.1 copy.27
  10.3 4.2 %all-to-all-start = ((bf16[2,8,8,256]{3,2,0,1:T(8,128)(2,1)}), bf16[2,8,8,256]{3,2,0,1:T(8,128)(2,1)S(1)}, u32[]{:S(2)}, u32[]{:S(2)}) async-start(bf16[2,8,8,256]{3,2,0,1:T(8,128)(2,1)} %copy.19), calls=%async_computation | async-start | bytes 131072 | tf_op jit(solution)/shard_map/all_to_all | solution.py:101
  19.5 6.3 %all-to-all-start.1 = ((bf16[8,2,128]{2,1,0:T(2,128)(2,1)}), bf16[8,2,128]{2,1,0:T(2,128)(2,1)S(1)}, u32[]{:S(2)}, u32[]{:S(2)}) async-start(bf16[8,2,128]{2,1,0:T(2,128)(2,1)} %reshape.198), calls=%async_computation.1 | async-start | bytes 8192 | tf_op jit(solution)/shard_map/all_to_all | solution.py:105
  26.8 5.5 %all-to-all-done.1 = bf16[8,2,128]{2,1,0:T(2,128)(2,1)S(1)} async-done(((bf16[8,2,128]{2,1,0:T(2,128)(2,1)}), bf16[8,2,128]{2,1,0:T(2,128)(2,1)S(1)}, u32[]{:S(2)}, u32[]{:S(2)}) %all-to-all-start.1) | async-done | bytes 4128 | tf_op jit(solution)/shard_map/all_to_all | solution.py:105
  32.7 165.4 %while.12 = (s32[]{:T(128)}, bf16[4,256,256]{1,2,0:T(8,128)(2,1)S(1)}, s32[256]{0:T(256)S(1)}, bf16[4,2,256]{1,2,0:T(8,128)(2,1)S(1)}, s32[]{:T(128)}, /*index=5*/bf16[]{:T(256)}, s32[]{:T(128)}) while((s32[]{:T(128)}, bf16[4,256,256]{1,2,0:T(8,128)(2,1)S(1)}, s32[256]{0:T(256)S(1)}, bf16[4,2,256]{1,2,0:T(8,128)(2,1)S(1)}, ...), condition=%wide.region_2.3_spmd.clone.clone, body=%wide.region_0.2_spmd.clone.clone.sunk | while | flops 276890368 | bytes 5572699 | solution.py:85
  32.7 10.6 %scatter_custom_fusion.6 = bf16[2,65536]{0,1:T(8,128)(2,1)} fusion(s32[256]{0:T(256)S(1)} %bitcast.117, bf16[]{:T(256)} %constant.62.clone.3..sunk, bf16[4,2,256]{1,2,0:T(8,128)(2,1)S(1)} %get-tuple-element.156, s32[]{:T(128)} %get-tuple-element.146, s32[]{:T(128)} %constant.66.clone.1..sunk), kind=kCustom, calls=%fused_computation.5.clone.1 | custom fusion | bytes 327690 | tf_op jit(solution)/shard_map/while/body/eval_jaxpr/scatter | solution.py:66
  43.3 21.5 %slice_reduce_fusion.3 = (bf16[65536]{0:T(1024)(128)(2,1)S(1)}, bf16[65536]{0:T(1024)(128)(2,1)S(1)}) fusion(bf16[2,65536]{0,1:T(8,128)(2,1)} %scatter_custom_fusion.6), kind=kLoop, calls=%fused_computation.3.clone.1 | loop fusion | bytes 524288 | tf_op jit(solution)/shard_map/while/body/eval_jaxpr/slice | solution.py:71
  68.3 1.1 fusion.131
  70.6 1.1 fusion.135
  72.9 1.1 fusion.137
  74.0 10.6 %scatter_custom_fusion.6 = bf16[2,65536]{0,1:T(8,128)(2,1)} fusion(s32[256]{0:T(256)S(1)} %bitcast.117, bf16[]{:T(256)} %constant.62.clone.3..sunk, bf16[4,2,256]{1,2,0:T(8,128)(2,1)S(1)} %get-tuple-element.156, s32[]{:T(128)} %get-tuple-element.146, s32[]{:T(128)} %constant.66.clone.1..sunk), kind=kCustom, calls=%fused_computation.5.clone.1 | custom fusion | bytes 327690 | tf_op jit(solution)/shard_map/while/body/eval_jaxpr/scatter | solution.py:66
  84.6 21.5 %slice_reduce_fusion.3 = (bf16[65536]{0:T(1024)(128)(2,1)S(1)}, bf16[65536]{0:T(1024)(128)(2,1)S(1)}) fusion(bf16[2,65536]{0,1:T(8,128)(2,1)} %scatter_custom_fusion.6), kind=kLoop, calls=%fused_computation.3.clone.1 | loop fusion | bytes 524288 | tf_op jit(solution)/shard_map/while/body/eval_jaxpr/slice | solution.py:71
  111.9 1.1 fusion.135
  114.2 1.1 fusion.137
  115.4 10.6 %scatter_custom_fusion.6 = bf16[2,65536]{0,1:T(8,128)(2,1)} fusion(s32[256]{0:T(256)S(1)} %bitcast.117, bf16[]{:T(256)} %constant.62.clone.3..sunk, bf16[4,2,256]{1,2,0:T(8,128)(2,1)S(1)} %get-tuple-element.156, s32[]{:T(128)} %get-tuple-element.146, s32[]{:T(128)} %constant.66.clone.1..sunk), kind=kCustom, calls=%fused_computation.5.clone.1 | custom fusion | bytes 327690 | tf_op jit(solution)/shard_map/while/body/eval_jaxpr/scatter | solution.py:66
  126.0 21.5 %slice_reduce_fusion.3 = (bf16[65536]{0:T(1024)(128)(2,1)S(1)}, bf16[65536]{0:T(1024)(128)(2,1)S(1)}) fusion(bf16[2,65536]{0,1:T(8,128)(2,1)} %scatter_custom_fusion.6), kind=kLoop, calls=%fused_computation.3.clone.1 | loop fusion | bytes 524288 | tf_op jit(solution)/shard_map/while/body/eval_jaxpr/slice | solution.py:71
  153.2 1.1 fusion.135
  155.5 1.1 fusion.137
  156.7 10.6 %scatter_custom_fusion.6 = bf16[2,65536]{0,1:T(8,128)(2,1)} fusion(s32[256]{0:T(256)S(1)} %bitcast.117, bf16[]{:T(256)} %constant.62.clone.3..sunk, bf16[4,2,256]{1,2,0:T(8,128)(2,1)S(1)} %get-tuple-element.156, s32[]{:T(128)} %get-tuple-element.146, s32[]{:T(128)} %constant.66.clone.1..sunk), kind=kCustom, calls=%fused_computation.5.clone.1 | custom fusion | bytes 327690 | tf_op jit(solution)/shard_map/while/body/eval_jaxpr/scatter | solution.py:66
  167.3 21.5 %slice_reduce_fusion.3 = (bf16[65536]{0:T(1024)(128)(2,1)S(1)}, bf16[65536]{0:T(1024)(128)(2,1)S(1)}) fusion(bf16[2,65536]{0,1:T(8,128)(2,1)} %scatter_custom_fusion.6), kind=kLoop, calls=%fused_computation.3.clone.1 | loop fusion | bytes 524288 | tf_op jit(solution)/shard_map/while/body/eval_jaxpr/slice | solution.py:71
  194.6 1.1 fusion.135
  196.9 1.1 fusion.137
  200.1 30.4 %all-reduce.2.cloned.1.call-done = f32[2,256,256]{2,1,0:T(8,128)} async-done(((f32[2,256,256]{2,1,0:T(8,128)}), f32[2,256,256]{2,1,0:T(8,128)}) %all-reduce.2.cloned.1.call-update) | async-done | bytes 524304 | tf_op jit(solution)/shard_map/psum | solution.py:108
  230.5 1.9 copy.40
  (69 shorter events, 37.2 us)
Async XLA Ops:
  10.3 8.3 %all-to-all-start = ((bf16[2,8,8,256]{3,2,0,1:T(8,128)(2,1)}), bf16[2,8,8,256]{3,2,0,1:T(8,128)(2,1)S(1)}, u32[]{:S(2)}, u32[]{:S(2)}) async-start(bf16[2,8,8,256]{3,2,0,1:T(8,128)(2,1)} %copy.19), calls=%async_computation | async-start | bytes 131072 | tf_op jit(solution)/shard_map/all_to_all | solution.py:101
  19.5 12.7 %all-to-all-start.1 = ((bf16[8,2,128]{2,1,0:T(2,128)(2,1)}), bf16[8,2,128]{2,1,0:T(2,128)(2,1)S(1)}, u32[]{:S(2)}, u32[]{:S(2)}) async-start(bf16[8,2,128]{2,1,0:T(2,128)(2,1)} %reshape.198), calls=%async_computation.1 | async-start | bytes 8192 | tf_op jit(solution)/shard_map/all_to_all | solution.py:105
  25.9 204.6 %all-reduce.2.cloned.1.call-start = ((), (), s32[]{:S(2)}) async-start(), calls=%async_computation.2 | async-start | bytes 1048576 | tf_op jit(solution)/shard_map/psum | solution.py:108
  32.7 165.8 %copy-start = (s32[2]{0:T(128)S(1)}, s32[2]{0:T(128)}, u32[]{:S(2)}) copy-start(s32[2]{0:T(128)} %param.13) | copy-start | bytes 28
Sparse Core Ops, SparseCore 0:
  200.2 30.2 all-reduce.1
where the time goes:
time: 240 us; the launch traced here: 239 us
  local copies, waits for them, and re-layouts  137 us (57%)
  matrix products  37.3 us (16%)
  waiting for transfers between devices  36.7 us (15%)
  between operations  13.5 us (6%)
  starting transfers between devices  10.6 us (4%)
  other arithmetic  4.08 us (2%)
    slice x4, local copies, waits for them, and re-layouts, one_plane(): planes[1]  86 us
    scatter x4, local copies, waits for them, and re-layouts, one_plane(): jnp.zeros((2, grid_len * grid_len), jnp.bfloat16).at[:, columns]  42.4 us
    dot_general x33, matrix products, contract(): return jnp.einsum(form, left, right, preferred_element_type=jnp.float32)  36.3 us
    psum x1, waiting for transfers between devices, shards(): return lax.psum(local_sum, 'band')  30.4 us
    all_to_all x1, starting transfers between devices, shards(): lax.all_to_all(z_values, 'pw', split_axis=2, concat_axis=3, tiled=True)  6.33 us
    all_to_all x1, waiting for transfers between devices, shards(): lax.all_to_all(z_values, 'pw', split_axis=2, concat_axis=3, tiled=True)  5.46 us
  transfers between devices with their start and end apart: 3, of which 3 were waited for; matrix products, arithmetic and copies ran while one was open for 2% of the time, Pallas kernels for 0%

commit v1 on v0

v1 whole, which is shorter than its diff:
```python
import functools
import math

import jax
import jax.numpy as jnp
from jax import lax
from jax.experimental import pallas as pl
from jax.experimental.pallas import tpu as pltpu
from jax.sharding import PartitionSpec as P

LANES = 128


def wrap(value, period):
    if period & (period - 1) == 0:
        return value & (period - 1)
    return lax.rem(value, period)


def cut(value, size):
    if size & (size - 1) == 0:
        return value >> (size.bit_length() - 1)
    return lax.div(value, size)


def cosine(index, period):
    fold = jnp.abs(wrap(index, period) - period // 2) - period // 4
    angle = fold.astype(jnp.float32) * (2.0 * math.pi / period)
    square = angle * angle
    series = -2.39e-08
    for factor in (2.7526e-06, -1.984090e-04, 8.3333315e-03, -1.666666664e-01, 1.0):
        series = series * square + factor
    return angle * series


def sine(index, period):
    return cosine(index + (period - period // 4), period)


def iota(shape, dim):
    return lax.broadcasted_iota(jnp.int32, shape, dim)


def dot_last(left, right):
    return lax.dot_general(
        left, right, (((1,), (1,)), ((), ())), preferred_element_type=jnp.float32
    )


def dot(left, right):
    return jnp.dot(left, right, preferred_element_type=jnp.float32)


def spread(scalars, index, shape):
    result = jnp.full(shape, scalars[0])
    for place, scalar in enumerate(scalars[1:], 1):
        result = jnp.where(index == place, scalar, result)
    return result


def stick_kernel(
    pw_count, length_ref, plane_ref, occupation_ref, rotation_ref, coeff_ref, out_ref, held, sem
):
    in_count, out_count = rotation_ref.shape[1:]
    grid_len = coeff_ref.shape[1]
    sticks = coeff_ref.shape[0] // (2 * in_count)
    plane_count = plane_ref.shape[0]
    own_planes = plane_count // pw_count
    own_bands = occupation_ref.shape[0]
    row_count = 2 * out_count * sticks
    band_index = lax.axis_index("band")
    first_stick = (band_index * pw_count + lax.axis_index("pw")) * sticks
    copy = pltpu.make_async_copy(coeff_ref, held, sem)
    copy.start()

    lengths = [length_ref[first_stick + place] for place in range(sticks)]
    planes = [plane_ref[place] for place in range(plane_count)]

    pick = (
        wrap(cut(iota((row_count, out_count), 0), sticks), out_count)
        == iota((row_count, out_count), 1)
    ).astype(jnp.bfloat16)
    from_real = dot_last(pick, rotation_ref[0])
    from_imag = dot_last(pick, rotation_ref[1])
    is_real = iota((row_count, in_count), 0) < out_count * sticks
    widen = (
        cut(iota((in_count, in_count * sticks), 1), sticks)
        == iota((in_count, in_count * sticks), 0)
    ).astype(jnp.bfloat16)
    shape = (row_count, in_count * sticks)
    same = wrap(iota(shape, 0), sticks) == wrap(iota(shape, 1), sticks)
    mixed = []
    for block in (
        jnp.where(is_real, from_real, from_imag),
        jnp.where(is_real, -from_imag, from_real),
    ):
        wide = dot(block.astype(jnp.bfloat16), widen)
        mixed.append(jnp.where(same, wide, 0.0).astype(jnp.bfloat16))
    rotation = jnp.concatenate(mixed, 1)

    plane_rows = spread(planes, iota((plane_count, grid_len), 0), (plane_count, grid_len))
    product = iota((plane_count, grid_len), 1) * plane_rows
    table = jnp.concatenate([cosine(product, grid_len), sine(product, grid_len)], 0).astype(
        jnp.bfloat16
    )

    shape = (plane_count, row_count)
    lane_lengths = spread(lengths, wrap(iota(shape, 1), sticks), shape)
    shift = (lane_lengths >> 1) * spread(planes, iota(shape, 0), shape)
    phase_cos = cosine(shift, grid_len)
    phase_sin = sine(shift, grid_len)
    real_lane = iota(shape, 1) < row_count // 2

    row_lengths = spread(lengths, iota((sticks, grid_len), 0), (sticks, grid_len))
    live = iota((sticks, grid_len), 1) < row_lengths

    copy.wait()
    rotated = dot(rotation, held[...])
    rotated = rotated.reshape(row_count // sticks, sticks, grid_len)
    rotated = jnp.where(live[None], rotated, 0.0).reshape(row_count, grid_len)
    sums = dot_last(table, rotated.astype(jnp.bfloat16))
    with_cos, with_sin = sums[:plane_count], sums[plane_count:]
    turned = pltpu.roll(with_sin, row_count // 2, 1)
    amplitude = with_cos + jnp.where(real_lane, -turned, turned)
    turned = pltpu.roll(amplitude, row_count // 2, 1) * phase_sin
    values = amplitude * phase_cos + jnp.where(real_lane, turned, -turned)

    lanes = out_ref.shape[2]
    spots = 2 * out_count
    tall = jnp.broadcast_to(values[:, None, :], (plane_count, sticks, row_count))
    own = iota((sticks, row_count), 0) == wrap(iota((sticks, row_count), 1), sticks)
    tall = jnp.where(own[None], tall, 0.0).reshape(plane_count * sticks, row_count)
    shape = (row_count, lanes)
    place = (
        (cut(iota(shape, 0), sticks) == lax.rem(iota(shape, 1), spots))
        & (iota(shape, 1) < own_planes * spots)
    ).astype(jnp.bfloat16)
    laid = dot(tall.astype(jnp.bfloat16), place).reshape(pw_count, own_planes, sticks, lanes)
    mine = cut(iota((own_planes, sticks, lanes), 2), spots) == iota((own_planes, sticks, lanes), 0)
    message = jnp.sum(jnp.where(mine[None], laid, 0.0), 1)
    occupied = jnp.zeros((sticks, lanes), jnp.int32)
    for own_band in range(own_bands):
        lane = own_planes * spots + band_index * own_bands + own_band
        occupied = jnp.where(
            iota((sticks, lanes), 1) == lane, occupation_ref[own_band], occupied
        )
    message = (message + occupied.astype(jnp.float32)[None]).astype(out_ref.dtype)
    for band in range(out_ref.shape[0] // pw_count):
        out_ref[band * pw_count : (band + 1) * pw_count] = message


def table_kernel(grid_len, column_ref, left_ref, right_ref):
    count = column_ref.shape[1]
    columns = column_ref[...]
    freq = iota((grid_len, count), 0)
    turns = freq * cut(columns, grid_len)
    left_ref[0] = cosine(turns, grid_len).astype(jnp.bfloat16)
    left_ref[1] = sine(turns, grid_len).astype(jnp.bfloat16)
    turns = freq * wrap(columns, grid_len)
    cos_table = cosine(turns, grid_len).astype(jnp.bfloat16)
    sin_table = sine(turns, grid_len).astype(jnp.bfloat16)
    right_ref[0, :grid_len] = cos_table
    right_ref[0, grid_len:] = sin_table
    right_ref[1, :grid_len] = -sin_table
    right_ref[1, grid_len:] = cos_table


def plane_kernel(
    bands, own_planes, norm_factor, message_ref, left_ref, right_ref, out_ref, value_ref
):
    chunks = value_ref.shape[0]
    chunk = value_ref.shape[2]
    grid_len = out_ref.shape[1]
    lanes = message_ref.shape[1]
    rows = value_ref.shape[1]
    spots = 2 * bands
    select = (iota((rows + bands, lanes), 0) == iota((rows + bands, lanes), 1)).astype(
        jnp.bfloat16
    )

    def turn(index, peak):
        first = index * chunk
        picked = dot_last(select, message_ref[pl.ds(first, chunk), :])
        value_ref[index] = picked[:rows]
        return jnp.maximum(peak, jnp.max(picked[rows:], 1, keepdims=True))

    peak = jnp.zeros((bands, 1), jnp.float32)
    if chunks == 1:
        peak = turn(0, peak)
    else:
        peak = lax.fori_loop(0, chunks, turn, peak)
    scale = jnp.sqrt(peak)
    for group in range(rows // bands):
        where = slice(group * bands, (group + 1) * bands)
        value_ref[:, where] = value_ref[:, where] * scale[None]

    def partial_wave(index, plane, band):
        lane = pl.ds(index * chunk, chunk) if chunks > 1 else slice(None)
        real = value_ref[index, pl.ds(plane * spots + band, 1), :]
        imag = value_ref[index, pl.ds(plane * spots + bands + band, 1), :]
        cos_table = left_ref[0, :, lane].astype(jnp.float32)
        sin_table = left_ref[1, :, lane].astype(jnp.float32)
        part_real = (cos_table * real - sin_table * imag).astype(jnp.bfloat16)
        part_imag = (sin_table * real + cos_table * imag).astype(jnp.bfloat16)
        return dot_last(part_real, right_ref[0, :, lane]) + dot_last(
            part_imag, right_ref[1, :, lane]
        )

    for plane in range(own_planes):

        def add_band(band, total):
            if chunks == 1:
                wave = partial_wave(0, plane, band)
            else:
                wave = lax.fori_loop(
                    0,
                    chunks,
                    lambda index, so_far: so_far + partial_wave(index, plane, band),
                    jnp.zeros((grid_len, 2 * grid_len), jnp.float32),
                )
            real, imag = wave[:, :grid_len], wave[:, grid_len:]
            out_ref[plane] += real * real + imag * imag
            return total

        out_ref[plane] = jnp.zeros((grid_len, grid_len), jnp.float32)
        lax.fori_loop(0, bands, add_band, 0)
        out_ref[plane] = out_ref[plane] * norm_factor


def shards(coeffs, rotation_matrix, stick_length, stick_column, plane_index, occupation):
    band_count = lax.axis_size("band")
    pw_count = lax.axis_size("pw")
    devices = band_count * pw_count
    in_count, sticks, grid_len = coeffs.shape[1:]
    bands = rotation_matrix.shape[2]
    stick_count = stick_column.shape[0]
    own_planes = plane_index.shape[0] // pw_count
    spots = 2 * bands
    rows = own_planes * spots
    lanes = -(-(rows + bands) // LANES) * LANES
    smem = pl.BlockSpec(memory_space=pltpu.SMEM)
    vmem = pl.BlockSpec(memory_space=pltpu.VMEM)
    room = pltpu.CompilerParams(vmem_limit_bytes=56 * 1024 * 1024)

    messages = pl.pallas_call(
        functools.partial(stick_kernel, pw_count),
        out_shape=jax.ShapeDtypeStruct((devices, sticks, lanes), jnp.bfloat16),
        in_specs=[smem, smem, smem, vmem, pl.BlockSpec(memory_space=pl.ANY)],
        out_specs=vmem,
        scratch_shapes=[
            pltpu.VMEM((2 * in_count * sticks, grid_len), jnp.bfloat16),
            pltpu.SemaphoreType.DMA,
        ],
        compiler_params=room,
        name="stick_values",
    )(
        stick_length,
        plane_index,
        occupation,
        rotation_matrix,
        coeffs.reshape(2 * in_count * sticks, grid_len),
    )
    left, right = pl.pallas_call(
        functools.partial(table_kernel, grid_len),
        out_shape=(
            jax.ShapeDtypeStruct((2, grid_len, stick_count), jnp.bfloat16),
            jax.ShapeDtypeStruct((2, 2 * grid_len, stick_count), jnp.bfloat16),
        ),
        in_specs=[vmem],
        out_specs=(vmem, vmem),
        compiler_params=room,
        cost_estimate=pl.CostEstimate(
            flops=80 * grid_len * stick_count,
            bytes_accessed=12 * grid_len * stick_count,
            transcendentals=0,
        ),
        name="stick_tables",
    )(stick_column.reshape(1, stick_count))
    arrived = lax.all_to_all(messages, ("band", "pw"), split_axis=0, concat_axis=0, tiled=True)
    chunk = min(grid_len, stick_count)
    norm_factor = 1.0 / float(bands * stick_count * grid_len)
    return pl.pallas_call(
        functools.partial(plane_kernel, bands, own_planes, norm_factor),
        out_shape=jax.ShapeDtypeStruct((own_planes, grid_len, grid_len), jnp.float32),
        in_specs=[vmem] * 3,
        out_specs=vmem,
        scratch_shapes=[pltpu.VMEM((stick_count // chunk, rows, chunk), jnp.float32)],
        compiler_params=room,
        name="plane_density",
    )(arrived.reshape(stick_count, lanes), left, right)


def solution(mesh):
    return jax.shard_map(
        shards,
        mesh=mesh,
        in_specs=(P(None, None, ("band", "pw"), None), P(), P(), P(), P(), P("band")),
        out_specs=P("pw", None, None),
        check_vma=False,
    )
```

time: 240 us -> 27.9 us (0.12)
  local copies, waits for them, and re-layouts: 137 us -> 1.99 us
  matrix products: 37.3 us -> 0 us
  waiting for transfers between devices: 36.7 us -> 5.06 us
  between operations: 13.5 us -> 0.02 us
  Pallas kernels: 0 us -> 13.2 us
  other arithmetic: 4.08 us -> 0 us
  starting transfers between devices: 10.6 us -> 7.3 us
    slice x4 -> x0, local copies, waits for them, and re-layouts: 86 us -> none  [one_plane(): planes[1]]
    scatter x4 -> x0, local copies, waits for them, and re-layouts: 42.4 us -> none  [one_plane(): jnp.zeros((2, grid_len * grid_len), jnp.bfloat16).at[:, columns]]
    dot_general x35 -> x0, matrix products: 37.3 us -> none  [the longest x33 36.3 us: contract(): return jnp.einsum(form, left, right, preferred_element_type=jnp.float32)]
    psum x1 -> x0, waiting for transfers between devices: 30.4 us -> none  [shards(): return lax.psum(local_sum, 'band')]
    pallas_call x0 -> x3, Pallas kernels: none -> 13.2 us  [the longest x1 7.83 us: shards(): pl.pallas_call(functools.partial(plane_kernel, bands, own_planes, norm_fa...]
    all_to_all x2 -> x1, starting transfers between devices: 10.5 us -> 7.3 us  [shards(): lax.all_to_all(messages, ('band', 'pw'), split_axis=0, concat_axis=0, til...]
    all_to_all x2 -> x1, waiting for transfers between devices: 6.21 us -> 5.06 us  [shards(): lax.all_to_all(messages, ('band', 'pw'), split_axis=0, concat_axis=0, til...]
  transfers between devices with their start and end apart: 3 -> 1, of which waited for: 3 -> 1; matrix products, arithmetic and copies ran while one was open for 2% -> 0% of each run, Pallas kernels for 0% -> 8%
where the time goes in v1:
time: 27.9 us; the launch traced here: 27.6 us
  Pallas kernels  13.2 us (47%)
  starting transfers between devices  7.3 us (26%)
  waiting for transfers between devices  5.06 us (18%)
  local copies, waits for them, and re-layouts  1.99 us (7%)
    pallas_call x1, Pallas kernels, shards(): pl.pallas_call(functools.partial(plane_kernel, bands, own_planes, norm_fa...  7.83 us
    all_to_all x1, starting transfers between devices, shards(): lax.all_to_all(messages, ('band', 'pw'), split_axis=0, concat_axis=0, til...  7.3 us
    all_to_all x1, waiting for transfers between devices, shards(): lax.all_to_all(messages, ('band', 'pw'), split_axis=0, concat_axis=0, til...  5.06 us
    pallas_call x1, Pallas kernels, shards(): pl.pallas_call(functools.partial(stick_kernel, pw_count), out_shape=jax.S...  3.14 us
    pallas_call x1, Pallas kernels, shards(): pl.pallas_call(functools.partial(table_kernel, grid_len), out_shape=(jax....  2.21 us
    unnamed x3, local copies, waits for them, and re-layouts  1.99 us
  transfers between devices with their start and end apart: 1, of which 1 were waited for; matrix products, arithmetic and copies ran while one was open for 0% of the time, Pallas kernels for 8%

profile of v1, /device:TPU:0, one launch (start us, length us, event | category | flops | bytes accessed | tf_op | source)
XLA Modules:
  0.0 27.6 jit_solution(6322118079110116817)
XLA Ops:
  0.0 1.4 %copy.7.rotation_ref = bf16[2,64,8]{2,1,0:T(8,128)(2,1)} copy(bf16[2,64,8]{1,2,0:T(8,128)(2,1)} %param.7) | data formatting | bytes 4096 | tf_op args[1]
  1.4 3.1 %stick_values.1 = bf16[32,8,128]{2,1,0:T(8,128)(2,1)} custom-call(s32[256]{0:T(256)} %length_ref.1, s32[16]{0:T(128)} %plane_ref.1, s32[2]{0:T(128)} %occupation_ref.1, bf16[2,64,8]{2,1,0:T(8,128)(2,1)} %copy.7.rotation_ref, bf16[1024,256]{1,0:T(8,128)(2,1)} %bitcast.3), custom_call_target="tpu_custom_call" | custom-call | tf_op jit(solution)/shard_map/stick_values/pallas_call | solution.py:245
  4.5 7.3 %all-to-all-start = ((bf16[32,8,128]{2,1,0:T(8,128)(2,1)}), bf16[32,8,128]{2,1,0:T(8,128)(2,1)S(1)}, u32[]{:S(2)}, u32[]{:S(2)}) async-start(bf16[32,8,128]{2,1,0:T(8,128)(2,1)} %stick_values.1), calls=%async_computation | async-start | bytes 131072 | tf_op jit(solution)/shard_map/all_to_all | solution.py:279
  11.8 2.2 %stick_tables.1 = (bf16[2,256,256]{2,1,0:T(8,128)(2,1)}, bf16[2,512,256]{2,1,0:T(8,128)(2,1)}) custom-call(s32[1,256]{1,0:T(1,128)} %bitcast.5), custom_call_target="tpu_custom_call" | custom-call | flops 5242880 | bytes 786432 | tf_op jit(solution)/shard_map/stick_tables/pallas_call | solution.py:263
  14.1 5.1 %all-to-all-done = bf16[32,8,128]{2,1,0:T(8,128)(2,1)S(1)} async-done(((bf16[32,8,128]{2,1,0:T(8,128)(2,1)}), bf16[32,8,128]{2,1,0:T(8,128)(2,1)S(1)}, u32[]{:S(2)}, u32[]{:S(2)}) %all-to-all-start) | async-done | bytes 65568 | tf_op jit(solution)/shard_map/all_to_all | solution.py:279
  19.1 0.0 copy-start
  19.1 0.6 %copy-done = bf16[32,8,128]{2,1,0:T(8,128)(2,1)} copy-done((bf16[32,8,128]{2,1,0:T(8,128)(2,1)}, bf16[32,8,128]{2,1,0:T(8,128)(2,1)S(1)}, u32[]{:S(2)}) %copy-start) | copy-done | bytes 65560
  19.7 7.8 %plane_density.1 = f32[2,256,256]{2,1,0:T(8,128)} custom-call(bf16[256,128]{1,0:T(8,128)(2,1)} %bitcast.4, bf16[2,256,256]{2,1,0:T(8,128)(2,1)} %get-tuple-element.7.left_ref, bf16[2,512,256]{2,1,0:T(8,128)(2,1)} %get-tuple-element.8.right_ref), custom_call_target="tpu_custom_call" | custom-call | tf_op jit(solution)/shard_map/plane_density/pallas_call | solution.py:282
Async XLA Ops:
  4.5 14.6 %all-to-all-start = ((bf16[32,8,128]{2,1,0:T(8,128)(2,1)}), bf16[32,8,128]{2,1,0:T(8,128)(2,1)S(1)}, u32[]{:S(2)}, u32[]{:S(2)}) async-start(bf16[32,8,128]{2,1,0:T(8,128)(2,1)} %stick_values.1), calls=%async_computation | async-start | bytes 131072 | tf_op jit(solution)/shard_map/all_to_all | solution.py:279
  19.1 0.6 %copy-start = (bf16[32,8,128]{2,1,0:T(8,128)(2,1)}, bf16[32,8,128]{2,1,0:T(8,128)(2,1)S(1)}, u32[]{:S(2)}) copy-start(bf16[32,8,128]{2,1,0:T(8,128)(2,1)S(1)} %all-to-all-done) | copy-start | bytes 196612

commit v2 on v1

--- a/solution.py
+++ b/solution.py
@@ -9,6 +9,10 @@
 from jax.sharding import PartitionSpec as P
 
 LANES = 128
+PACK = 16
+P_BLOCK = 64
+BAND_GROUP = 8
+MIB = 1024 * 1024
 
 
 def wrap(value, period):
@@ -51,6 +55,18 @@
     return jnp.dot(left, right, preferred_element_type=jnp.float32)
 
 
+def loop(count, body, carry):
+    if count > 16:
+        return lax.fori_loop(0, count, body, carry)
+    for index in range(count):
+        carry = body(index, carry)
+    return carry
+
+
+def room(*sizes):
+    return pltpu.CompilerParams(vmem_limit_bytes=min(56 * MIB, 16 * MIB + 2 * sum(sizes)))
+
+
 def spread(scalars, index, shape):
     result = jnp.full(shape, scalars[0])
     for place, scalar in enumerate(scalars[1:], 1):
@@ -61,7 +77,7 @@
 def stick_kernel(
     pw_count, length_ref, plane_ref, occupation_ref, rotation_ref, coeff_ref, out_ref, held, sem
 ):
-    in_count, out_count = rotation_ref.shape[1:]
+    out_count, in_count = rotation_ref.shape[1:]
     grid_len = coeff_ref.shape[1]
     sticks = coeff_ref.shape[0] // (2 * in_count)
     plane_count = plane_ref.shape[0]
@@ -80,8 +96,8 @@
         wrap(cut(iota((row_count, out_count), 0), sticks), out_count)
         == iota((row_count, out_count), 1)
     ).astype(jnp.bfloat16)
-    from_real = dot_last(pick, rotation_ref[0])
-    from_imag = dot_last(pick, rotation_ref[1])
+    from_real = dot(pick, rotation_ref[0])
+    from_imag = dot(pick, rotation_ref[1])
     is_real = iota((row_count, in_count), 0) < out_count * sticks
     widen = (
         cut(iota((in_count, in_count * sticks), 1), sticks)
@@ -151,29 +167,39 @@
 
 def table_kernel(grid_len, column_ref, left_ref, right_ref):
     count = column_ref.shape[1]
+    half = grid_len // 2
     columns = column_ref[...]
-    freq = iota((grid_len, count), 0)
-    turns = freq * cut(columns, grid_len)
+    turns = iota((grid_len, count), 0) * cut(columns, grid_len)
     left_ref[0] = cosine(turns, grid_len).astype(jnp.bfloat16)
     left_ref[1] = sine(turns, grid_len).astype(jnp.bfloat16)
-    turns = freq * wrap(columns, grid_len)
-    cos_table = cosine(turns, grid_len).astype(jnp.bfloat16)
-    sin_table = sine(turns, grid_len).astype(jnp.bfloat16)
-    right_ref[0, :grid_len] = cos_table
-    right_ref[0, grid_len:] = sin_table
-    right_ref[1, :grid_len] = -sin_table
-    right_ref[1, grid_len:] = cos_table
+    tall = jnp.transpose(jnp.broadcast_to(wrap(columns, grid_len), (half, count)))
+    freq = iota((count, half), 1)
+    right_ref[:, :half] = cosine(tall * freq, grid_len).astype(jnp.bfloat16)
+    turns = jnp.where(freq == 0, tall * half, tall * freq + (grid_len - grid_len // 4))
+    right_ref[:, half:] = cosine(turns, grid_len).astype(jnp.bfloat16)
 
 
 def plane_kernel(
-    bands, own_planes, norm_factor, message_ref, left_ref, right_ref, out_ref, value_ref
+    bands,
+    own_planes,
+    norm_factor,
+    message_ref,
+    left_ref,
+    right_ref,
+    out_ref,
+    value_ref,
+    weight_ref,
+    held_ref,
+    sem,
 ):
-    chunks = value_ref.shape[0]
-    chunk = value_ref.shape[2]
+    chunks, rows, chunk = value_ref.shape
     grid_len = out_ref.shape[1]
+    half = grid_len // 2
     lanes = message_ref.shape[1]
-    rows = value_ref.shape[1]
     spots = 2 * bands
+    height = math.gcd(grid_len, P_BLOCK)
+    blocks = grid_len // height
+    group = math.gcd(bands, BAND_GROUP)
     select = (iota((rows + bands, lanes), 0) == iota((rows + bands, lanes), 1)).astype(
         jnp.bfloat16
     )
@@ -184,47 +210,73 @@
         value_ref[index] = picked[:rows]
         return jnp.maximum(peak, jnp.max(picked[rows:], 1, keepdims=True))
 
-    peak = jnp.zeros((bands, 1), jnp.float32)
-    if chunks == 1:
-        peak = turn(0, peak)
-    else:
-        peak = lax.fori_loop(0, chunks, turn, peak)
-    scale = jnp.sqrt(peak)
-    for group in range(rows // bands):
-        where = slice(group * bands, (group + 1) * bands)
-        value_ref[:, where] = value_ref[:, where] * scale[None]
-
-    def partial_wave(index, plane, band):
-        lane = pl.ds(index * chunk, chunk) if chunks > 1 else slice(None)
-        real = value_ref[index, pl.ds(plane * spots + band, 1), :]
-        imag = value_ref[index, pl.ds(plane * spots + bands + band, 1), :]
-        cos_table = left_ref[0, :, lane].astype(jnp.float32)
-        sin_table = left_ref[1, :, lane].astype(jnp.float32)
-        part_real = (cos_table * real - sin_table * imag).astype(jnp.bfloat16)
-        part_imag = (sin_table * real + cos_table * imag).astype(jnp.bfloat16)
-        return dot_last(part_real, right_ref[0, :, lane]) + dot_last(
-            part_imag, right_ref[1, :, lane]
-        )
-
-    for plane in range(own_planes):
-
-        def add_band(band, total):
+    peak = loop(chunks, turn, jnp.zeros((bands, 1), jnp.float32))
+    weight_ref[...] = jnp.broadcast_to(peak * norm_factor, weight_ref.shape)
+
+    def stick_sums(index, plane, block, first_band):
+        lane = pl.ds(index * chunk, chunk)
+        row = pl.ds(block * height, height)
+        cos_table = left_ref[0, row, lane].reshape(height // PACK, PACK, chunk)
+        sin_table = left_ref[1, row, lane].reshape(height // PACK, PACK, chunk)
+        parts = []
+        for band in range(group):
+            at = plane * spots + first_band + band
+            real, imag = (
+                jnp.broadcast_to(value_ref[index, pl.ds(spot, 1), :], (PACK, chunk)).astype(
+                    jnp.bfloat16
+                )[None]
+                for spot in (at, at + bands)
+            )
+            parts.append((cos_table * real - sin_table * imag).reshape(height, chunk))
+            parts.append((sin_table * real + cos_table * imag).reshape(height, chunk))
+        return dot(jnp.concatenate(parts, 0), right_ref[pl.ds(index * chunk, chunk), :])
+
+    def one_block(step, carry):
+        plane, block = step // blocks, step % blocks
+
+        def one_group(index, sums):
+            first_band = index * group
             if chunks == 1:
-                wave = partial_wave(0, plane, band)
+                found = stick_sums(0, plane, block, first_band)
             else:
-                wave = lax.fori_loop(
+                found = lax.fori_loop(
                     0,
                     chunks,
-                    lambda index, so_far: so_far + partial_wave(index, plane, band),
-                    jnp.zeros((grid_len, 2 * grid_len), jnp.float32),
+                    lambda at, so_far: so_far + stick_sums(at, plane, block, first_band),
+                    jnp.zeros((2 * group * height, grid_len), jnp.float32),
                 )
-            real, imag = wave[:, :grid_len], wave[:, grid_len:]
-            out_ref[plane] += real * real + imag * imag
-            return total
-
-        out_ref[plane] = jnp.zeros((grid_len, grid_len), jnp.float32)
-        lax.fori_loop(0, bands, add_band, 0)
-        out_ref[plane] = out_ref[plane] * norm_factor
+            with_cos, with_sin, mixed = sums
+            for band in range(group):
+                top = 2 * band * height
+                a, d = found[top : top + height, :half], found[top : top + height, half:]
+                top += height
+                c, b = found[top : top + height, :half], found[top : top + height, half:]
+                weight = weight_ref[pl.ds(first_band + band, 1), :half]
+                with_cos += weight * (a * a + c * c)
+                with_sin += weight * (b * b + d * d)
+                mixed += weight * (c * d - a * b)
+            return with_cos, with_sin, mixed
+
+        zero = jnp.zeros((height, half), jnp.float32)
+        with_cos, with_sin, mixed = loop(bands // group, one_group, (zero, zero, zero))
+        lane = iota((height, half), 1)
+        both, mixed = with_cos + with_sin, mixed + mixed
+        ahead = jnp.where(lane == 0, with_cos, both + mixed)
+        back = jnp.where(lane == 0, with_sin, both - mixed)
+        row = pl.ds(block * height, height)
+        held_ref[plane, row, :half] = ahead
+        held_ref[plane, row, half:] = jnp.take_along_axis(
+            back, jnp.where(lane == 0, 0, half - lane), axis=1
+        )
+        pltpu.make_async_copy(
+            held_ref.at[plane, row], out_ref.at[plane, row], sem.at[step]
+        ).start()
+        return carry
+
+    loop(own_planes * blocks, one_block, 0)
+    for step in range(own_planes * blocks):
+        where = (step // blocks, pl.ds(step % blocks * height, height))
+        pltpu.make_async_copy(held_ref.at[where], out_ref.at[where], sem.at[step]).wait()
 
 
 def shards(coeffs, rotation_matrix, stick_length, stick_column, plane_index, occupation):
@@ -240,7 +292,7 @@
     lanes = -(-(rows + bands) // LANES) * LANES
     smem = pl.BlockSpec(memory_space=pltpu.SMEM)
     vmem = pl.BlockSpec(memory_space=pltpu.VMEM)
-    room = pltpu.CompilerParams(vmem_limit_bytes=56 * 1024 * 1024)
+    table_bytes = 6 * grid_len * stick_count
 
     messages = pl.pallas_call(
         functools.partial(stick_kernel, pw_count),
@@ -251,24 +303,24 @@
             pltpu.VMEM((2 * in_count * sticks, grid_len), jnp.bfloat16),
             pltpu.SemaphoreType.DMA,
         ],
-        compiler_params=room,
+        compiler_params=pltpu.CompilerParams(vmem_limit_bytes=56 * MIB),
         name="stick_values",
     )(
         stick_length,
         plane_index,
         occupation,
-        rotation_matrix,
+        jnp.swapaxes(rotation_matrix, 1, 2),
         coeffs.reshape(2 * in_count * sticks, grid_len),
     )
     left, right = pl.pallas_call(
         functools.partial(table_kernel, grid_len),
         out_shape=(
             jax.ShapeDtypeStruct((2, grid_len, stick_count), jnp.bfloat16),
-            jax.ShapeDtypeStruct((2, 2 * grid_len, stick_count), jnp.bfloat16),
+            jax.ShapeDtypeStruct((stick_count, grid_len), jnp.bfloat16),
         ),
         in_specs=[vmem],
         out_specs=(vmem, vmem),
-        compiler_params=room,
+        compiler_params=room(table_bytes),
         cost_estimate=pl.CostEstimate(
             flops=80 * grid_len * stick_count,
             bytes_accessed=12 * grid_len * stick_count,
@@ -279,13 +331,19 @@
     arrived = lax.all_to_all(messages, ("band", "pw"), split_axis=0, concat_axis=0, tiled=True)
     chunk = min(grid_len, stick_count)
     norm_factor = 1.0 / float(bands * stick_count * grid_len)
+    blocks = own_planes * (grid_len // math.gcd(grid_len, P_BLOCK))
     return pl.pallas_call(
         functools.partial(plane_kernel, bands, own_planes, norm_factor),
         out_shape=jax.ShapeDtypeStruct((own_planes, grid_len, grid_len), jnp.float32),
         in_specs=[vmem] * 3,
-        out_specs=vmem,
-        scratch_shapes=[pltpu.VMEM((stick_count // chunk, rows, chunk), jnp.float32)],
-        compiler_params=room,
+        out_specs=pl.BlockSpec(memory_space=pl.ANY),
+        scratch_shapes=[
+            pltpu.VMEM((stick_count // chunk, rows, chunk), jnp.float32),
+            pltpu.VMEM((bands, LANES), jnp.float32),
+            pltpu.VMEM((own_planes, grid_len, grid_len), jnp.float32),
+            pltpu.SemaphoreType.DMA((blocks,)),
+        ],
+        compiler_params=room(table_bytes, 2 * stick_count * lanes),
         name="plane_density",
     )(arrived.reshape(stick_count, lanes), left, right)
 

time: 27.9 us -> 20.9 us (0.75)
  Pallas kernels: 13.2 us -> 6.81 us
  local copies, waits for them, and re-layouts: 1.99 us -> 0.67 us
  waiting for transfers between devices: 5.06 us -> 5.86 us
    pallas_call x1, Pallas kernels: 7.83 us -> 3 us  [shards(): pl.pallas_call(functools.partial(plane_kernel, bands, own_planes, norm_fa...]
    pallas_call x1, Pallas kernels: 2.21 us -> 0.73 us  [shards(): pl.pallas_call(functools.partial(table_kernel, grid_len), out_shape=(jax....]
    unnamed x3 -> x2, local copies, waits for them, and re-layouts: 1.99 us -> 0.67 us
    all_to_all x1, waiting for transfers between devices: 5.06 us -> 5.86 us  [shards(): lax.all_to_all(messages, ('band', 'pw'), split_axis=0, concat_axis=0, til...]
  transfers between devices with their start and end apart: 1 -> 1, of which waited for: 1 -> 1; matrix products, arithmetic and copies ran while one was open for 0% -> 0% of each run, Pallas kernels for 8% -> 4%
where the time goes in v2:
time: 20.9 us; the launch traced here: 20.7 us
  starting transfers between devices  7.3 us (35%)
  Pallas kernels  6.81 us (33%)
  waiting for transfers between devices  5.86 us (28%)
  local copies, waits for them, and re-layouts  0.67 us (3%)
    all_to_all x1, starting transfers between devices, shards(): lax.all_to_all(messages, ('band', 'pw'), split_axis=0, concat_axis=0, til...  7.3 us
    all_to_all x1, waiting for transfers between devices, shards(): lax.all_to_all(messages, ('band', 'pw'), split_axis=0, concat_axis=0, til...  5.86 us
    pallas_call x1, Pallas kernels, shards(): pl.pallas_call(functools.partial(stick_kernel, pw_count), out_shape=jax.S...  3.08 us
    pallas_call x1, Pallas kernels, shards(): pl.pallas_call(functools.partial(plane_kernel, bands, own_planes, norm_fa...  3 us
    pallas_call x1, Pallas kernels, shards(): pl.pallas_call(functools.partial(table_kernel, grid_len), out_shape=(jax....  0.73 us
    unnamed x2, local copies, waits for them, and re-layouts  0.67 us
  transfers between devices with their start and end apart: 1, of which 1 were waited for; matrix products, arithmetic and copies ran while one was open for 0% of the time, Pallas kernels for 4%

profile of v2, /device:TPU:0, one launch (start us, length us, event | category | flops | bytes accessed | tf_op | source)
XLA Modules:
  0.0 20.7 jit_solution(5326526328413071581)
XLA Ops:
  0.0 3.1 %stick_values.1 = bf16[32,8,128]{2,1,0:T(8,128)(2,1)} custom-call(s32[256]{0:T(256)} %length_ref.1, s32[16]{0:T(128)} %plane_ref.1, s32[2]{0:T(128)} %occupation_ref.1, bf16[2,8,64]{2,1,0:T(8,128)(2,1)} %bitcast.7, bf16[1024,256]{1,0:T(8,128)(2,1)} %bitcast.6), custom_call_target="tpu_custom_call" | custom-call | tf_op jit(solution)/shard_map/stick_values/pallas_call | solution.py:297
  3.1 7.3 %all-to-all-start = ((bf16[32,8,128]{2,1,0:T(8,128)(2,1)}), bf16[32,8,128]{2,1,0:T(8,128)(2,1)S(1)}, u32[]{:S(2)}, u32[]{:S(2)}) async-start(bf16[32,8,128]{2,1,0:T(8,128)(2,1)} %stick_values.1), calls=%async_computation | async-start | bytes 131072 | tf_op jit(solution)/shard_map/all_to_all | solution.py:331
  10.4 0.0 copy-start
  10.4 0.7 %copy-done = s32[256]{0:T(256)S(1)} copy-done((s32[256]{0:T(256)S(1)}, s32[256]{0:T(256)}, u32[]{:S(2)}) %copy-start) | copy-done | bytes 1048
  11.1 0.7 %stick_tables.1 = (bf16[2,256,256]{2,1,0:T(8,128)(2,1)S(1)}, bf16[256,256]{1,0:T(8,128)(2,1)S(1)}) custom-call(s32[1,256]{1,0:T(1,128)S(1)} %bitcast.5), custom_call_target="tpu_custom_call" | custom-call | flops 5242880 | bytes 786432 | tf_op jit(solution)/shard_map/stick_tables/pallas_call | solution.py:315
  11.8 5.9 %all-to-all-done = bf16[32,8,128]{2,1,0:T(8,128)(2,1)S(1)} async-done(((bf16[32,8,128]{2,1,0:T(8,128)(2,1)}), bf16[32,8,128]{2,1,0:T(8,128)(2,1)S(1)}, u32[]{:S(2)}, u32[]{:S(2)}) %all-to-all-start) | async-done | bytes 65568 | tf_op jit(solution)/shard_map/all_to_all | solution.py:331
  17.7 3.0 %plane_density.1 = f32[2,256,256]{2,1,0:T(8,128)} custom-call(bf16[256,128]{1,0:T(8,128)(2,1)S(1)} %bitcast.4, bf16[2,256,256]{2,1,0:T(8,128)(2,1)S(1)} %get-tuple-element.7.left_ref, bf16[256,256]{1,0:T(8,128)(2,1)S(1)} %get-tuple-element.8.right_ref), custom_call_target="tpu_custom_call" | custom-call | tf_op jit(solution)/shard_map/plane_density/pallas_call | solution.py:335
Async XLA Ops:
  3.1 14.6 %all-to-all-start = ((bf16[32,8,128]{2,1,0:T(8,128)(2,1)}), bf16[32,8,128]{2,1,0:T(8,128)(2,1)S(1)}, u32[]{:S(2)}, u32[]{:S(2)}) async-start(bf16[32,8,128]{2,1,0:T(8,128)(2,1)} %stick_values.1), calls=%async_computation | async-start | bytes 131072 | tf_op jit(solution)/shard_map/all_to_all | solution.py:331
  10.4 0.7 %copy-start = (s32[256]{0:T(256)S(1)}, s32[256]{0:T(256)}, u32[]{:S(2)}) copy-start(s32[256]{0:T(256)} %param.9) | copy-start | bytes 3076

commit v3 on v2

--- a/solution.py
+++ b/solution.py
@@ -75,27 +75,49 @@
 
 
 def stick_kernel(
-    pw_count, length_ref, plane_ref, occupation_ref, rotation_ref, coeff_ref, out_ref, held, sem
+    length_hbm,
+    plane_hbm,
+    occupation_hbm,
+    rotation_hbm,
+    coeff_hbm,
+    out_ref,
+    length_ref,
+    plane_ref,
+    occupation_ref,
+    rotation_ref,
+    coeff_ref,
+    sems,
 ):
+    copies = [
+        pltpu.make_async_copy(source, target, sems.at[index])
+        for index, (source, target) in enumerate(
+            (
+                (rotation_hbm, rotation_ref),
+                (coeff_hbm, coeff_ref),
+                (plane_hbm, plane_ref),
+                (length_hbm, length_ref),
+                (occupation_hbm, occupation_ref),
+            )
+        )
+    ]
+    for copy in copies:
+        copy.start()
     out_count, in_count = rotation_ref.shape[1:]
     grid_len = coeff_ref.shape[1]
     sticks = coeff_ref.shape[0] // (2 * in_count)
     plane_count = plane_ref.shape[0]
+    pw_count = out_ref.shape[0]
     own_planes = plane_count // pw_count
     own_bands = occupation_ref.shape[0]
     row_count = 2 * out_count * sticks
     band_index = lax.axis_index("band")
     first_stick = (band_index * pw_count + lax.axis_index("pw")) * sticks
-    copy = pltpu.make_async_copy(coeff_ref, held, sem)
-    copy.start()
-
-    lengths = [length_ref[first_stick + place] for place in range(sticks)]
-    planes = [plane_ref[place] for place in range(plane_count)]
 
     pick = (
         wrap(cut(iota((row_count, out_count), 0), sticks), out_count)
         == iota((row_count, out_count), 1)
     ).astype(jnp.bfloat16)
+    copies[0].wait()
     from_real = dot(pick, rotation_ref[0])
     from_imag = dot(pick, rotation_ref[1])
     is_real = iota((row_count, in_count), 0) < out_count * sticks
@@ -114,6 +136,10 @@
         mixed.append(jnp.where(same, wide, 0.0).astype(jnp.bfloat16))
     rotation = jnp.concatenate(mixed, 1)
 
+    for copy in copies[2:]:
+        copy.wait()
+    lengths = [length_ref[first_stick + place] for place in range(sticks)]
+    planes = [plane_ref[place] for place in range(plane_count)]
     plane_rows = spread(planes, iota((plane_count, grid_len), 0), (plane_count, grid_len))
     product = iota((plane_count, grid_len), 1) * plane_rows
     table = jnp.concatenate([cosine(product, grid_len), sine(product, grid_len)], 0).astype(
@@ -130,8 +156,8 @@
     row_lengths = spread(lengths, iota((sticks, grid_len), 0), (sticks, grid_len))
     live = iota((sticks, grid_len), 1) < row_lengths
 
-    copy.wait()
-    rotated = dot(rotation, held[...])
+    copies[1].wait()
+    rotated = dot(rotation, coeff_ref[...])
     rotated = rotated.reshape(row_count // sticks, sticks, grid_len)
     rotated = jnp.where(live[None], rotated, 0.0).reshape(row_count, grid_len)
     sums = dot_last(table, rotated.astype(jnp.bfloat16))
@@ -160,15 +186,34 @@
         occupied = jnp.where(
             iota((sticks, lanes), 1) == lane, occupation_ref[own_band], occupied
         )
-    message = (message + occupied.astype(jnp.float32)[None]).astype(out_ref.dtype)
-    for band in range(out_ref.shape[0] // pw_count):
-        out_ref[band * pw_count : (band + 1) * pw_count] = message
-
-
-def table_kernel(grid_len, column_ref, left_ref, right_ref):
+    out_ref[...] = (message + occupied.astype(jnp.float32)[None]).astype(out_ref.dtype)
+
+
+def regroup_kernel(*refs):
+    band_count = refs[-1].shape[0]
+    pw_index = lax.axis_index("pw")
+    for offset, out_ref in enumerate(refs[band_count:]):
+        for place, gathered_ref in enumerate(refs[:band_count]):
+            out_ref[place] = gathered_ref[pw_index ^ offset]
+
+
+def table_kernel(grid_len, sticks, column_hbm, left_ref, right_ref, column_ref, sem):
+    copy = pltpu.make_async_copy(column_hbm, column_ref, sem)
+    copy.start()
+    copy.wait()
     count = column_ref.shape[1]
     half = grid_len // 2
-    columns = column_ref[...]
+    me = lax.axis_index("band") * lax.axis_size("pw") + lax.axis_index("pw")
+    columns = jnp.broadcast_to(column_ref[...], (8, count))
+    stride = sticks
+    while stride < count:
+        high = cut(iota((8, count), 1), stride) & 1
+        exchanged = jnp.where(
+            high == 1, pltpu.roll(columns, stride, 1), pltpu.roll(columns, count - stride, 1)
+        )
+        columns = jnp.where(cut(me * sticks, stride) & 1 == 1, exchanged, columns)
+        stride *= 2
+    columns = columns[:1]
     turns = iota((grid_len, count), 0) * cut(columns, grid_len)
     left_ref[0] = cosine(turns, grid_len).astype(jnp.bfloat16)
     left_ref[1] = sine(turns, grid_len).astype(jnp.bfloat16)
@@ -183,19 +228,13 @@
     bands,
     own_planes,
     norm_factor,
-    message_ref,
-    left_ref,
-    right_ref,
-    out_ref,
-    value_ref,
-    weight_ref,
-    held_ref,
-    sem,
+    *refs,
 ):
+    *arrived, left_ref, right_ref, out_ref, message_ref, value_ref, weight_ref, held_ref, sem = refs
     chunks, rows, chunk = value_ref.shape
     grid_len = out_ref.shape[1]
     half = grid_len // 2
-    lanes = message_ref.shape[1]
+    sticks, lanes = message_ref.shape[1:]
     spots = 2 * bands
     height = math.gcd(grid_len, P_BLOCK)
     blocks = grid_len // height
@@ -204,9 +243,15 @@
         jnp.bfloat16
     )
 
+    for offset, arrived_ref in enumerate(arrived):
+        for place in range(arrived_ref.shape[0]):
+            message_ref[place * len(arrived) + offset] = arrived_ref[place]
+
     def turn(index, peak):
-        first = index * chunk
-        picked = dot_last(select, message_ref[pl.ds(first, chunk), :])
+        pieces = chunk // sticks
+        picked = dot_last(
+            select, message_ref[pl.ds(index * pieces, pieces)].reshape(chunk, lanes)
+        )
         value_ref[index] = picked[:rows]
         return jnp.maximum(peak, jnp.max(picked[rows:], 1, keepdims=True))
 
@@ -282,7 +327,6 @@
 def shards(coeffs, rotation_matrix, stick_length, stick_column, plane_index, occupation):
     band_count = lax.axis_size("band")
     pw_count = lax.axis_size("pw")
-    devices = band_count * pw_count
     in_count, sticks, grid_len = coeffs.shape[1:]
     bands = rotation_matrix.shape[2]
     stick_count = stick_column.shape[0]
@@ -290,36 +334,68 @@
     spots = 2 * bands
     rows = own_planes * spots
     lanes = -(-(rows + bands) // LANES) * LANES
-    smem = pl.BlockSpec(memory_space=pltpu.SMEM)
     vmem = pl.BlockSpec(memory_space=pltpu.VMEM)
+    hbm = pl.BlockSpec(memory_space=pltpu.HBM)
     table_bytes = 6 * grid_len * stick_count
+    message_bytes = 2 * stick_count * lanes
+
+    def exchange(array, axis, offset):
+        count = lax.axis_size(axis)
+        return lax.ppermute(array, axis, [(place, place ^ offset) for place in range(count)])
 
     messages = pl.pallas_call(
-        functools.partial(stick_kernel, pw_count),
-        out_shape=jax.ShapeDtypeStruct((devices, sticks, lanes), jnp.bfloat16),
-        in_specs=[smem, smem, smem, vmem, pl.BlockSpec(memory_space=pl.ANY)],
+        stick_kernel,
+        out_shape=jax.ShapeDtypeStruct((pw_count, sticks, lanes), jnp.bfloat16),
+        in_specs=[hbm] * 5,
         out_specs=vmem,
         scratch_shapes=[
+            pltpu.SMEM(stick_length.shape, jnp.int32),
+            pltpu.SMEM(plane_index.shape, jnp.int32),
+            pltpu.SMEM(occupation.shape, jnp.int32),
+            pltpu.VMEM((2, bands, in_count), jnp.bfloat16),
             pltpu.VMEM((2 * in_count * sticks, grid_len), jnp.bfloat16),
-            pltpu.SemaphoreType.DMA,
+            pltpu.SemaphoreType.DMA((5,)),
         ],
-        compiler_params=pltpu.CompilerParams(vmem_limit_bytes=56 * MIB),
+        compiler_params=room(),
         name="stick_values",
     )(
-        stick_length,
-        plane_index,
-        occupation,
-        jnp.swapaxes(rotation_matrix, 1, 2),
-        coeffs.reshape(2 * in_count * sticks, grid_len),
-    )
+        *(
+            pltpu.with_memory_space_constraint(array, pltpu.HBM)
+            for array in (
+                stick_length,
+                plane_index,
+                occupation,
+                jnp.swapaxes(rotation_matrix, 1, 2),
+                coeffs.reshape(2 * in_count * sticks, grid_len),
+            )
+        )
+    )
+    gathered = [messages] + [exchange(messages, "band", place) for place in range(1, band_count)]
+    parcel = jax.ShapeDtypeStruct((band_count, sticks, lanes), jnp.bfloat16)
+    parcels = pl.pallas_call(
+        regroup_kernel,
+        out_shape=(parcel,) * pw_count,
+        in_specs=[vmem] * band_count,
+        out_specs=(vmem,) * pw_count,
+        compiler_params=room(message_bytes),
+        name="regroup",
+    )(*gathered)
+    arrived = [parcels[0]] + [
+        exchange(parcels[offset], "pw", offset) for offset in range(pw_count - 1, 0, -1)
+    ][::-1]
+    column_row, own = lax.optimization_barrier(
+        (stick_column.reshape(1, stick_count), parcels[0])
+    )
+    arrived[0] = own
     left, right = pl.pallas_call(
-        functools.partial(table_kernel, grid_len),
+        functools.partial(table_kernel, grid_len, sticks),
         out_shape=(
             jax.ShapeDtypeStruct((2, grid_len, stick_count), jnp.bfloat16),
             jax.ShapeDtypeStruct((stick_count, grid_len), jnp.bfloat16),
         ),
-        in_specs=[vmem],
+        in_specs=[hbm],
         out_specs=(vmem, vmem),
+        scratch_shapes=[pltpu.VMEM((1, stick_count), jnp.int32), pltpu.SemaphoreType.DMA],
         compiler_params=room(table_bytes),
         cost_estimate=pl.CostEstimate(
             flops=80 * grid_len * stick_count,
@@ -327,25 +403,25 @@
             transcendentals=0,
         ),
         name="stick_tables",
-    )(stick_column.reshape(1, stick_count))
-    arrived = lax.all_to_all(messages, ("band", "pw"), split_axis=0, concat_axis=0, tiled=True)
+    )(pltpu.with_memory_space_constraint(column_row, pltpu.HBM))
     chunk = min(grid_len, stick_count)
     norm_factor = 1.0 / float(bands * stick_count * grid_len)
     blocks = own_planes * (grid_len // math.gcd(grid_len, P_BLOCK))
     return pl.pallas_call(
         functools.partial(plane_kernel, bands, own_planes, norm_factor),
         out_shape=jax.ShapeDtypeStruct((own_planes, grid_len, grid_len), jnp.float32),
-        in_specs=[vmem] * 3,
-        out_specs=pl.BlockSpec(memory_space=pl.ANY),
+        in_specs=[vmem] * (pw_count + 2),
+        out_specs=hbm,
         scratch_shapes=[
+            pltpu.VMEM((band_count * pw_count, sticks, lanes), jnp.bfloat16),
             pltpu.VMEM((stick_count // chunk, rows, chunk), jnp.float32),
             pltpu.VMEM((bands, LANES), jnp.float32),
             pltpu.VMEM((own_planes, grid_len, grid_len), jnp.float32),
             pltpu.SemaphoreType.DMA((blocks,)),
         ],
-        compiler_params=room(table_bytes, 2 * stick_count * lanes),
+        compiler_params=room(table_bytes, message_bytes),
         name="plane_density",
-    )(arrived.reshape(stick_count, lanes), left, right)
+    )(*arrived, left, right)
 
 
 def solution(mesh):

time: 20.9 us -> 28.7 us (1.37)
  starting transfers between devices: 7.3 us -> 14.3 us
  waiting for transfers between devices: 5.86 us -> 7.47 us
  local copies, waits for them, and re-layouts: 0.67 us -> 0 us
    ppermute x0 -> x10, starting transfers between devices: none -> 14.3 us  [exchange(): lax.ppermute(array, axis, [(place, place ^ offset) for place in range(cou...]
    ppermute x0 -> x10, waiting for transfers between devices: none -> 7.47 us  [exchange(): lax.ppermute(array, axis, [(place, place ^ offset) for place in range(cou...]
    all_to_all x1 -> x0, starting transfers between devices: 7.3 us -> none  [shards(): lax.all_to_all(messages, ('band', 'pw'), split_axis=0, concat_axis=0, til...]
    all_to_all x1 -> x0, waiting for transfers between devices: 5.86 us -> none  [shards(): lax.all_to_all(messages, ('band', 'pw'), split_axis=0, concat_axis=0, til...]
    unnamed x2 -> x0, local copies, waits for them, and re-layouts: 0.67 us -> none
    pallas_call x2 -> x3, Pallas kernels: 3.81 us -> 3.61 us  [the longest x1 1.85 us: shards(): pl.pallas_call(stick_kernel, out_shape=jax.ShapeDtypeStruct((pw_count, st...]
  transfers between devices with their start and end apart: 1 -> 10, of which waited for: 1 -> 3; matrix products, arithmetic and copies ran while one was open for 0% -> 0% of each run, Pallas kernels for 4% -> 6%
where the time goes in v3:
time: 28.7 us; the launch traced here: 28.5 us
  starting transfers between devices  14.3 us (50%)
  waiting for transfers between devices  7.47 us (26%)
  Pallas kernels  6.67 us (23%)
    ppermute x10, starting transfers between devices, exchange(): lax.ppermute(array, axis, [(place, place ^ offset) for place in range(cou...  14.3 us
    ppermute x10, waiting for transfers between devices, exchange(): lax.ppermute(array, axis, [(place, place ^ offset) for place in range(cou...  7.47 us
    pallas_call x1, Pallas kernels, shards(): pl.pallas_call(functools.partial(plane_kernel, bands, own_planes, norm_fa...  3.06 us
    pallas_call x1, Pallas kernels, shards(): pl.pallas_call(stick_kernel, out_shape=jax.ShapeDtypeStruct((pw_count, st...  1.85 us
    pallas_call x1, Pallas kernels, shards(): pl.pallas_call(functools.partial(table_kernel, grid_len, sticks), out_sha...  1.74 us
  transfers between devices with their start and end apart: 10, of which 3 were waited for; matrix products, arithmetic and copies ran while one was open for 0% of the time, Pallas kernels for 6%

profile of v3, /device:TPU:0, one launch (start us, length us, event | category | flops | bytes accessed | tf_op | source)
XLA Modules:
  0.0 28.5 jit_solution(9608974980345655337)
XLA Ops:
  0.0 1.9 %stick_values.1.refs_0_ = bf16[8,8,128]{2,1,0:T(8,128)(2,1)S(1)} custom-call(s32[256]{0:T(256)} %length_hbm.1, s32[16]{0:T(128)} %plane_hbm.1, s32[2]{0:T(128)} %occupation_hbm.1, bf16[2,8,64]{2,1,0:T(8,128)(2,1)} %bitcast.4, bf16[1024,256]{1,0:T(8,128)(2,1)} %bitcast.3), custom_call_target="tpu_custom_call" | custom-call | tf_op jit(solution)/shard_map/stick_values/pallas_call | solution.py:346
  1.9 2.4 %collective-permute-start.2 = (bf16[8,8,128]{2,1,0:T(8,128)(2,1)S(1)}, bf16[8,8,128]{2,1,0:T(8,128)(2,1)S(1)}, u32[]{:S(2)}, u32[]{:S(2)}) collective-permute-start(bf16[8,8,128]{2,1,0:T(8,128)(2,1)S(1)} %stick_values.1.refs_0_), channel_id=1, source_target_pairs={{0,24},{8,16},{16,8},{24,0},{1,25},{9,17},{17,9},{25,1},{2,26},{10... | collective-permute-start | bytes 49160 | tf_op jit(solution)/shard_map/ppermute | solution.py:344
  4.3 0.6 %collective-permute-start.1 = (bf16[8,8,128]{2,1,0:T(8,128)(2,1)S(1)}, bf16[8,8,128]{2,1,0:T(8,128)(2,1)S(1)}, u32[]{:S(2)}, u32[]{:S(2)}) collective-permute-start(bf16[8,8,128]{2,1,0:T(8,128)(2,1)S(1)} %stick_values.1.refs_0_), channel_id=1, source_target_pairs={{0,16},{8,24},{16,0},{24,8},{1,17},{9,25},{17,1},{25,9},{2,18},{10... | collective-permute-start | bytes 49160 | tf_op jit(solution)/shard_map/ppermute | solution.py:344
  4.9 0.0 collective-permute-start
  5.0 0.8 %collective-permute-done.2.refs_3_ = bf16[8,8,128]{2,1,0:T(8,128)(2,1)S(1)} collective-permute-done((bf16[8,8,128]{2,1,0:T(8,128)(2,1)S(1)}, bf16[8,8,128]{2,1,0:T(8,128)(2,1)S(1)}, u32[]{:S(2)}, u32[]{:S(2)}) %collective-permute-start.2) | collective-permute-done | bytes 16416 | tf_op jit(solution)/shard_map/ppermute | solution.py:344
  5.7 2.3 %collective-permute-done.1.refs_2_ = bf16[8,8,128]{2,1,0:T(8,128)(2,1)S(1)} collective-permute-done((bf16[8,8,128]{2,1,0:T(8,128)(2,1)S(1)}, bf16[8,8,128]{2,1,0:T(8,128)(2,1)S(1)}, u32[]{:S(2)}, u32[]{:S(2)}) %collective-permute-start.1) | collective-permute-done | bytes 16416 | tf_op jit(solution)/shard_map/ppermute | solution.py:344
  8.0 0.0 collective-permute-done.refs_1_
  8.1 1.6 %collective-permute-start.3 = (bf16[4,8,128]{2,1,0:T(8,128)(2,1)S(1)}, bf16[4,8,128]{2,1,0:T(8,128)(2,1)S(1)}, u32[]{:S(2)}, u32[]{:S(2)}) collective-permute-start(bf16[4,8,128]{2,1,0:T(8,128)(2,1)S(1)} %get-tuple-element.19), channel_id=1, source_target_pairs={{0,1},{1,0},{2,3},{3,2},{4,5},{5,4},{6,7},{7,6},{8,9},{9,8},{10,11... | collective-permute-start | bytes 24584 | tf_op jit(solution)/shard_map/ppermute | solution.py:344
  9.7 1.6 %collective-permute-start.4 = (bf16[4,8,128]{2,1,0:T(8,128)(2,1)S(1)}, bf16[4,8,128]{2,1,0:T(8,128)(2,1)S(1)}, u32[]{:S(2)}, u32[]{:S(2)}) collective-permute-start(bf16[4,8,128]{2,1,0:T(8,128)(2,1)S(1)} %get-tuple-element.20), channel_id=1, source_target_pairs={{0,2},{1,3},{2,0},{3,1},{4,6},{5,7},{6,4},{7,5},{8,10},{9,11},{10,... | collective-permute-start | bytes 24584 | tf_op jit(solution)/shard_map/ppermute | solution.py:344
  11.2 0.4 %collective-permute-start.5 = (bf16[4,8,128]{2,1,0:T(8,128)(2,1)S(1)}, bf16[4,8,128]{2,1,0:T(8,128)(2,1)S(1)}, u32[]{:S(2)}, u32[]{:S(2)}) collective-permute-start(bf16[4,8,128]{2,1,0:T(8,128)(2,1)S(1)} %get-tuple-element.21), channel_id=1, source_target_pairs={{0,3},{1,2},{2,1},{3,0},{4,7},{5,6},{6,5},{7,4},{8,11},{9,10},{10,... | collective-permute-start | bytes 24584 | tf_op jit(solution)/shard_map/ppermute | solution.py:344
  11.6 2.6 %collective-permute-start.6 = (bf16[4,8,128]{2,1,0:T(8,128)(2,1)S(1)}, bf16[4,8,128]{2,1,0:T(8,128)(2,1)S(1)}, u32[]{:S(2)}, u32[]{:S(2)}) collective-permute-start(bf16[4,8,128]{2,1,0:T(8,128)(2,1)S(1)} %get-tuple-element.22), channel_id=1, source_target_pairs={{0,4},{1,5},{2,6},{3,7},{4,0},{5,1},{6,2},{7,3},{8,12},{9,13},{10,... | collective-permute-start | bytes 24584 | tf_op jit(solution)/shard_map/ppermute | solution.py:344
  14.2 1.3 %collective-permute-start.7 = (bf16[4,8,128]{2,1,0:T(8,128)(2,1)S(1)}, bf16[4,8,128]{2,1,0:T(8,128)(2,1)S(1)}, u32[]{:S(2)}, u32[]{:S(2)}) collective-permute-start(bf16[4,8,128]{2,1,0:T(8,128)(2,1)S(1)} %get-tuple-element.23), channel_id=1, source_target_pairs={{0,5},{1,4},{2,7},{3,6},{4,1},{5,0},{6,3},{7,2},{8,13},{9,12},{10,... | collective-permute-start | bytes 24584 | tf_op jit(solution)/shard_map/ppermute | solution.py:344
  15.5 0.0 collective-permute-done.3.refs_1_
  15.5 3.6 %collective-permute-start.8 = (bf16[4,8,128]{2,1,0:T(8,128)(2,1)S(1)}, bf16[4,8,128]{2,1,0:T(8,128)(2,1)S(1)}, u32[]{:S(2)}, u32[]{:S(2)}) collective-permute-start(bf16[4,8,128]{2,1,0:T(8,128)(2,1)S(1)} %get-tuple-element.24), channel_id=1, source_target_pairs={{0,6},{1,7},{2,4},{3,5},{4,2},{5,3},{6,0},{7,1},{8,14},{9,15},{10,... | collective-permute-start | bytes 24584 | tf_op jit(solution)/shard_map/ppermute | solution.py:344
  19.1 0.0 collective-permute-done.4.refs_2_
  19.1 0.2 collective-permute-start.9
  19.3 1.7 %stick_tables.1 = (bf16[2,256,256]{2,1,0:T(8,128)(2,1)S(1)}, bf16[256,256]{1,0:T(8,128)(2,1)S(1)}) custom-call(s32[1,256]{1,0:T(1,128)} %bitcast.5), custom_call_target="tpu_custom_call" | custom-call | flops 5242880 | bytes 786432 | tf_op jit(solution)/shard_map/stick_tables/pallas_call | solution.py:390
  21.0 0.0 collective-permute-done.5.refs_3_
  21.0 0.0 collective-permute-done.6.refs_4_
  21.0 0.0 collective-permute-done.7.refs_5_
  21.1 0.0 collective-permute-done.8.refs_6_
  21.1 4.4 %collective-permute-done.9.refs_7_ = bf16[4,8,128]{2,1,0:T(8,128)(2,1)S(1)} collective-permute-done((bf16[4,8,128]{2,1,0:T(8,128)(2,1)S(1)}, bf16[4,8,128]{2,1,0:T(8,128)(2,1)S(1)}, u32[]{:S(2)}, u32[]{:S(2)}) %collective-permute-start.9) | collective-permute-done | bytes 8224 | tf_op jit(solution)/shard_map/ppermute | solution.py:344
  25.5 3.1 %plane_density.1 = f32[2,256,256]{2,1,0:T(8,128)} custom-call(bf16[4,8,128]{2,1,0:T(8,128)(2,1)S(1)} %get-tuple-element.18.refs_0_, bf16[4,8,128]{2,1,0:T(8,128)(2,1)S(1)} %collective-permute-done.3.refs_1_, bf16[4,8,128]{2,1,0:T(8,128)(2,1)S(1)} %collective-permute-done.4.refs_2_, bf16[4,8,128]{2,1,0:T(8,128)(2,1)S(1)} %collective-permute-done.5.refs_3_, ...), custom_call_target="tpu_custom_call" | custom-call | tf_op jit(solution)/shard_map/plane_density/pallas_call | solution.py:410
  (1 shorter events, 0.0 us)
Async XLA Ops:
  1.9 3.9 %collective-permute-start.2 = (bf16[8,8,128]{2,1,0:T(8,128)(2,1)S(1)}, bf16[8,8,128]{2,1,0:T(8,128)(2,1)S(1)}, u32[]{:S(2)}, u32[]{:S(2)}) collective-permute-start(bf16[8,8,128]{2,1,0:T(8,128)(2,1)S(1)} %stick_values.1.refs_0_), channel_id=1, source_target_pairs={{0,24},{8,16},{16,8},{24,0},{1,25},{9,17},{17,9},{25,1},{2,26},{10... | collective-permute-start | bytes 49160 | tf_op jit(solution)/shard_map/ppermute | solution.py:344
  4.3 3.7 %collective-permute-start.1 = (bf16[8,8,128]{2,1,0:T(8,128)(2,1)S(1)}, bf16[8,8,128]{2,1,0:T(8,128)(2,1)S(1)}, u32[]{:S(2)}, u32[]{:S(2)}) collective-permute-start(bf16[8,8,128]{2,1,0:T(8,128)(2,1)S(1)} %stick_values.1.refs_0_), channel_id=1, source_target_pairs={{0,16},{8,24},{16,0},{24,8},{1,17},{9,25},{17,1},{25,9},{2,18},{10... | collective-permute-start | bytes 49160 | tf_op jit(solution)/shard_map/ppermute | solution.py:344
  4.9 3.1 %collective-permute-start = (bf16[8,8,128]{2,1,0:T(8,128)(2,1)S(1)}, bf16[8,8,128]{2,1,0:T(8,128)(2,1)S(1)}, u32[]{:S(2)}, u32[]{:S(2)}) collective-permute-start(bf16[8,8,128]{2,1,0:T(8,128)(2,1)S(1)} %stick_values.1.refs_0_), channel_id=1, source_target_pairs={{0,8},{8,0},{16,24},{24,16},{1,9},{9,1},{17,25},{25,17},{2,10},{10... | collective-permute-start | bytes 49160 | tf_op jit(solution)/shard_map/ppermute | solution.py:344
  8.1 7.4 %collective-permute-start.3 = (bf16[4,8,128]{2,1,0:T(8,128)(2,1)S(1)}, bf16[4,8,128]{2,1,0:T(8,128)(2,1)S(1)}, u32[]{:S(2)}, u32[]{:S(2)}) collective-permute-start(bf16[4,8,128]{2,1,0:T(8,128)(2,1)S(1)} %get-tuple-element.19), channel_id=1, source_target_pairs={{0,1},{1,0},{2,3},{3,2},{4,5},{5,4},{6,7},{7,6},{8,9},{9,8},{10,11... | collective-permute-start | bytes 24584 | tf_op jit(solution)/shard_map/ppermute | solution.py:344
  9.7 9.5 %collective-permute-start.4 = (bf16[4,8,128]{2,1,0:T(8,128)(2,1)S(1)}, bf16[4,8,128]{2,1,0:T(8,128)(2,1)S(1)}, u32[]{:S(2)}, u32[]{:S(2)}) collective-permute-start(bf16[4,8,128]{2,1,0:T(8,128)(2,1)S(1)} %get-tuple-element.20), channel_id=1, source_target_pairs={{0,2},{1,3},{2,0},{3,1},{4,6},{5,7},{6,4},{7,5},{8,10},{9,11},{10,... | collective-permute-start | bytes 24584 | tf_op jit(solution)/shard_map/ppermute | solution.py:344
  11.2 9.8 %collective-permute-start.5 = (bf16[4,8,128]{2,1,0:T(8,128)(2,1)S(1)}, bf16[4,8,128]{2,1,0:T(8,128)(2,1)S(1)}, u32[]{:S(2)}, u32[]{:S(2)}) collective-permute-start(bf16[4,8,128]{2,1,0:T(8,128)(2,1)S(1)} %get-tuple-element.21), channel_id=1, source_target_pairs={{0,3},{1,2},{2,1},{3,0},{4,7},{5,6},{6,5},{7,4},{8,11},{9,10},{10,... | collective-permute-start | bytes 24584 | tf_op jit(solution)/shard_map/ppermute | solution.py:344
  11.6 9.4 %collective-permute-start.6 = (bf16[4,8,128]{2,1,0:T(8,128)(2,1)S(1)}, bf16[4,8,128]{2,1,0:T(8,128)(2,1)S(1)}, u32[]{:S(2)}, u32[]{:S(2)}) collective-permute-start(bf16[4,8,128]{2,1,0:T(8,128)(2,1)S(1)} %get-tuple-element.22), channel_id=1, source_target_pairs={{0,4},{1,5},{2,6},{3,7},{4,0},{5,1},{6,2},{7,3},{8,12},{9,13},{10,... | collective-permute-start | bytes 24584 | tf_op jit(solution)/shard_map/ppermute | solution.py:344
  14.2 6.8 %collective-permute-start.7 = (bf16[4,8,128]{2,1,0:T(8,128)(2,1)S(1)}, bf16[4,8,128]{2,1,0:T(8,128)(2,1)S(1)}, u32[]{:S(2)}, u32[]{:S(2)}) collective-permute-start(bf16[4,8,128]{2,1,0:T(8,128)(2,1)S(1)} %get-tuple-element.23), channel_id=1, source_target_pairs={{0,5},{1,4},{2,7},{3,6},{4,1},{5,0},{6,3},{7,2},{8,13},{9,12},{10,... | collective-permute-start | bytes 24584 | tf_op jit(solution)/shard_map/ppermute | solution.py:344
  15.5 5.5 %collective-permute-start.8 = (bf16[4,8,128]{2,1,0:T(8,128)(2,1)S(1)}, bf16[4,8,128]{2,1,0:T(8,128)(2,1)S(1)}, u32[]{:S(2)}, u32[]{:S(2)}) collective-permute-start(bf16[4,8,128]{2,1,0:T(8,128)(2,1)S(1)} %get-tuple-element.24), channel_id=1, source_target_pairs={{0,6},{1,7},{2,4},{3,5},{4,2},{5,3},{6,0},{7,1},{8,14},{9,15},{10,... | collective-permute-start | bytes 24584 | tf_op jit(solution)/shard_map/ppermute | solution.py:344
  19.1 6.3 %collective-permute-start.9 = (bf16[4,8,128]{2,1,0:T(8,128)(2,1)S(1)}, bf16[4,8,128]{2,1,0:T(8,128)(2,1)S(1)}, u32[]{:S(2)}, u32[]{:S(2)}) collective-permute-start(bf16[4,8,128]{2,1,0:T(8,128)(2,1)S(1)} %get-tuple-element.25), channel_id=1, source_target_pairs={{0,7},{1,6},{2,5},{3,4},{4,3},{5,2},{6,1},{7,0},{8,15},{9,14},{10,... | collective-permute-start | bytes 24584 | tf_op jit(solution)/shard_map/ppermute | solution.py:344

commit v4 on v3

--- a/solution.py
+++ b/solution.py
@@ -106,7 +106,7 @@
     grid_len = coeff_ref.shape[1]
     sticks = coeff_ref.shape[0] // (2 * in_count)
     plane_count = plane_ref.shape[0]
-    pw_count = out_ref.shape[0]
+    pw_count = lax.axis_size("pw")
     own_planes = plane_count // pw_count
     own_bands = occupation_ref.shape[0]
     row_count = 2 * out_count * sticks
@@ -186,34 +186,18 @@
         occupied = jnp.where(
             iota((sticks, lanes), 1) == lane, occupation_ref[own_band], occupied
         )
-    out_ref[...] = (message + occupied.astype(jnp.float32)[None]).astype(out_ref.dtype)
-
-
-def regroup_kernel(*refs):
-    band_count = refs[-1].shape[0]
-    pw_index = lax.axis_index("pw")
-    for offset, out_ref in enumerate(refs[band_count:]):
-        for place, gathered_ref in enumerate(refs[:band_count]):
-            out_ref[place] = gathered_ref[pw_index ^ offset]
-
-
-def table_kernel(grid_len, sticks, column_hbm, left_ref, right_ref, column_ref, sem):
+    message = (message + occupied.astype(jnp.float32)[None]).astype(out_ref.dtype)
+    for band in range(out_ref.shape[0] // pw_count):
+        out_ref[band * pw_count : (band + 1) * pw_count] = message
+
+
+def table_kernel(grid_len, column_hbm, left_ref, right_ref, column_ref, sem):
     copy = pltpu.make_async_copy(column_hbm, column_ref, sem)
     copy.start()
     copy.wait()
     count = column_ref.shape[1]
     half = grid_len // 2
-    me = lax.axis_index("band") * lax.axis_size("pw") + lax.axis_index("pw")
-    columns = jnp.broadcast_to(column_ref[...], (8, count))
-    stride = sticks
-    while stride < count:
-        high = cut(iota((8, count), 1), stride) & 1
-        exchanged = jnp.where(
-            high == 1, pltpu.roll(columns, stride, 1), pltpu.roll(columns, count - stride, 1)
-        )
-        columns = jnp.where(cut(me * sticks, stride) & 1 == 1, exchanged, columns)
-        stride *= 2
-    columns = columns[:1]
+    columns = column_ref[...]
     turns = iota((grid_len, count), 0) * cut(columns, grid_len)
     left_ref[0] = cosine(turns, grid_len).astype(jnp.bfloat16)
     left_ref[1] = sine(turns, grid_len).astype(jnp.bfloat16)
@@ -228,9 +212,15 @@
     bands,
     own_planes,
     norm_factor,
-    *refs,
+    message_ref,
+    left_ref,
+    right_ref,
+    out_ref,
+    value_ref,
+    weight_ref,
+    held_ref,
+    sem,
 ):
-    *arrived, left_ref, right_ref, out_ref, message_ref, value_ref, weight_ref, held_ref, sem = refs
     chunks, rows, chunk = value_ref.shape
     grid_len = out_ref.shape[1]
     half = grid_len // 2
@@ -242,10 +232,6 @@
     select = (iota((rows + bands, lanes), 0) == iota((rows + bands, lanes), 1)).astype(
         jnp.bfloat16
     )
-
-    for offset, arrived_ref in enumerate(arrived):
-        for place in range(arrived_ref.shape[0]):
-            message_ref[place * len(arrived) + offset] = arrived_ref[place]
 
     def turn(index, peak):
         pieces = chunk // sticks
@@ -327,6 +313,7 @@
 def shards(coeffs, rotation_matrix, stick_length, stick_column, plane_index, occupation):
     band_count = lax.axis_size("band")
     pw_count = lax.axis_size("pw")
+    devices = band_count * pw_count
     in_count, sticks, grid_len = coeffs.shape[1:]
     bands = rotation_matrix.shape[2]
     stick_count = stick_column.shape[0]
@@ -339,13 +326,9 @@
     table_bytes = 6 * grid_len * stick_count
     message_bytes = 2 * stick_count * lanes
 
-    def exchange(array, axis, offset):
-        count = lax.axis_size(axis)
-        return lax.ppermute(array, axis, [(place, place ^ offset) for place in range(count)])
-
     messages = pl.pallas_call(
         stick_kernel,
-        out_shape=jax.ShapeDtypeStruct((pw_count, sticks, lanes), jnp.bfloat16),
+        out_shape=jax.ShapeDtypeStruct((devices, sticks, lanes), jnp.bfloat16),
         in_specs=[hbm] * 5,
         out_specs=vmem,
         scratch_shapes=[
@@ -356,7 +339,7 @@
             pltpu.VMEM((2 * in_count * sticks, grid_len), jnp.bfloat16),
             pltpu.SemaphoreType.DMA((5,)),
         ],
-        compiler_params=room(),
+        compiler_params=room(2 * message_bytes),
         name="stick_values",
     )(
         *(
@@ -370,25 +353,9 @@
             )
         )
     )
-    gathered = [messages] + [exchange(messages, "band", place) for place in range(1, band_count)]
-    parcel = jax.ShapeDtypeStruct((band_count, sticks, lanes), jnp.bfloat16)
-    parcels = pl.pallas_call(
-        regroup_kernel,
-        out_shape=(parcel,) * pw_count,
-        in_specs=[vmem] * band_count,
-        out_specs=(vmem,) * pw_count,
-        compiler_params=room(message_bytes),
-        name="regroup",
-    )(*gathered)
-    arrived = [parcels[0]] + [
-        exchange(parcels[offset], "pw", offset) for offset in range(pw_count - 1, 0, -1)
-    ][::-1]
-    column_row, own = lax.optimization_barrier(
-        (stick_column.reshape(1, stick_count), parcels[0])
-    )
-    arrived[0] = own
+    arrived = lax.all_to_all(messages, ("band", "pw"), split_axis=0, concat_axis=0, tiled=True)
     left, right = pl.pallas_call(
-        functools.partial(table_kernel, grid_len, sticks),
+        functools.partial(table_kernel, grid_len),
         out_shape=(
             jax.ShapeDtypeStruct((2, grid_len, stick_count), jnp.bfloat16),
             jax.ShapeDtypeStruct((stick_count, grid_len), jnp.bfloat16),
@@ -403,17 +370,16 @@
             transcendentals=0,
         ),
         name="stick_tables",
-    )(pltpu.with_memory_space_constraint(column_row, pltpu.HBM))
+    )(pltpu.with_memory_space_constraint(stick_column.reshape(1, stick_count), pltpu.HBM))
     chunk = min(grid_len, stick_count)
     norm_factor = 1.0 / float(bands * stick_count * grid_len)
     blocks = own_planes * (grid_len // math.gcd(grid_len, P_BLOCK))
     return pl.pallas_call(
         functools.partial(plane_kernel, bands, own_planes, norm_factor),
         out_shape=jax.ShapeDtypeStruct((own_planes, grid_len, grid_len), jnp.float32),
-        in_specs=[vmem] * (pw_count + 2),
+        in_specs=[vmem] * 3,
         out_specs=hbm,
         scratch_shapes=[
-            pltpu.VMEM((band_count * pw_count, sticks, lanes), jnp.bfloat16),
             pltpu.VMEM((stick_count // chunk, rows, chunk), jnp.float32),
             pltpu.VMEM((bands, LANES), jnp.float32),
             pltpu.VMEM((own_planes, grid_len, grid_len), jnp.float32),
@@ -421,7 +387,7 @@
         ],
         compiler_params=room(table_bytes, message_bytes),
         name="plane_density",
-    )(*arrived, left, right)
+    )(arrived, left, right)
 
 
 def solution(mesh):

time: 28.7 us -> 20.3 us (0.71)
  starting transfers between devices: 14.3 us -> 7.3 us
  waiting for transfers between devices: 7.47 us -> 5.85 us
    ppermute x10 -> x0, starting transfers between devices: 14.3 us -> none  [exchange(): lax.ppermute(array, axis, [(place, place ^ offset) for place in range(cou...]
    ppermute x10 -> x0, waiting for transfers between devices: 7.47 us -> none  [exchange(): lax.ppermute(array, axis, [(place, place ^ offset) for place in range(cou...]
    all_to_all x0 -> x1, starting transfers between devices: none -> 7.3 us  [shards(): lax.all_to_all(messages, ('band', 'pw'), split_axis=0, concat_axis=0, til...]
    all_to_all x0 -> x1, waiting for transfers between devices: none -> 5.85 us  [shards(): lax.all_to_all(messages, ('band', 'pw'), split_axis=0, concat_axis=0, til...]
    pallas_call x3 -> x2, Pallas kernels: 3.61 us -> 3.9 us  [the longest x1 2.48 us: shards(): pl.pallas_call(stick_kernel, out_shape=jax.ShapeDtypeStruct((devices, sti...]
  transfers between devices with their start and end apart: 10 -> 1, of which waited for: 3 -> 1; matrix products, arithmetic and copies ran while one was open for 0% -> 0% of each run, Pallas kernels for 6% -> 7%
where the time goes in v4:
time: 20.3 us; the launch traced here: 20.1 us
  starting transfers between devices  7.3 us (36%)
  Pallas kernels  6.91 us (34%)
  waiting for transfers between devices  5.85 us (29%)
    all_to_all x1, starting transfers between devices, shards(): lax.all_to_all(messages, ('band', 'pw'), split_axis=0, concat_axis=0, til...  7.3 us
    all_to_all x1, waiting for transfers between devices, shards(): lax.all_to_all(messages, ('band', 'pw'), split_axis=0, concat_axis=0, til...  5.85 us
    pallas_call x1, Pallas kernels, shards(): pl.pallas_call(functools.partial(plane_kernel, bands, own_planes, norm_fa...  3 us
    pallas_call x1, Pallas kernels, shards(): pl.pallas_call(stick_kernel, out_shape=jax.ShapeDtypeStruct((devices, sti...  2.48 us
    pallas_call x1, Pallas kernels, shards(): pl.pallas_call(functools.partial(table_kernel, grid_len), out_shape=(jax....  1.42 us
  transfers between devices with their start and end apart: 1, of which 1 were waited for; matrix products, arithmetic and copies ran while one was open for 0% of the time, Pallas kernels for 7%

profile of v4, /device:TPU:0, one launch (start us, length us, event | category | flops | bytes accessed | tf_op | source)
XLA Modules:
  0.0 20.1 jit_solution(6850980317909074090)
XLA Ops:
  0.0 2.5 %stick_values.1 = bf16[32,8,128]{2,1,0:T(8,128)(2,1)} custom-call(s32[256]{0:T(256)} %length_hbm.1, s32[16]{0:T(128)} %plane_hbm.1, s32[2]{0:T(128)} %occupation_hbm.1, bf16[2,8,64]{2,1,0:T(8,128)(2,1)} %bitcast.4, bf16[1024,256]{1,0:T(8,128)(2,1)} %bitcast.3), custom_call_target="tpu_custom_call" | custom-call | tf_op jit(solution)/shard_map/stick_values/pallas_call | solution.py:329
  2.5 7.3 %all-to-all-start = ((bf16[32,8,128]{2,1,0:T(8,128)(2,1)}), bf16[32,8,128]{2,1,0:T(8,128)(2,1)S(1)}, u32[]{:S(2)}, u32[]{:S(2)}) async-start(bf16[32,8,128]{2,1,0:T(8,128)(2,1)} %stick_values.1), calls=%async_computation | async-start | bytes 131072 | tf_op jit(solution)/shard_map/all_to_all | solution.py:356
  9.8 1.4 %stick_tables.1 = (bf16[2,256,256]{2,1,0:T(8,128)(2,1)S(1)}, bf16[256,256]{1,0:T(8,128)(2,1)S(1)}) custom-call(s32[1,256]{1,0:T(1,128)} %bitcast.5), custom_call_target="tpu_custom_call" | custom-call | flops 5242880 | bytes 786432 | tf_op jit(solution)/shard_map/stick_tables/pallas_call | solution.py:357
  11.2 5.8 %all-to-all-done.message_ref = bf16[32,8,128]{2,1,0:T(8,128)(2,1)S(1)} async-done(((bf16[32,8,128]{2,1,0:T(8,128)(2,1)}), bf16[32,8,128]{2,1,0:T(8,128)(2,1)S(1)}, u32[]{:S(2)}, u32[]{:S(2)}) %all-to-all-start) | async-done | bytes 65568 | tf_op jit(solution)/shard_map/all_to_all | solution.py:356
  17.1 3.0 %plane_density.1 = f32[2,256,256]{2,1,0:T(8,128)} custom-call(bf16[32,8,128]{2,1,0:T(8,128)(2,1)S(1)} %all-to-all-done.message_ref, bf16[2,256,256]{2,1,0:T(8,128)(2,1)S(1)} %get-tuple-element.7.left_ref, bf16[256,256]{1,0:T(8,128)(2,1)S(1)} %get-tuple-element.8.right_ref), custom_call_target="tpu_custom_call" | custom-call | tf_op jit(solution)/shard_map/plane_density/pallas_call | solution.py:377
Async XLA Ops:
  2.5 14.6 %all-to-all-start = ((bf16[32,8,128]{2,1,0:T(8,128)(2,1)}), bf16[32,8,128]{2,1,0:T(8,128)(2,1)S(1)}, u32[]{:S(2)}, u32[]{:S(2)}) async-start(bf16[32,8,128]{2,1,0:T(8,128)(2,1)} %stick_values.1), calls=%async_computation | async-start | bytes 131072 | tf_op jit(solution)/shard_map/all_to_all | solution.py:356

commit v5 on v4

--- a/solution.py
+++ b/solution.py
@@ -65,6 +65,17 @@
 
 def room(*sizes):
     return pltpu.CompilerParams(vmem_limit_bytes=min(56 * MIB, 16 * MIB + 2 * sum(sizes)))
+
+
+def message_form(sticks, own_planes, bands):
+    spots = own_planes * 2 * bands
+    lanes = -(-spots // LANES) * LANES
+    groups = math.gcd(sticks, lanes // spots)
+    value_rows = sticks // groups
+    rows = 1
+    while rows < value_rows + 1:
+        rows *= 2
+    return groups, value_rows, rows, lanes
 
 
 def spread(scalars, index, shape):
@@ -105,11 +116,12 @@
     out_count, in_count = rotation_ref.shape[1:]
     grid_len = coeff_ref.shape[1]
     sticks = coeff_ref.shape[0] // (2 * in_count)
-    plane_count = plane_ref.shape[0]
+    plane_count = plane_ref.shape[1]
     pw_count = lax.axis_size("pw")
     own_planes = plane_count // pw_count
     own_bands = occupation_ref.shape[0]
     row_count = 2 * out_count * sticks
+    groups, value_rows, message_rows, lanes = message_form(sticks, own_planes, out_count)
     band_index = lax.axis_index("band")
     first_stick = (band_index * pw_count + lax.axis_index("pw")) * sticks
 
@@ -138,70 +150,99 @@
 
     for copy in copies[2:]:
         copy.wait()
-    lengths = [length_ref[first_stick + place] for place in range(sticks)]
-    planes = [plane_ref[place] for place in range(plane_count)]
-    plane_rows = spread(planes, iota((plane_count, grid_len), 0), (plane_count, grid_len))
-    product = iota((plane_count, grid_len), 1) * plane_rows
+    tall = plane_count * message_rows
+    shape = (tall, plane_count)
+    kind = cut(iota(shape, 0), message_rows)
+    plane_of = lax.rem(kind, pw_count) * own_planes + lax.div(kind, pw_count)
+    planes = jnp.broadcast_to(plane_ref[...].astype(jnp.float32), (grid_len, plane_count))
+    plane_rows = dot_last(
+        (plane_of == iota(shape, 1)).astype(jnp.bfloat16), planes.astype(jnp.bfloat16)
+    ).astype(jnp.int32)
+    product = iota((tall, grid_len), 1) * plane_rows
     table = jnp.concatenate([cosine(product, grid_len), sine(product, grid_len)], 0).astype(
         jnp.bfloat16
     )
 
-    shape = (plane_count, row_count)
+    lengths = [length_ref[first_stick + place] for place in range(sticks)]
+    shape = (1, row_count)
     lane_lengths = spread(lengths, wrap(iota(shape, 1), sticks), shape)
-    shift = (lane_lengths >> 1) * spread(planes, iota(shape, 0), shape)
+    repeats = -(-row_count // grid_len)
+    wide_planes = jnp.concatenate([plane_rows] * repeats, 1)[:, :row_count]
+    shift = (lane_lengths >> 1) * wide_planes
     phase_cos = cosine(shift, grid_len)
     phase_sin = sine(shift, grid_len)
+    shape = (tall, row_count)
     real_lane = iota(shape, 1) < row_count // 2
 
     row_lengths = spread(lengths, iota((sticks, grid_len), 0), (sticks, grid_len))
     live = iota((sticks, grid_len), 1) < row_lengths
+
+    stick_of = wrap(iota(shape, 1), sticks)
+    in_row = lax.rem(stick_of, value_rows) == wrap(iota(shape, 0), message_rows)
+    shape = (row_count, lanes)
+    spots = 2 * out_count
+    to_lane = iota(shape, 1)
+    from_stick = wrap(iota(shape, 0), sticks)
+    place = (
+        (cut(iota(shape, 0), sticks) == lax.rem(to_lane, spots))
+        & (lax.div(from_stick, value_rows) == lax.div(to_lane, own_planes * spots))
+    ).astype(jnp.bfloat16)
+    part_rows = pw_count * message_rows
+    shape = (part_rows, lanes)
+    plane_lane = lax.div(lax.rem(iota(shape, 1), own_planes * spots), spots)
+    message = jnp.zeros(shape, jnp.float32)
+    is_occupation = wrap(iota(shape, 0), message_rows) == value_rows
+    for own_band in range(own_bands):
+        lane = band_index * own_bands + own_band
+        message = jnp.where(
+            is_occupation & (iota(shape, 1) == lane),
+            occupation_ref[own_band].astype(jnp.float32),
+            message,
+        )
 
     copies[1].wait()
     rotated = dot(rotation, coeff_ref[...])
     rotated = rotated.reshape(row_count // sticks, sticks, grid_len)
     rotated = jnp.where(live[None], rotated, 0.0).reshape(row_count, grid_len)
     sums = dot_last(table, rotated.astype(jnp.bfloat16))
-    with_cos, with_sin = sums[:plane_count], sums[plane_count:]
+    with_cos, with_sin = sums[:tall], sums[tall:]
     turned = pltpu.roll(with_sin, row_count // 2, 1)
     amplitude = with_cos + jnp.where(real_lane, -turned, turned)
     turned = pltpu.roll(amplitude, row_count // 2, 1) * phase_sin
     values = amplitude * phase_cos + jnp.where(real_lane, turned, -turned)
-
-    lanes = out_ref.shape[2]
-    spots = 2 * out_count
-    tall = jnp.broadcast_to(values[:, None, :], (plane_count, sticks, row_count))
-    own = iota((sticks, row_count), 0) == wrap(iota((sticks, row_count), 1), sticks)
-    tall = jnp.where(own[None], tall, 0.0).reshape(plane_count * sticks, row_count)
-    shape = (row_count, lanes)
-    place = (
-        (cut(iota(shape, 0), sticks) == lax.rem(iota(shape, 1), spots))
-        & (iota(shape, 1) < own_planes * spots)
-    ).astype(jnp.bfloat16)
-    laid = dot(tall.astype(jnp.bfloat16), place).reshape(pw_count, own_planes, sticks, lanes)
-    mine = cut(iota((own_planes, sticks, lanes), 2), spots) == iota((own_planes, sticks, lanes), 0)
-    message = jnp.sum(jnp.where(mine[None], laid, 0.0), 1)
-    occupied = jnp.zeros((sticks, lanes), jnp.int32)
-    for own_band in range(own_bands):
-        lane = own_planes * spots + band_index * own_bands + own_band
-        occupied = jnp.where(
-            iota((sticks, lanes), 1) == lane, occupation_ref[own_band], occupied
-        )
-    message = (message + occupied.astype(jnp.float32)[None]).astype(out_ref.dtype)
+    laid = dot(jnp.where(in_row, values, 0.0).astype(jnp.bfloat16), place)
+    for own_plane in range(own_planes):
+        part = laid[own_plane * part_rows : (own_plane + 1) * part_rows]
+        message += jnp.where(plane_lane == own_plane, part, 0.0)
+    message = message.astype(out_ref.dtype).reshape(pw_count, message_rows, lanes)
     for band in range(out_ref.shape[0] // pw_count):
         out_ref[band * pw_count : (band + 1) * pw_count] = message
 
 
-def table_kernel(grid_len, column_hbm, left_ref, right_ref, column_ref, sem):
+def table_kernel(grid_len, chunk, sticks, value_rows, column_hbm, left_ref, right_ref, column_ref, sem):
     copy = pltpu.make_async_copy(column_hbm, column_ref, sem)
     copy.start()
     copy.wait()
     count = column_ref.shape[1]
     half = grid_len // 2
-    columns = column_ref[...]
-    turns = iota((grid_len, count), 0) * cut(columns, grid_len)
+    shape = (chunk, chunk)
+    to, pieces = iota(shape, 1), chunk // sticks
+    group, rest = lax.div(to, pieces * value_rows), lax.rem(to, pieces * value_rows)
+    source = lax.div(rest, value_rows) * sticks + group * value_rows + lax.rem(rest, value_rows)
+    order = (iota(shape, 0) == source).astype(jnp.bfloat16)
+    columns = jnp.broadcast_to(column_ref[...], (8, count))
+    columns = jnp.where(
+        iota((8, count), 0) == 0, cut(columns, grid_len), wrap(columns, grid_len)
+    ).astype(jnp.float32)
+    ordered = [
+        dot(columns[:, first : first + chunk].astype(jnp.bfloat16), order)
+        for first in range(0, count, chunk)
+    ]
+    columns = jnp.concatenate(ordered, 1).astype(jnp.int32)
+    turns = iota((grid_len, count), 0) * columns[:1]
     left_ref[0] = cosine(turns, grid_len).astype(jnp.bfloat16)
     left_ref[1] = sine(turns, grid_len).astype(jnp.bfloat16)
-    tall = jnp.transpose(jnp.broadcast_to(wrap(columns, grid_len), (half, count)))
+    tall = jnp.transpose(jnp.broadcast_to(columns[1:2], (half, count)))
     freq = iota((count, half), 1)
     right_ref[:, :half] = cosine(tall * freq, grid_len).astype(jnp.bfloat16)
     turns = jnp.where(freq == 0, tall * half, tall * freq + (grid_len - grid_len // 4))
@@ -212,6 +253,7 @@
     bands,
     own_planes,
     norm_factor,
+    sticks,
     message_ref,
     left_ref,
     right_ref,
@@ -224,22 +266,32 @@
     chunks, rows, chunk = value_ref.shape
     grid_len = out_ref.shape[1]
     half = grid_len // 2
-    sticks, lanes = message_ref.shape[1:]
     spots = 2 * bands
     height = math.gcd(grid_len, P_BLOCK)
     blocks = grid_len // height
     group = math.gcd(bands, BAND_GROUP)
-    select = (iota((rows + bands, lanes), 0) == iota((rows + bands, lanes), 1)).astype(
-        jnp.bfloat16
-    )
+    groups, value_rows, message_rows, lanes = message_form(sticks, own_planes, bands)
+    source_rows = chunk // sticks * message_rows
+    shape = (chunk, source_rows)
+    wanted = lax.rem(iota(shape, 0), chunk // groups)
+    gather = (
+        lax.div(wanted, value_rows) * message_rows + lax.rem(wanted, value_rows) == iota(shape, 1)
+    ).astype(jnp.bfloat16)
+    shape = (chunk, lanes)
+    in_group = lax.div(iota(shape, 0), chunk // groups) == lax.div(iota(shape, 1), rows)
+    shape = (rows, lanes)
+    select = (lax.rem(iota(shape, 1), rows) == iota(shape, 0)).astype(jnp.bfloat16)
+    shape = (bands, lanes)
+    select_band = (iota(shape, 1) == iota(shape, 0)).astype(jnp.bfloat16)
+    is_occupation = wrap(iota((bands, source_rows), 1), message_rows) == value_rows
 
     def turn(index, peak):
         pieces = chunk // sticks
-        picked = dot_last(
-            select, message_ref[pl.ds(index * pieces, pieces)].reshape(chunk, lanes)
-        )
-        value_ref[index] = picked[:rows]
-        return jnp.maximum(peak, jnp.max(picked[rows:], 1, keepdims=True))
+        message = message_ref[pl.ds(index * pieces, pieces)].reshape(source_rows, lanes)
+        picked = jnp.where(in_group, dot(gather, message), 0.0).astype(jnp.bfloat16)
+        value_ref[index] = dot_last(select, picked)
+        found = jnp.where(is_occupation, dot_last(select_band, message), 0.0)
+        return jnp.maximum(peak, jnp.max(found, 1, keepdims=True))
 
     peak = loop(chunks, turn, jnp.zeros((bands, 1), jnp.float32))
     weight_ref[...] = jnp.broadcast_to(peak * norm_factor, weight_ref.shape)
@@ -320,20 +372,20 @@
     own_planes = plane_index.shape[0] // pw_count
     spots = 2 * bands
     rows = own_planes * spots
-    lanes = -(-(rows + bands) // LANES) * LANES
+    groups, value_rows, message_rows, lanes = message_form(sticks, own_planes, bands)
     vmem = pl.BlockSpec(memory_space=pltpu.VMEM)
     hbm = pl.BlockSpec(memory_space=pltpu.HBM)
     table_bytes = 6 * grid_len * stick_count
-    message_bytes = 2 * stick_count * lanes
+    message_bytes = 2 * devices * message_rows * lanes
 
     messages = pl.pallas_call(
         stick_kernel,
-        out_shape=jax.ShapeDtypeStruct((devices, sticks, lanes), jnp.bfloat16),
+        out_shape=jax.ShapeDtypeStruct((devices, message_rows, lanes), jnp.bfloat16),
         in_specs=[hbm] * 5,
         out_specs=vmem,
         scratch_shapes=[
             pltpu.SMEM(stick_length.shape, jnp.int32),
-            pltpu.SMEM(plane_index.shape, jnp.int32),
+            pltpu.VMEM((1, plane_index.shape[0]), jnp.int32),
             pltpu.SMEM(occupation.shape, jnp.int32),
             pltpu.VMEM((2, bands, in_count), jnp.bfloat16),
             pltpu.VMEM((2 * in_count * sticks, grid_len), jnp.bfloat16),
@@ -346,7 +398,7 @@
             pltpu.with_memory_space_constraint(array, pltpu.HBM)
             for array in (
                 stick_length,
-                plane_index,
+                plane_index.reshape(1, -1),
                 occupation,
                 jnp.swapaxes(rotation_matrix, 1, 2),
                 coeffs.reshape(2 * in_count * sticks, grid_len),
@@ -354,8 +406,9 @@
         )
     )
     arrived = lax.all_to_all(messages, ("band", "pw"), split_axis=0, concat_axis=0, tiled=True)
+    chunk = min(grid_len, stick_count)
     left, right = pl.pallas_call(
-        functools.partial(table_kernel, grid_len),
+        functools.partial(table_kernel, grid_len, chunk, sticks, value_rows),
         out_shape=(
             jax.ShapeDtypeStruct((2, grid_len, stick_count), jnp.bfloat16),
             jax.ShapeDtypeStruct((stick_count, grid_len), jnp.bfloat16),
@@ -371,11 +424,10 @@
         ),
         name="stick_tables",
     )(pltpu.with_memory_space_constraint(stick_column.reshape(1, stick_count), pltpu.HBM))
-    chunk = min(grid_len, stick_count)
     norm_factor = 1.0 / float(bands * stick_count * grid_len)
     blocks = own_planes * (grid_len // math.gcd(grid_len, P_BLOCK))
     return pl.pallas_call(
-        functools.partial(plane_kernel, bands, own_planes, norm_factor),
+        functools.partial(plane_kernel, bands, own_planes, norm_factor, sticks),
         out_shape=jax.ShapeDtypeStruct((own_planes, grid_len, grid_len), jnp.float32),
         in_specs=[vmem] * 3,
         out_specs=hbm,

time: 20.3 us -> 20.6 us (1.015)
  Pallas kernels: 6.91 us -> 7.36 us
    pallas_call x2, Pallas kernels: 3.9 us -> 4.17 us  [the longest x1 2.73 us: shards(): pl.pallas_call(stick_kernel, out_shape=jax.ShapeDtypeStruct((devices, mes...]
where the time goes in v5:
time: 20.6 us; the launch traced here: 20.4 us
  Pallas kernels  7.36 us (36%)
  starting transfers between devices  7.3 us (35%)
  waiting for transfers between devices  5.73 us (28%)
    all_to_all x1, starting transfers between devices, shards(): lax.all_to_all(messages, ('band', 'pw'), split_axis=0, concat_axis=0, til...  7.3 us
    all_to_all x1, waiting for transfers between devices, shards(): lax.all_to_all(messages, ('band', 'pw'), split_axis=0, concat_axis=0, til...  5.73 us
    pallas_call x1, Pallas kernels, shards(): pl.pallas_call(functools.partial(plane_kernel, bands, own_planes, norm_fa...  3.18 us
    pallas_call x1, Pallas kernels, shards(): pl.pallas_call(stick_kernel, out_shape=jax.ShapeDtypeStruct((devices, mes...  2.73 us
    pallas_call x1, Pallas kernels, shards(): pl.pallas_call(functools.partial(table_kernel, grid_len, chunk, sticks, v...  1.45 us
  transfers between devices with their start and end apart: 1, of which 1 were waited for; matrix products, arithmetic and copies ran while one was open for 0% of the time, Pallas kernels for 7%

profile of v5, /device:TPU:0, one launch (start us, length us, event | category | flops | bytes accessed | tf_op | source)
XLA Modules:
  0.0 20.4 jit_solution(3319429953366290179)
XLA Ops:
  0.0 2.7 %stick_values.1 = bf16[32,4,128]{2,1,0:T(4,128)(2,1)} custom-call(s32[256]{0:T(256)} %length_hbm.1, s32[1,16]{1,0:T(1,128)} %bitcast.6, s32[2]{0:T(128)} %occupation_hbm.1, bf16[2,8,64]{2,1,0:T(8,128)(2,1)} %bitcast.5, bf16[1024,256]{1,0:T(8,128)(2,1)} %bitcast.4), custom_call_target="tpu_custom_call" | custom-call | tf_op jit(solution)/shard_map/stick_values/pallas_call | solution.py:381
  2.7 7.3 %all-to-all-start = ((bf16[32,4,128]{2,1,0:T(4,128)(2,1)}), bf16[32,4,128]{2,1,0:T(4,128)(2,1)S(1)}, u32[]{:S(2)}, u32[]{:S(2)}) async-start(bf16[32,4,128]{2,1,0:T(4,128)(2,1)} %stick_values.1), calls=%async_computation | async-start | bytes 65536 | tf_op jit(solution)/shard_map/all_to_all | solution.py:408
  10.0 1.4 %stick_tables.1 = (bf16[2,256,256]{2,1,0:T(8,128)(2,1)S(1)}, bf16[256,256]{1,0:T(8,128)(2,1)S(1)}) custom-call(s32[1,256]{1,0:T(1,128)} %bitcast.7), custom_call_target="tpu_custom_call" | custom-call | flops 5242880 | bytes 786432 | tf_op jit(solution)/shard_map/stick_tables/pallas_call | solution.py:410
  11.5 5.7 %all-to-all-done.message_ref = bf16[32,4,128]{2,1,0:T(4,128)(2,1)S(1)} async-done(((bf16[32,4,128]{2,1,0:T(4,128)(2,1)}), bf16[32,4,128]{2,1,0:T(4,128)(2,1)S(1)}, u32[]{:S(2)}, u32[]{:S(2)}) %all-to-all-start) | async-done | bytes 32800 | tf_op jit(solution)/shard_map/all_to_all | solution.py:408
  17.2 3.2 %plane_density.1 = f32[2,256,256]{2,1,0:T(8,128)} custom-call(bf16[32,4,128]{2,1,0:T(4,128)(2,1)S(1)} %all-to-all-done.message_ref, bf16[2,256,256]{2,1,0:T(8,128)(2,1)S(1)} %get-tuple-element.7.left_ref, bf16[256,256]{1,0:T(8,128)(2,1)S(1)} %get-tuple-element.8.right_ref), custom_call_target="tpu_custom_call" | custom-call | tf_op jit(solution)/shard_map/plane_density/pallas_call | solution.py:429
Async XLA Ops:
  2.7 14.5 %all-to-all-start = ((bf16[32,4,128]{2,1,0:T(4,128)(2,1)}), bf16[32,4,128]{2,1,0:T(4,128)(2,1)S(1)}, u32[]{:S(2)}, u32[]{:S(2)}) async-start(bf16[32,4,128]{2,1,0:T(4,128)(2,1)} %stick_values.1), calls=%async_computation | async-start | bytes 65536 | tf_op jit(solution)/shard_map/all_to_all | solution.py:408

commit v6 on v4

--- a/solution.py
+++ b/solution.py
@@ -10,7 +10,7 @@
 
 LANES = 128
 PACK = 16
-P_BLOCK = 64
+P_BLOCK = 32
 BAND_GROUP = 8
 MIB = 1024 * 1024
 
@@ -328,7 +328,7 @@
 
     messages = pl.pallas_call(
         stick_kernel,
-        out_shape=jax.ShapeDtypeStruct((devices, sticks, lanes), jnp.bfloat16),
+        out_shape=pltpu.VMEM((devices, sticks, lanes), jnp.bfloat16),
         in_specs=[hbm] * 5,
         out_specs=vmem,
         scratch_shapes=[

time: 20.3 us -> 20.2 us (level)
  no operation moved by 1% of the time
where the time goes in v6:
time: 20.2 us; the launch traced here: 20 us
  starting transfers between devices  7.3 us (36%)
  Pallas kernels  6.83 us (34%)
  waiting for transfers between devices  5.85 us (29%)
    all_to_all x1, starting transfers between devices, shards(): lax.all_to_all(messages, ('band', 'pw'), split_axis=0, concat_axis=0, til...  7.3 us
    all_to_all x1, waiting for transfers between devices, shards(): lax.all_to_all(messages, ('band', 'pw'), split_axis=0, concat_axis=0, til...  5.85 us
    pallas_call x1, Pallas kernels, shards(): pl.pallas_call(functools.partial(plane_kernel, bands, own_planes, norm_fa...  2.93 us
    pallas_call x1, Pallas kernels, shards(): pl.pallas_call(stick_kernel, out_shape=pltpu.VMEM((devices, sticks, lanes...  2.48 us
    pallas_call x1, Pallas kernels, shards(): pl.pallas_call(functools.partial(table_kernel, grid_len), out_shape=(jax....  1.42 us
  transfers between devices with their start and end apart: 1, of which 1 were waited for; matrix products, arithmetic and copies ran while one was open for 0% of the time, Pallas kernels for 7%

profile of v6, /device:TPU:0, one launch (start us, length us, event | category | flops | bytes accessed | tf_op | source)
XLA Modules:
  0.0 20.0 jit_solution(8502864909176035701)
XLA Ops:
  0.0 2.5 %stick_values.1 = bf16[32,8,128]{2,1,0:T(8,128)(2,1)} custom-call(s32[256]{0:T(256)} %length_hbm.1, s32[16]{0:T(128)} %plane_hbm.1, s32[2]{0:T(128)} %occupation_hbm.1, bf16[2,8,64]{2,1,0:T(8,128)(2,1)} %bitcast.4, bf16[1024,256]{1,0:T(8,128)(2,1)} %bitcast.3), custom_call_target="tpu_custom_call" | custom-call | tf_op jit(solution)/shard_map/stick_values/pallas_call | solution.py:329
  2.5 7.3 %all-to-all-start = ((bf16[32,8,128]{2,1,0:T(8,128)(2,1)}), bf16[32,8,128]{2,1,0:T(8,128)(2,1)S(1)}, u32[]{:S(2)}, u32[]{:S(2)}) async-start(bf16[32,8,128]{2,1,0:T(8,128)(2,1)} %stick_values.1), calls=%async_computation | async-start | bytes 131072 | tf_op jit(solution)/shard_map/all_to_all | solution.py:356
  9.8 1.4 %stick_tables.1 = (bf16[2,256,256]{2,1,0:T(8,128)(2,1)S(1)}, bf16[256,256]{1,0:T(8,128)(2,1)S(1)}) custom-call(s32[1,256]{1,0:T(1,128)} %bitcast.5), custom_call_target="tpu_custom_call" | custom-call | flops 5242880 | bytes 786432 | tf_op jit(solution)/shard_map/stick_tables/pallas_call | solution.py:357
  11.2 5.8 %all-to-all-done.message_ref = bf16[32,8,128]{2,1,0:T(8,128)(2,1)S(1)} async-done(((bf16[32,8,128]{2,1,0:T(8,128)(2,1)}), bf16[32,8,128]{2,1,0:T(8,128)(2,1)S(1)}, u32[]{:S(2)}, u32[]{:S(2)}) %all-to-all-start) | async-done | bytes 65568 | tf_op jit(solution)/shard_map/all_to_all | solution.py:356
  17.1 2.9 %plane_density.1 = f32[2,256,256]{2,1,0:T(8,128)} custom-call(bf16[32,8,128]{2,1,0:T(8,128)(2,1)S(1)} %all-to-all-done.message_ref, bf16[2,256,256]{2,1,0:T(8,128)(2,1)S(1)} %get-tuple-element.7.left_ref, bf16[256,256]{1,0:T(8,128)(2,1)S(1)} %get-tuple-element.8.right_ref), custom_call_target="tpu_custom_call" | custom-call | tf_op jit(solution)/shard_map/plane_density/pallas_call | solution.py:377
Async XLA Ops:
  2.5 14.6 %all-to-all-start = ((bf16[32,8,128]{2,1,0:T(8,128)(2,1)}), bf16[32,8,128]{2,1,0:T(8,128)(2,1)S(1)}, u32[]{:S(2)}, u32[]{:S(2)}) async-start(bf16[32,8,128]{2,1,0:T(8,128)(2,1)} %stick_values.1), calls=%async_computation | async-start | bytes 131072 | tf_op jit(solution)/shard_map/all_to_all | solution.py:356

commit v7 on v6

--- a/solution.py
+++ b/solution.py
@@ -187,17 +187,19 @@
             iota((sticks, lanes), 1) == lane, occupation_ref[own_band], occupied
         )
     message = (message + occupied.astype(jnp.float32)[None]).astype(out_ref.dtype)
+    message = jnp.concatenate([message[pw_count - 1 :], message[: pw_count - 1]], 0)
     for band in range(out_ref.shape[0] // pw_count):
         out_ref[band * pw_count : (band + 1) * pw_count] = message
 
 
-def table_kernel(grid_len, column_hbm, left_ref, right_ref, column_ref, sem):
+def table_kernel(grid_len, sticks, column_hbm, left_ref, right_ref, column_ref, sem):
     copy = pltpu.make_async_copy(column_hbm, column_ref, sem)
     copy.start()
     copy.wait()
     count = column_ref.shape[1]
     half = grid_len // 2
-    columns = column_ref[...]
+    columns = jnp.broadcast_to(column_ref[...], (8, count))
+    columns = pltpu.roll(columns, sticks, 1)[:1]
     turns = iota((grid_len, count), 0) * cut(columns, grid_len)
     left_ref[0] = cosine(turns, grid_len).astype(jnp.bfloat16)
     left_ref[1] = sine(turns, grid_len).astype(jnp.bfloat16)
@@ -353,9 +355,16 @@
             )
         )
     )
-    arrived = lax.all_to_all(messages, ("band", "pw"), split_axis=0, concat_axis=0, tiled=True)
+    arrived = lax.all_to_all(
+        messages,
+        ("band", "pw"),
+        split_axis=0,
+        concat_axis=0,
+        axis_index_groups=[[devices - 1, *range(devices - 1)]],
+        tiled=True,
+    )
     left, right = pl.pallas_call(
-        functools.partial(table_kernel, grid_len),
+        functools.partial(table_kernel, grid_len, sticks),
         out_shape=(
             jax.ShapeDtypeStruct((2, grid_len, stick_count), jnp.bfloat16),
             jax.ShapeDtypeStruct((stick_count, grid_len), jnp.bfloat16),

time: 20.2 us -> 20.2 us (level)
  transfers between devices with their start and end apart: 1 -> 1, of which waited for: 1 -> 1; matrix products, arithmetic and copies ran while one was open for 0% -> 0% of each run, Pallas kernels for 7% -> 8%
where the time goes in v7:
time: 20.2 us; the launch traced here: 20 us
  starting transfers between devices  7.3 us (36%)
  Pallas kernels  6.93 us (34%)
  waiting for transfers between devices  5.74 us (28%)
    all_to_all x1, starting transfers between devices, shards(): lax.all_to_all(messages, ('band', 'pw'), split_axis=0, concat_axis=0, axi...  7.3 us
    all_to_all x1, waiting for transfers between devices, shards(): lax.all_to_all(messages, ('band', 'pw'), split_axis=0, concat_axis=0, axi...  5.74 us
    pallas_call x1, Pallas kernels, shards(): pl.pallas_call(functools.partial(plane_kernel, bands, own_planes, norm_fa...  2.92 us
    pallas_call x1, Pallas kernels, shards(): pl.pallas_call(stick_kernel, out_shape=pltpu.VMEM((devices, sticks, lanes...  2.48 us
    pallas_call x1, Pallas kernels, shards(): pl.pallas_call(functools.partial(table_kernel, grid_len, sticks), out_sha...  1.53 us
  transfers between devices with their start and end apart: 1, of which 1 were waited for; matrix products, arithmetic and copies ran while one was open for 0% of the time, Pallas kernels for 8%

profile of v7, /device:TPU:0, one launch (start us, length us, event | category | flops | bytes accessed | tf_op | source)
XLA Modules:
  0.0 20.0 jit_solution(16972139841540776686)
XLA Ops:
  0.0 2.5 %stick_values.1 = bf16[32,8,128]{2,1,0:T(8,128)(2,1)} custom-call(s32[256]{0:T(256)} %length_hbm.1, s32[16]{0:T(128)} %plane_hbm.1, s32[2]{0:T(128)} %occupation_hbm.1, bf16[2,8,64]{2,1,0:T(8,128)(2,1)} %bitcast.4, bf16[1024,256]{1,0:T(8,128)(2,1)} %bitcast.3), custom_call_target="tpu_custom_call" | custom-call | tf_op jit(solution)/shard_map/stick_values/pallas_call | solution.py:331
  2.5 7.3 %all-to-all-start = ((bf16[32,8,128]{2,1,0:T(8,128)(2,1)}), bf16[32,8,128]{2,1,0:T(8,128)(2,1)S(1)}, u32[]{:S(2)}, u32[]{:S(2)}) async-start(bf16[32,8,128]{2,1,0:T(8,128)(2,1)} %stick_values.1), calls=%async_computation | async-start | bytes 131072 | tf_op jit(solution)/shard_map/all_to_all | solution.py:358
  9.8 1.5 %stick_tables.1 = (bf16[2,256,256]{2,1,0:T(8,128)(2,1)S(1)}, bf16[256,256]{1,0:T(8,128)(2,1)S(1)}) custom-call(s32[1,256]{1,0:T(1,128)} %bitcast.5), custom_call_target="tpu_custom_call" | custom-call | flops 5242880 | bytes 786432 | tf_op jit(solution)/shard_map/stick_tables/pallas_call | solution.py:366
  11.3 5.7 %all-to-all-done.message_ref = bf16[32,8,128]{2,1,0:T(8,128)(2,1)S(1)} async-done(((bf16[32,8,128]{2,1,0:T(8,128)(2,1)}), bf16[32,8,128]{2,1,0:T(8,128)(2,1)S(1)}, u32[]{:S(2)}, u32[]{:S(2)}) %all-to-all-start) | async-done | bytes 65568 | tf_op jit(solution)/shard_map/all_to_all | solution.py:358
  17.1 2.9 %plane_density.1 = f32[2,256,256]{2,1,0:T(8,128)} custom-call(bf16[32,8,128]{2,1,0:T(8,128)(2,1)S(1)} %all-to-all-done.message_ref, bf16[2,256,256]{2,1,0:T(8,128)(2,1)S(1)} %get-tuple-element.7.left_ref, bf16[256,256]{1,0:T(8,128)(2,1)S(1)} %get-tuple-element.8.right_ref), custom_call_target="tpu_custom_call" | custom-call | tf_op jit(solution)/shard_map/plane_density/pallas_call | solution.py:386
Async XLA Ops:
  2.5 14.6 %all-to-all-start = ((bf16[32,8,128]{2,1,0:T(8,128)(2,1)}), bf16[32,8,128]{2,1,0:T(8,128)(2,1)S(1)}, u32[]{:S(2)}, u32[]{:S(2)}) async-start(bf16[32,8,128]{2,1,0:T(8,128)(2,1)} %stick_values.1), calls=%async_computation | async-start | bytes 131072 | tf_op jit(solution)/shard_map/all_to_all | solution.py:358

commit v8 on v6

--- a/solution.py
+++ b/solution.py
@@ -12,6 +12,7 @@
 PACK = 16
 P_BLOCK = 32
 BAND_GROUP = 8
+COEFF_COPIES = 4
 MIB = 1024 * 1024
 
 
@@ -80,20 +81,23 @@
     occupation_hbm,
     rotation_hbm,
     coeff_hbm,
-    out_ref,
+    out_hbm,
     length_ref,
     plane_ref,
     occupation_ref,
     rotation_ref,
     coeff_ref,
+    message_ref,
     sems,
 ):
+    piece = coeff_ref.shape[0] // COEFF_COPIES
+    pieces = [pl.ds(first * piece, piece) for first in range(COEFF_COPIES)]
     copies = [
         pltpu.make_async_copy(source, target, sems.at[index])
         for index, (source, target) in enumerate(
             (
                 (rotation_hbm, rotation_ref),
-                (coeff_hbm, coeff_ref),
+                *((coeff_hbm.at[rows], coeff_ref.at[rows]) for rows in pieces),
                 (plane_hbm, plane_ref),
                 (length_hbm, length_ref),
                 (occupation_hbm, occupation_ref),
@@ -136,7 +140,7 @@
         mixed.append(jnp.where(same, wide, 0.0).astype(jnp.bfloat16))
     rotation = jnp.concatenate(mixed, 1)
 
-    for copy in copies[2:]:
+    for copy in copies[1 + COEFF_COPIES :]:
         copy.wait()
     lengths = [length_ref[first_stick + place] for place in range(sticks)]
     planes = [plane_ref[place] for place in range(plane_count)]
@@ -156,8 +160,10 @@
     row_lengths = spread(lengths, iota((sticks, grid_len), 0), (sticks, grid_len))
     live = iota((sticks, grid_len), 1) < row_lengths
 
-    copies[1].wait()
-    rotated = dot(rotation, coeff_ref[...])
+    rotated = jnp.zeros((row_count, grid_len), jnp.float32)
+    for index, rows in enumerate(pieces):
+        copies[1 + index].wait()
+        rotated += dot(rotation[:, index * piece : (index + 1) * piece], coeff_ref[rows])
     rotated = rotated.reshape(row_count // sticks, sticks, grid_len)
     rotated = jnp.where(live[None], rotated, 0.0).reshape(row_count, grid_len)
     sums = dot_last(table, rotated.astype(jnp.bfloat16))
@@ -167,7 +173,7 @@
     turned = pltpu.roll(amplitude, row_count // 2, 1) * phase_sin
     values = amplitude * phase_cos + jnp.where(real_lane, turned, -turned)
 
-    lanes = out_ref.shape[2]
+    lanes = out_hbm.shape[2]
     spots = 2 * out_count
     tall = jnp.broadcast_to(values[:, None, :], (plane_count, sticks, row_count))
     own = iota((sticks, row_count), 0) == wrap(iota((sticks, row_count), 1), sticks)
@@ -186,9 +192,18 @@
         occupied = jnp.where(
             iota((sticks, lanes), 1) == lane, occupation_ref[own_band], occupied
         )
-    message = (message + occupied.astype(jnp.float32)[None]).astype(out_ref.dtype)
-    for band in range(out_ref.shape[0] // pw_count):
-        out_ref[band * pw_count : (band + 1) * pw_count] = message
+    message = (message + occupied.astype(jnp.float32)[None]).astype(out_hbm.dtype)
+    message_ref[...] = message
+    copies = [
+        pltpu.make_async_copy(
+            message_ref, out_hbm.at[pl.ds(band * pw_count, pw_count)], sems.at[band]
+        )
+        for band in range(out_hbm.shape[0] // pw_count)
+    ]
+    for copy in copies:
+        copy.start()
+    for copy in copies:
+        copy.wait()
 
 
 def table_kernel(grid_len, column_hbm, left_ref, right_ref, column_ref, sem):
@@ -262,52 +277,88 @@
             parts.append((sin_table * real + cos_table * imag).reshape(height, chunk))
         return dot(jnp.concatenate(parts, 0), right_ref[pl.ds(index * chunk, chunk), :])
 
-    def one_block(step, carry):
-        plane, block = step // blocks, step % blocks
-
-        def one_group(index, sums):
-            first_band = index * group
+    def group_sums(step):
+        first_band, block = step % groups * group, step // groups
+        found = []
+        for plane in range(own_planes):
             if chunks == 1:
-                found = stick_sums(0, plane, block, first_band)
+                found.append(stick_sums(0, plane, block, first_band))
             else:
-                found = lax.fori_loop(
-                    0,
-                    chunks,
-                    lambda at, so_far: so_far + stick_sums(at, plane, block, first_band),
-                    jnp.zeros((2 * group * height, grid_len), jnp.float32),
+                found.append(
+                    lax.fori_loop(
+                        0,
+                        chunks,
+                        lambda at, so_far: so_far + stick_sums(at, plane, block, first_band),
+                        jnp.zeros((2 * group * height, grid_len), jnp.float32),
+                    )
                 )
-            with_cos, with_sin, mixed = sums
+        return found
+
+    def add_squares(step, found, sums):
+        first_band = step % groups * group
+        result = []
+        for plane in range(own_planes):
+            with_cos, with_sin, mixed = sums[plane]
             for band in range(group):
                 top = 2 * band * height
-                a, d = found[top : top + height, :half], found[top : top + height, half:]
+                a = found[plane][top : top + height, :half]
+                d = found[plane][top : top + height, half:]
                 top += height
-                c, b = found[top : top + height, :half], found[top : top + height, half:]
+                c = found[plane][top : top + height, :half]
+                b = found[plane][top : top + height, half:]
                 weight = weight_ref[pl.ds(first_band + band, 1), :half]
                 with_cos += weight * (a * a + c * c)
                 with_sin += weight * (b * b + d * d)
                 mixed += weight * (c * d - a * b)
-            return with_cos, with_sin, mixed
-
-        zero = jnp.zeros((height, half), jnp.float32)
-        with_cos, with_sin, mixed = loop(bands // group, one_group, (zero, zero, zero))
+            result.append((with_cos, with_sin, mixed))
+        return result
+
+    def copy_out(plane, block):
+        where = (plane, pl.ds(block * height, height))
+        return pltpu.make_async_copy(
+            held_ref.at[where], out_ref.at[where], sem.at[plane * blocks + block]
+        )
+
+    def finish(block, sums):
         lane = iota((height, half), 1)
-        both, mixed = with_cos + with_sin, mixed + mixed
-        ahead = jnp.where(lane == 0, with_cos, both + mixed)
-        back = jnp.where(lane == 0, with_sin, both - mixed)
         row = pl.ds(block * height, height)
-        held_ref[plane, row, :half] = ahead
-        held_ref[plane, row, half:] = jnp.take_along_axis(
-            back, jnp.where(lane == 0, 0, half - lane), axis=1
-        )
-        pltpu.make_async_copy(
-            held_ref.at[plane, row], out_ref.at[plane, row], sem.at[step]
-        ).start()
-        return carry
-
-    loop(own_planes * blocks, one_block, 0)
-    for step in range(own_planes * blocks):
-        where = (step // blocks, pl.ds(step % blocks * height, height))
-        pltpu.make_async_copy(held_ref.at[where], out_ref.at[where], sem.at[step]).wait()
+        for plane, (with_cos, with_sin, mixed) in enumerate(sums):
+            both, mixed = with_cos + with_sin, mixed + mixed
+            ahead = jnp.where(lane == 0, with_cos, both + mixed)
+            back = jnp.where(lane == 0, with_sin, both - mixed)
+            held_ref[plane, row, :half] = ahead
+            held_ref[plane, row, half:] = jnp.take_along_axis(
+                back, jnp.where(lane == 0, 0, half - lane), axis=1
+            )
+            copy_out(plane, block).start()
+
+    zero = jnp.zeros((height, half), jnp.float32)
+    empty = [(zero, zero, zero)] * own_planes
+    groups = bands // group
+    if blocks * groups > 32:
+
+        def one_block(block, carry):
+            def one_group(index, sums):
+                step = block * groups + index
+                return add_squares(step, group_sums(step), sums)
+
+            finish(block, lax.fori_loop(0, groups, one_group, empty))
+            return carry
+
+        lax.fori_loop(0, blocks, one_block, 0)
+    else:
+        sums, ahead = empty, group_sums(0)
+        for step in range(blocks * groups):
+            found = ahead
+            if step + 1 < blocks * groups:
+                ahead = group_sums(step + 1)
+            sums = add_squares(step, found, sums)
+            if (step + 1) % groups == 0:
+                finish(step // groups, sums)
+                sums = empty
+    for plane in range(own_planes):
+        for block in range(blocks):
+            copy_out(plane, block).wait()
 
 
 def shards(coeffs, rotation_matrix, stick_length, stick_column, plane_index, occupation):
@@ -328,16 +379,17 @@
 
     messages = pl.pallas_call(
         stick_kernel,
-        out_shape=pltpu.VMEM((devices, sticks, lanes), jnp.bfloat16),
+        out_shape=jax.ShapeDtypeStruct((devices, sticks, lanes), jnp.bfloat16),
         in_specs=[hbm] * 5,
-        out_specs=vmem,
+        out_specs=hbm,
         scratch_shapes=[
             pltpu.SMEM(stick_length.shape, jnp.int32),
             pltpu.SMEM(plane_index.shape, jnp.int32),
             pltpu.SMEM(occupation.shape, jnp.int32),
             pltpu.VMEM((2, bands, in_count), jnp.bfloat16),
             pltpu.VMEM((2 * in_count * sticks, grid_len), jnp.bfloat16),
-            pltpu.SemaphoreType.DMA((5,)),
+            pltpu.VMEM((pw_count, sticks, lanes), jnp.bfloat16),
+            pltpu.SemaphoreType.DMA((max(4 + COEFF_COPIES, band_count),)),
         ],
         compiler_params=room(2 * message_bytes),
         name="stick_values",

time: 20.2 us -> 20.3 us (level)
  no operation moved by 1% of the time
where the time goes in v8:
time: 20.3 us; the launch traced here: 20.1 us
  starting transfers between devices  7.3 us (36%)
  Pallas kernels  6.88 us (34%)
  waiting for transfers between devices  5.85 us (29%)
    all_to_all x1, starting transfers between devices, shards(): lax.all_to_all(messages, ('band', 'pw'), split_axis=0, concat_axis=0, til...  7.3 us
    all_to_all x1, waiting for transfers between devices, shards(): lax.all_to_all(messages, ('band', 'pw'), split_axis=0, concat_axis=0, til...  5.85 us
    pallas_call x1, Pallas kernels, shards(): pl.pallas_call(functools.partial(plane_kernel, bands, own_planes, norm_fa...  2.88 us
    pallas_call x1, Pallas kernels, shards(): pl.pallas_call(stick_kernel, out_shape=jax.ShapeDtypeStruct((devices, sti...  2.58 us
    pallas_call x1, Pallas kernels, shards(): pl.pallas_call(functools.partial(table_kernel, grid_len), out_shape=(jax....  1.42 us
  transfers between devices with their start and end apart: 1, of which 1 were waited for; matrix products, arithmetic and copies ran while one was open for 0% of the time, Pallas kernels for 7%

profile of v8, /device:TPU:0, one launch (start us, length us, event | category | flops | bytes accessed | tf_op | source)
XLA Modules:
  0.0 20.1 jit_solution(11838625192182654602)
XLA Ops:
  0.0 2.6 %stick_values.1 = bf16[32,8,128]{2,1,0:T(8,128)(2,1)} custom-call(s32[256]{0:T(256)} %length_hbm.1, s32[16]{0:T(128)} %plane_hbm.1, s32[2]{0:T(128)} %occupation_hbm.1, bf16[2,8,64]{2,1,0:T(8,128)(2,1)} %bitcast.4, bf16[1024,256]{1,0:T(8,128)(2,1)} %bitcast.3), custom_call_target="tpu_custom_call" | custom-call | tf_op jit(solution)/shard_map/stick_values/pallas_call | solution.py:380
  2.6 7.3 %all-to-all-start = ((bf16[32,8,128]{2,1,0:T(8,128)(2,1)}), bf16[32,8,128]{2,1,0:T(8,128)(2,1)S(1)}, u32[]{:S(2)}, u32[]{:S(2)}) async-start(bf16[32,8,128]{2,1,0:T(8,128)(2,1)} %stick_values.1), calls=%async_computation | async-start | bytes 131072 | tf_op jit(solution)/shard_map/all_to_all | solution.py:408
  9.9 1.4 %stick_tables.1 = (bf16[2,256,256]{2,1,0:T(8,128)(2,1)S(1)}, bf16[256,256]{1,0:T(8,128)(2,1)S(1)}) custom-call(s32[1,256]{1,0:T(1,128)} %bitcast.5), custom_call_target="tpu_custom_call" | custom-call | flops 5242880 | bytes 786432 | tf_op jit(solution)/shard_map/stick_tables/pallas_call | solution.py:409
  11.3 5.8 %all-to-all-done.message_ref = bf16[32,8,128]{2,1,0:T(8,128)(2,1)S(1)} async-done(((bf16[32,8,128]{2,1,0:T(8,128)(2,1)}), bf16[32,8,128]{2,1,0:T(8,128)(2,1)S(1)}, u32[]{:S(2)}, u32[]{:S(2)}) %all-to-all-start) | async-done | bytes 65568 | tf_op jit(solution)/shard_map/all_to_all | solution.py:408
  17.2 2.9 %plane_density.1 = f32[2,256,256]{2,1,0:T(8,128)} custom-call(bf16[32,8,128]{2,1,0:T(8,128)(2,1)S(1)} %all-to-all-done.message_ref, bf16[2,256,256]{2,1,0:T(8,128)(2,1)S(1)} %get-tuple-element.7.left_ref, bf16[256,256]{1,0:T(8,128)(2,1)S(1)} %get-tuple-element.8.right_ref), custom_call_target="tpu_custom_call" | custom-call | tf_op jit(solution)/shard_map/plane_density/pallas_call | solution.py:429
Async XLA Ops:
  2.6 14.6 %all-to-all-start = ((bf16[32,8,128]{2,1,0:T(8,128)(2,1)}), bf16[32,8,128]{2,1,0:T(8,128)(2,1)S(1)}, u32[]{:S(2)}, u32[]{:S(2)}) async-start(bf16[32,8,128]{2,1,0:T(8,128)(2,1)} %stick_values.1), calls=%async_computation | async-start | bytes 131072 | tf_op jit(solution)/shard_map/all_to_all | solution.py:408

commit v9 on v8

--- a/solution.py
+++ b/solution.py
@@ -9,10 +9,10 @@
 from jax.sharding import PartitionSpec as P
 
 LANES = 128
-PACK = 16
 P_BLOCK = 32
 BAND_GROUP = 8
-COEFF_COPIES = 4
+GROUP_LANES = 256
+COEFF_COPIES = 1
 MIB = 1024 * 1024
 
 
@@ -114,86 +114,103 @@
     own_planes = plane_count // pw_count
     own_bands = occupation_ref.shape[0]
     row_count = 2 * out_count * sticks
+    lanes = message_ref.shape[2]
     band_index = lax.axis_index("band")
     first_stick = (band_index * pw_count + lax.axis_index("pw")) * sticks
 
-    pick = (
-        wrap(cut(iota((row_count, out_count), 0), sticks), out_count)
-        == iota((row_count, out_count), 1)
-    ).astype(jnp.bfloat16)
+    group_lanes = GROUP_LANES // (own_planes * 2 * out_count) * (own_planes * 2 * out_count)
+    spots = own_planes * 2 * out_count
+    group_pw = group_lanes // spots
+
+    wide = in_count * sticks
+    widen = (cut(iota((in_count, wide), 1), sticks) == iota((in_count, wide), 0)).astype(
+        jnp.bfloat16
+    )
+    same = wrap(iota((sticks, wide), 1), sticks) == iota((sticks, wide), 0)
     copies[0].wait()
-    from_real = dot(pick, rotation_ref[0])
-    from_imag = dot(pick, rotation_ref[1])
-    is_real = iota((row_count, in_count), 0) < out_count * sticks
-    widen = (
-        cut(iota((in_count, in_count * sticks), 1), sticks)
-        == iota((in_count, in_count * sticks), 0)
-    ).astype(jnp.bfloat16)
-    shape = (row_count, in_count * sticks)
-    same = wrap(iota(shape, 0), sticks) == wrap(iota(shape, 1), sticks)
-    mixed = []
-    for block in (
-        jnp.where(is_real, from_real, from_imag),
-        jnp.where(is_real, -from_imag, from_real),
-    ):
-        wide = dot(block.astype(jnp.bfloat16), widen)
-        mixed.append(jnp.where(same, wide, 0.0).astype(jnp.bfloat16))
-    rotation = jnp.concatenate(mixed, 1)
+    parts = [dot(rotation_ref[part], widen) for part in range(2)]
+    rows = {}
+    for band in range(out_count):
+        real, imag = (
+            jnp.where(same, jnp.broadcast_to(part[band : band + 1], (sticks, wide)), 0.0)
+            for part in parts
+        )
+        rows[0, band] = jnp.concatenate([real, -imag], 1)
+        rows[1, band] = jnp.concatenate([imag, real], 1)
+    rotation = jnp.concatenate([rows[key] for key in sorted(rows)], 0).astype(jnp.bfloat16)
 
     for copy in copies[1 + COEFF_COPIES :]:
         copy.wait()
     lengths = [length_ref[first_stick + place] for place in range(sticks)]
-    planes = [plane_ref[place] for place in range(plane_count)]
-    plane_rows = spread(planes, iota((plane_count, grid_len), 0), (plane_count, grid_len))
-    product = iota((plane_count, grid_len), 1) * plane_rows
-    table = jnp.concatenate([cosine(product, grid_len), sine(product, grid_len)], 0).astype(
-        jnp.bfloat16
-    )
-
-    shape = (plane_count, row_count)
-    lane_lengths = spread(lengths, wrap(iota(shape, 1), sticks), shape)
-    shift = (lane_lengths >> 1) * spread(planes, iota(shape, 0), shape)
-    phase_cos = cosine(shift, grid_len)
-    phase_sin = sine(shift, grid_len)
-    real_lane = iota(shape, 1) < row_count // 2
-
     row_lengths = spread(lengths, iota((sticks, grid_len), 0), (sticks, grid_len))
     live = iota((sticks, grid_len), 1) < row_lengths
-
+    shape = (sticks, lanes)
+    occupied = jnp.zeros(shape, jnp.int32)
+    for own_band in range(own_bands):
+        lane = spots + band_index * own_bands + own_band
+        occupied = jnp.where(iota(shape, 1) == lane, occupation_ref[own_band], occupied)
+    occupied = occupied.astype(jnp.float32)
+
+    shape = (sticks, group_lanes)
+    lane = iota(shape, 1)
+    lane_plane = lax.div(lane, 2 * out_count)
+    real_lane = lax.rem(lane, 2 * out_count) < out_count
+    lane_band = lax.rem(lane, out_count)
+    half_lengths = spread(lengths, iota(shape, 0), shape) >> 1
+
+    def forms(first_pw):
+        planes = [
+            plane_ref[first_pw * own_planes + place] for place in range(group_pw * own_planes)
+        ]
+        lane_planes = spread(planes, lane_plane, shape)
+        product = iota((grid_len, group_lanes), 0) * lane_planes[:1]
+        table = jnp.concatenate([cosine(product, grid_len), sine(product, grid_len)], 1)
+        shift = half_lengths * lane_planes
+        return table.astype(jnp.bfloat16), cosine(shift, grid_len), sine(shift, grid_len)
+
+    def pick(sums, part):
+        chosen = jnp.zeros(shape, jnp.float32)
+        for band in range(out_count):
+            top = (part * out_count + band) * sticks
+            chosen = jnp.where(lane_band == band, sums[top : top + sticks], chosen)
+        return chosen
+
+    def send(first_pw, rotated, form):
+        table, phase_cos, phase_sin = form
+        sums = dot(rotated, table)
+        with_cos, with_sin = sums[:, :group_lanes], sums[:, group_lanes:]
+        real = pick(with_cos, 0) - pick(with_sin, 1)
+        imag = pick(with_sin, 0) + pick(with_cos, 1)
+        values = jnp.where(
+            real_lane, real * phase_cos + imag * phase_sin, imag * phase_cos - real * phase_sin
+        )
+        for place in range(group_pw):
+            first = place * spots
+            tile = first // lanes * lanes
+            piece = values[:, tile : tile + lanes]
+            if first > tile:
+                piece = pltpu.roll(piece, lanes - (first - tile), 1)
+            piece = jnp.where(iota((sticks, lanes), 1) < spots, piece, occupied)
+            message_ref[first_pw + place] = piece.astype(message_ref.dtype)
+
+    if group_pw == pw_count:
+        form = forms(0)
     rotated = jnp.zeros((row_count, grid_len), jnp.float32)
-    for index, rows in enumerate(pieces):
+    for index, where in enumerate(pieces):
         copies[1 + index].wait()
-        rotated += dot(rotation[:, index * piece : (index + 1) * piece], coeff_ref[rows])
+        rotated += dot(rotation[:, index * piece : (index + 1) * piece], coeff_ref[where])
     rotated = rotated.reshape(row_count // sticks, sticks, grid_len)
     rotated = jnp.where(live[None], rotated, 0.0).reshape(row_count, grid_len)
-    sums = dot_last(table, rotated.astype(jnp.bfloat16))
-    with_cos, with_sin = sums[:plane_count], sums[plane_count:]
-    turned = pltpu.roll(with_sin, row_count // 2, 1)
-    amplitude = with_cos + jnp.where(real_lane, -turned, turned)
-    turned = pltpu.roll(amplitude, row_count // 2, 1) * phase_sin
-    values = amplitude * phase_cos + jnp.where(real_lane, turned, -turned)
-
-    lanes = out_hbm.shape[2]
-    spots = 2 * out_count
-    tall = jnp.broadcast_to(values[:, None, :], (plane_count, sticks, row_count))
-    own = iota((sticks, row_count), 0) == wrap(iota((sticks, row_count), 1), sticks)
-    tall = jnp.where(own[None], tall, 0.0).reshape(plane_count * sticks, row_count)
-    shape = (row_count, lanes)
-    place = (
-        (cut(iota(shape, 0), sticks) == lax.rem(iota(shape, 1), spots))
-        & (iota(shape, 1) < own_planes * spots)
-    ).astype(jnp.bfloat16)
-    laid = dot(tall.astype(jnp.bfloat16), place).reshape(pw_count, own_planes, sticks, lanes)
-    mine = cut(iota((own_planes, sticks, lanes), 2), spots) == iota((own_planes, sticks, lanes), 0)
-    message = jnp.sum(jnp.where(mine[None], laid, 0.0), 1)
-    occupied = jnp.zeros((sticks, lanes), jnp.int32)
-    for own_band in range(own_bands):
-        lane = own_planes * spots + band_index * own_bands + own_band
-        occupied = jnp.where(
-            iota((sticks, lanes), 1) == lane, occupation_ref[own_band], occupied
-        )
-    message = (message + occupied.astype(jnp.float32)[None]).astype(out_hbm.dtype)
-    message_ref[...] = message
+    rotated = rotated.astype(jnp.bfloat16)
+    if group_pw == pw_count:
+        send(0, rotated, form)
+    else:
+
+        def one_group(index, carry):
+            send(index * group_pw, rotated, forms(index * group_pw))
+            return carry
+
+        lax.fori_loop(0, pw_count // group_pw, one_group, 0)
     copies = [
         pltpu.make_async_copy(
             message_ref, out_hbm.at[pl.ds(band * pw_count, pw_count)], sems.at[band]
@@ -214,8 +231,8 @@
     half = grid_len // 2
     columns = column_ref[...]
     turns = iota((grid_len, count), 0) * cut(columns, grid_len)
-    left_ref[0] = cosine(turns, grid_len).astype(jnp.bfloat16)
-    left_ref[1] = sine(turns, grid_len).astype(jnp.bfloat16)
+    left_ref[0] = cosine(turns, grid_len).astype(jnp.bfloat16).astype(jnp.float32)
+    left_ref[1] = sine(turns, grid_len).astype(jnp.bfloat16).astype(jnp.float32)
     tall = jnp.transpose(jnp.broadcast_to(wrap(columns, grid_len), (half, count)))
     freq = iota((count, half), 1)
     right_ref[:, :half] = cosine(tall * freq, grid_len).astype(jnp.bfloat16)
@@ -232,7 +249,6 @@
     right_ref,
     out_ref,
     value_ref,
-    weight_ref,
     held_ref,
     sem,
 ):
@@ -257,24 +273,21 @@
         return jnp.maximum(peak, jnp.max(picked[rows:], 1, keepdims=True))
 
     peak = loop(chunks, turn, jnp.zeros((bands, 1), jnp.float32))
-    weight_ref[...] = jnp.broadcast_to(peak * norm_factor, weight_ref.shape)
+    scale = jnp.sqrt(peak * norm_factor)[None]
+    for first in range(0, rows, bands):
+        value_ref[:, first : first + bands] = value_ref[:, first : first + bands] * scale
 
     def stick_sums(index, plane, block, first_band):
         lane = pl.ds(index * chunk, chunk)
         row = pl.ds(block * height, height)
-        cos_table = left_ref[0, row, lane].reshape(height // PACK, PACK, chunk)
-        sin_table = left_ref[1, row, lane].reshape(height // PACK, PACK, chunk)
+        cos_table, sin_table = left_ref[0, row, lane], left_ref[1, row, lane]
         parts = []
         for band in range(group):
             at = plane * spots + first_band + band
-            real, imag = (
-                jnp.broadcast_to(value_ref[index, pl.ds(spot, 1), :], (PACK, chunk)).astype(
-                    jnp.bfloat16
-                )[None]
-                for spot in (at, at + bands)
-            )
-            parts.append((cos_table * real - sin_table * imag).reshape(height, chunk))
-            parts.append((sin_table * real + cos_table * imag).reshape(height, chunk))
+            real = value_ref[index, pl.ds(at, 1), :]
+            imag = value_ref[index, pl.ds(at + bands, 1), :]
+            parts.append((cos_table * real - sin_table * imag).astype(jnp.bfloat16))
+            parts.append((sin_table * real + cos_table * imag).astype(jnp.bfloat16))
         return dot(jnp.concatenate(parts, 0), right_ref[pl.ds(index * chunk, chunk), :])
 
     def group_sums(step):
@@ -294,8 +307,7 @@
                 )
         return found
 
-    def add_squares(step, found, sums):
-        first_band = step % groups * group
+    def add_squares(found, sums):
         result = []
         for plane in range(own_planes):
             with_cos, with_sin, mixed = sums[plane]
@@ -306,10 +318,9 @@
                 top += height
                 c = found[plane][top : top + height, :half]
                 b = found[plane][top : top + height, half:]
-                weight = weight_ref[pl.ds(first_band + band, 1), :half]
-                with_cos += weight * (a * a + c * c)
-                with_sin += weight * (b * b + d * d)
-                mixed += weight * (c * d - a * b)
+                with_cos += a * a + c * c
+                with_sin += b * b + d * d
+                mixed += c * d - a * b
             result.append((with_cos, with_sin, mixed))
         return result
 
@@ -340,7 +351,7 @@
         def one_block(block, carry):
             def one_group(index, sums):
                 step = block * groups + index
-                return add_squares(step, group_sums(step), sums)
+                return add_squares(group_sums(step), sums)
 
             finish(block, lax.fori_loop(0, groups, one_group, empty))
             return carry
@@ -352,7 +363,7 @@
             found = ahead
             if step + 1 < blocks * groups:
                 ahead = group_sums(step + 1)
-            sums = add_squares(step, found, sums)
+            sums = add_squares(found, sums)
             if (step + 1) % groups == 0:
                 finish(step // groups, sums)
                 sums = empty
@@ -374,7 +385,7 @@
     lanes = -(-(rows + bands) // LANES) * LANES
     vmem = pl.BlockSpec(memory_space=pltpu.VMEM)
     hbm = pl.BlockSpec(memory_space=pltpu.HBM)
-    table_bytes = 6 * grid_len * stick_count
+    table_bytes = 10 * grid_len * stick_count
     message_bytes = 2 * stick_count * lanes
 
     messages = pl.pallas_call(
@@ -409,7 +420,7 @@
     left, right = pl.pallas_call(
         functools.partial(table_kernel, grid_len),
         out_shape=(
-            jax.ShapeDtypeStruct((2, grid_len, stick_count), jnp.bfloat16),
+            jax.ShapeDtypeStruct((2, grid_len, stick_count), jnp.float32),
             jax.ShapeDtypeStruct((stick_count, grid_len), jnp.bfloat16),
         ),
         in_specs=[hbm],
@@ -433,7 +444,6 @@
         out_specs=hbm,
         scratch_shapes=[
             pltpu.VMEM((stick_count // chunk, rows, chunk), jnp.float32),
-            pltpu.VMEM((bands, LANES), jnp.float32),
             pltpu.VMEM((own_planes, grid_len, grid_len), jnp.float32),
             pltpu.SemaphoreType.DMA((blocks,)),
         ],

time: 20.3 us -> 20.8 us (1.025)
  Pallas kernels: 6.88 us -> 7.4 us
    pallas_call x1, Pallas kernels: 2.88 us -> 3.41 us  [shards(): pl.pallas_call(functools.partial(plane_kernel, bands, own_planes, norm_fa...]
where the time goes in v9:
time: 20.8 us; the launch traced here: 20.5 us
  Pallas kernels  7.4 us (36%)
  starting transfers between devices  7.3 us (35%)
  waiting for transfers between devices  5.82 us (28%)
    all_to_all x1, starting transfers between devices, shards(): lax.all_to_all(messages, ('band', 'pw'), split_axis=0, concat_axis=0, til...  7.3 us
    all_to_all x1, waiting for transfers between devices, shards(): lax.all_to_all(messages, ('band', 'pw'), split_axis=0, concat_axis=0, til...  5.82 us
    pallas_call x1, Pallas kernels, shards(): pl.pallas_call(functools.partial(plane_kernel, bands, own_planes, norm_fa...  3.41 us
    pallas_call x1, Pallas kernels, shards(): pl.pallas_call(stick_kernel, out_shape=jax.ShapeDtypeStruct((devices, sti...  2.54 us
    pallas_call x1, Pallas kernels, shards(): pl.pallas_call(functools.partial(table_kernel, grid_len), out_shape=(jax....  1.45 us
  transfers between devices with their start and end apart: 1, of which 1 were waited for; matrix products, arithmetic and copies ran while one was open for 0% of the time, Pallas kernels for 7%

profile of v9, /device:TPU:0, one launch (start us, length us, event | category | flops | bytes accessed | tf_op | source)
XLA Modules:
  0.0 20.5 jit_solution(18380817181601646843)
XLA Ops:
  0.0 2.5 %stick_values.1 = bf16[32,8,128]{2,1,0:T(8,128)(2,1)} custom-call(s32[256]{0:T(256)} %length_hbm.1, s32[16]{0:T(128)} %plane_hbm.1, s32[2]{0:T(128)} %occupation_hbm.1, bf16[2,8,64]{2,1,0:T(8,128)(2,1)} %bitcast.4, bf16[1024,256]{1,0:T(8,128)(2,1)} %bitcast.3), custom_call_target="tpu_custom_call" | custom-call | tf_op jit(solution)/shard_map/stick_values/pallas_call | solution.py:391
  2.6 7.3 %all-to-all-start = ((bf16[32,8,128]{2,1,0:T(8,128)(2,1)}), bf16[32,8,128]{2,1,0:T(8,128)(2,1)S(1)}, u32[]{:S(2)}, u32[]{:S(2)}) async-start(bf16[32,8,128]{2,1,0:T(8,128)(2,1)} %stick_values.1), calls=%async_computation | async-start | bytes 131072 | tf_op jit(solution)/shard_map/all_to_all | solution.py:419
  9.9 1.5 %stick_tables.1 = (f32[2,256,256]{2,1,0:T(8,128)S(1)}, bf16[256,256]{1,0:T(8,128)(2,1)S(1)}) custom-call(s32[1,256]{1,0:T(1,128)} %bitcast.5), custom_call_target="tpu_custom_call" | custom-call | flops 5242880 | bytes 786432 | tf_op jit(solution)/shard_map/stick_tables/pallas_call | solution.py:420
  11.3 5.8 %all-to-all-done.message_ref = bf16[32,8,128]{2,1,0:T(8,128)(2,1)S(1)} async-done(((bf16[32,8,128]{2,1,0:T(8,128)(2,1)}), bf16[32,8,128]{2,1,0:T(8,128)(2,1)S(1)}, u32[]{:S(2)}, u32[]{:S(2)}) %all-to-all-start) | async-done | bytes 65568 | tf_op jit(solution)/shard_map/all_to_all | solution.py:419
  17.1 3.4 %plane_density.1 = f32[2,256,256]{2,1,0:T(8,128)} custom-call(bf16[32,8,128]{2,1,0:T(8,128)(2,1)S(1)} %all-to-all-done.message_ref, f32[2,256,256]{2,1,0:T(8,128)S(1)} %get-tuple-element.7.left_ref, bf16[256,256]{1,0:T(8,128)(2,1)S(1)} %get-tuple-element.8.right_ref), custom_call_target="tpu_custom_call" | custom-call | tf_op jit(solution)/shard_map/plane_density/pallas_call | solution.py:440
Async XLA Ops:
  2.6 14.6 %all-to-all-start = ((bf16[32,8,128]{2,1,0:T(8,128)(2,1)}), bf16[32,8,128]{2,1,0:T(8,128)(2,1)S(1)}, u32[]{:S(2)}, u32[]{:S(2)}) async-start(bf16[32,8,128]{2,1,0:T(8,128)(2,1)} %stick_values.1), calls=%async_computation | async-start | bytes 131072 | tf_op jit(solution)/shard_map/all_to_all | solution.py:419

commit v10 on v9

--- a/solution.py
+++ b/solution.py
@@ -9,7 +9,8 @@
 from jax.sharding import PartitionSpec as P
 
 LANES = 128
-P_BLOCK = 32
+PACK = 16
+P_BLOCK = 64
 BAND_GROUP = 8
 GROUP_LANES = 256
 COEFF_COPIES = 1
@@ -159,12 +160,23 @@
     half_lengths = spread(lengths, iota(shape, 0), shape) >> 1
 
     def forms(first_pw):
-        planes = [
-            plane_ref[first_pw * own_planes + place] for place in range(group_pw * own_planes)
-        ]
+        kinds = group_pw * own_planes
+        planes = [plane_ref[first_pw * own_planes + place] for place in range(kinds)]
+        kind = iota((2 * kinds, grid_len), 0)
+        planes_down = spread(planes, lax.rem(kind, kinds), kind.shape)
+        quarter = jnp.where(kind < kinds, 0, grid_len - grid_len // 4)
+        waves = cosine(iota(kind.shape, 1) * planes_down + quarter, grid_len)
+        place = iota((2 * kinds, 2 * group_lanes), 1)
+        wanted = lax.div(lax.rem(place, group_lanes), 2 * out_count)
+        wanted = jnp.where(place < group_lanes, wanted, wanted + kinds)
+        widen = (iota(place.shape, 0) == wanted).astype(jnp.bfloat16)
+        table = lax.dot_general(
+            waves.astype(jnp.bfloat16),
+            widen,
+            (((0,), (0,)), ((), ())),
+            preferred_element_type=jnp.float32,
+        )
         lane_planes = spread(planes, lane_plane, shape)
-        product = iota((grid_len, group_lanes), 0) * lane_planes[:1]
-        table = jnp.concatenate([cosine(product, grid_len), sine(product, grid_len)], 1)
         shift = half_lengths * lane_planes
         return table.astype(jnp.bfloat16), cosine(shift, grid_len), sine(shift, grid_len)
 
@@ -231,8 +243,8 @@
     half = grid_len // 2
     columns = column_ref[...]
     turns = iota((grid_len, count), 0) * cut(columns, grid_len)
-    left_ref[0] = cosine(turns, grid_len).astype(jnp.bfloat16).astype(jnp.float32)
-    left_ref[1] = sine(turns, grid_len).astype(jnp.bfloat16).astype(jnp.float32)
+    left_ref[0] = cosine(turns, grid_len).astype(jnp.bfloat16)
+    left_ref[1] = sine(turns, grid_len).astype(jnp.bfloat16)
     tall = jnp.transpose(jnp.broadcast_to(wrap(columns, grid_len), (half, count)))
     freq = iota((count, half), 1)
     right_ref[:, :half] = cosine(tall * freq, grid_len).astype(jnp.bfloat16)
@@ -249,6 +261,7 @@
     right_ref,
     out_ref,
     value_ref,
+    weight_ref,
     held_ref,
     sem,
 ):
@@ -273,21 +286,24 @@
         return jnp.maximum(peak, jnp.max(picked[rows:], 1, keepdims=True))
 
     peak = loop(chunks, turn, jnp.zeros((bands, 1), jnp.float32))
-    scale = jnp.sqrt(peak * norm_factor)[None]
-    for first in range(0, rows, bands):
-        value_ref[:, first : first + bands] = value_ref[:, first : first + bands] * scale
+    weight_ref[...] = jnp.broadcast_to(peak * norm_factor, weight_ref.shape)
 
     def stick_sums(index, plane, block, first_band):
         lane = pl.ds(index * chunk, chunk)
         row = pl.ds(block * height, height)
-        cos_table, sin_table = left_ref[0, row, lane], left_ref[1, row, lane]
+        cos_table = left_ref[0, row, lane].reshape(height // PACK, PACK, chunk)
+        sin_table = left_ref[1, row, lane].reshape(height // PACK, PACK, chunk)
         parts = []
         for band in range(group):
             at = plane * spots + first_band + band
-            real = value_ref[index, pl.ds(at, 1), :]
-            imag = value_ref[index, pl.ds(at + bands, 1), :]
-            parts.append((cos_table * real - sin_table * imag).astype(jnp.bfloat16))
-            parts.append((sin_table * real + cos_table * imag).astype(jnp.bfloat16))
+            real, imag = (
+                jnp.broadcast_to(value_ref[index, pl.ds(spot, 1), :], (PACK, chunk)).astype(
+                    jnp.bfloat16
+                )[None]
+                for spot in (at, at + bands)
+            )
+            parts.append((cos_table * real - sin_table * imag).reshape(height, chunk))
+            parts.append((sin_table * real + cos_table * imag).reshape(height, chunk))
         return dot(jnp.concatenate(parts, 0), right_ref[pl.ds(index * chunk, chunk), :])
 
     def group_sums(step):
@@ -307,7 +323,8 @@
                 )
         return found
 
-    def add_squares(found, sums):
+    def add_squares(step, found, sums):
+        first_band = step % groups * group
         result = []
         for plane in range(own_planes):
             with_cos, with_sin, mixed = sums[plane]
@@ -318,9 +335,10 @@
                 top += height
                 c = found[plane][top : top + height, :half]
                 b = found[plane][top : top + height, half:]
-                with_cos += a * a + c * c
-                with_sin += b * b + d * d
-                mixed += c * d - a * b
+                weight = weight_ref[pl.ds(first_band + band, 1), :half]
+                with_cos += weight * (a * a + c * c)
+                with_sin += weight * (b * b + d * d)
+                mixed += weight * (c * d - a * b)
             result.append((with_cos, with_sin, mixed))
         return result
 
@@ -346,27 +364,16 @@
     zero = jnp.zeros((height, half), jnp.float32)
     empty = [(zero, zero, zero)] * own_planes
     groups = bands // group
-    if blocks * groups > 32:
-
-        def one_block(block, carry):
-            def one_group(index, sums):
-                step = block * groups + index
-                return add_squares(group_sums(step), sums)
-
-            finish(block, lax.fori_loop(0, groups, one_group, empty))
-            return carry
-
-        lax.fori_loop(0, blocks, one_block, 0)
-    else:
-        sums, ahead = empty, group_sums(0)
-        for step in range(blocks * groups):
-            found = ahead
-            if step + 1 < blocks * groups:
-                ahead = group_sums(step + 1)
-            sums = add_squares(found, sums)
-            if (step + 1) % groups == 0:
-                finish(step // groups, sums)
-                sums = empty
+
+    def one_block(block, carry):
+        def one_group(index, sums):
+            step = block * groups + index
+            return add_squares(step, group_sums(step), sums)
+
+        finish(block, loop(groups, one_group, empty))
+        return carry
+
+    lax.fori_loop(0, blocks, one_block, 0)
     for plane in range(own_planes):
         for block in range(blocks):
             copy_out(plane, block).wait()
@@ -385,7 +392,7 @@
     lanes = -(-(rows + bands) // LANES) * LANES
     vmem = pl.BlockSpec(memory_space=pltpu.VMEM)
     hbm = pl.BlockSpec(memory_space=pltpu.HBM)
-    table_bytes = 10 * grid_len * stick_count
+    table_bytes = 6 * grid_len * stick_count
     message_bytes = 2 * stick_count * lanes
 
     messages = pl.pallas_call(
@@ -420,7 +427,7 @@
     left, right = pl.pallas_call(
         functools.partial(table_kernel, grid_len),
         out_shape=(
-            jax.ShapeDtypeStruct((2, grid_len, stick_count), jnp.float32),
+            jax.ShapeDtypeStruct((2, grid_len, stick_count), jnp.bfloat16),
             jax.ShapeDtypeStruct((stick_count, grid_len), jnp.bfloat16),
         ),
         in_specs=[hbm],
@@ -444,6 +451,7 @@
         out_specs=hbm,
         scratch_shapes=[
             pltpu.VMEM((stick_count // chunk, rows, chunk), jnp.float32),
+            pltpu.VMEM((bands, LANES), jnp.float32),
             pltpu.VMEM((own_planes, grid_len, grid_len), jnp.float32),
             pltpu.SemaphoreType.DMA((blocks,)),
         ],

time: 20.8 us -> 20.7 us (level)
  no operation moved by 1% of the time
where the time goes in v10:
time: 20.7 us; the launch traced here: 20.5 us
  Pallas kernels  7.34 us (35%)
  starting transfers between devices  7.3 us (35%)
  waiting for transfers between devices  5.85 us (28%)
    all_to_all x1, starting transfers between devices, shards(): lax.all_to_all(messages, ('band', 'pw'), split_axis=0, concat_axis=0, til...  7.3 us
    all_to_all x1, waiting for transfers between devices, shards(): lax.all_to_all(messages, ('band', 'pw'), split_axis=0, concat_axis=0, til...  5.85 us
    pallas_call x1, Pallas kernels, shards(): pl.pallas_call(functools.partial(plane_kernel, bands, own_planes, norm_fa...  3.55 us
    pallas_call x1, Pallas kernels, shards(): pl.pallas_call(stick_kernel, out_shape=jax.ShapeDtypeStruct((devices, sti...  2.37 us
    pallas_call x1, Pallas kernels, shards(): pl.pallas_call(functools.partial(table_kernel, grid_len), out_shape=(jax....  1.42 us
  transfers between devices with their start and end apart: 1, of which 1 were waited for; matrix products, arithmetic and copies ran while one was open for 0% of the time, Pallas kernels for 7%

profile of v10, /device:TPU:0, one launch (start us, length us, event | category | flops | bytes accessed | tf_op | source)
XLA Modules:
  0.0 20.5 jit_solution(13709304538550415388)
XLA Ops:
  0.0 2.4 %stick_values.1 = bf16[32,8,128]{2,1,0:T(8,128)(2,1)} custom-call(s32[256]{0:T(256)} %length_hbm.1, s32[16]{0:T(128)} %plane_hbm.1, s32[2]{0:T(128)} %occupation_hbm.1, bf16[2,8,64]{2,1,0:T(8,128)(2,1)} %bitcast.4, bf16[1024,256]{1,0:T(8,128)(2,1)} %bitcast.3), custom_call_target="tpu_custom_call" | custom-call | tf_op jit(solution)/shard_map/stick_values/pallas_call | solution.py:398
  2.4 7.3 %all-to-all-start = ((bf16[32,8,128]{2,1,0:T(8,128)(2,1)}), bf16[32,8,128]{2,1,0:T(8,128)(2,1)S(1)}, u32[]{:S(2)}, u32[]{:S(2)}) async-start(bf16[32,8,128]{2,1,0:T(8,128)(2,1)} %stick_values.1), calls=%async_computation | async-start | bytes 131072 | tf_op jit(solution)/shard_map/all_to_all | solution.py:426
  9.7 1.4 %stick_tables.1 = (bf16[2,256,256]{2,1,0:T(8,128)(2,1)S(1)}, bf16[256,256]{1,0:T(8,128)(2,1)S(1)}) custom-call(s32[1,256]{1,0:T(1,128)} %bitcast.5), custom_call_target="tpu_custom_call" | custom-call | flops 5242880 | bytes 786432 | tf_op jit(solution)/shard_map/stick_tables/pallas_call | solution.py:427
  11.1 5.8 %all-to-all-done.message_ref = bf16[32,8,128]{2,1,0:T(8,128)(2,1)S(1)} async-done(((bf16[32,8,128]{2,1,0:T(8,128)(2,1)}), bf16[32,8,128]{2,1,0:T(8,128)(2,1)S(1)}, u32[]{:S(2)}, u32[]{:S(2)}) %all-to-all-start) | async-done | bytes 65568 | tf_op jit(solution)/shard_map/all_to_all | solution.py:426
  17.0 3.5 %plane_density.1 = f32[2,256,256]{2,1,0:T(8,128)} custom-call(bf16[32,8,128]{2,1,0:T(8,128)(2,1)S(1)} %all-to-all-done.message_ref, bf16[2,256,256]{2,1,0:T(8,128)(2,1)S(1)} %get-tuple-element.7.left_ref, bf16[256,256]{1,0:T(8,128)(2,1)S(1)} %get-tuple-element.8.right_ref), custom_call_target="tpu_custom_call" | custom-call | tf_op jit(solution)/shard_map/plane_density/pallas_call | solution.py:447
Async XLA Ops:
  2.4 14.6 %all-to-all-start = ((bf16[32,8,128]{2,1,0:T(8,128)(2,1)}), bf16[32,8,128]{2,1,0:T(8,128)(2,1)S(1)}, u32[]{:S(2)}, u32[]{:S(2)}) async-start(bf16[32,8,128]{2,1,0:T(8,128)(2,1)} %stick_values.1), calls=%async_computation | async-start | bytes 131072 | tf_op jit(solution)/shard_map/all_to_all | solution.py:426

commit v11 on v10

--- a/solution.py
+++ b/solution.py
@@ -10,7 +10,7 @@
 
 LANES = 128
 PACK = 16
-P_BLOCK = 64
+P_BLOCK = 32
 BAND_GROUP = 8
 GROUP_LANES = 256
 COEFF_COPIES = 1
@@ -242,14 +242,20 @@
     count = column_ref.shape[1]
     half = grid_len // 2
     columns = column_ref[...]
-    turns = iota((grid_len, count), 0) * cut(columns, grid_len)
+    turns = iota((half, count), 0) * cut(columns, grid_len)
     left_ref[0] = cosine(turns, grid_len).astype(jnp.bfloat16)
     left_ref[1] = sine(turns, grid_len).astype(jnp.bfloat16)
-    tall = jnp.transpose(jnp.broadcast_to(wrap(columns, grid_len), (half, count)))
+    tall = jnp.transpose(jnp.broadcast_to(columns, (half, count)))
+    sign = (1 - 2 * (cut(tall, grid_len) & 1)).astype(jnp.float32)
+    tall = wrap(tall, grid_len)
     freq = iota((count, half), 1)
-    right_ref[:, :half] = cosine(tall * freq, grid_len).astype(jnp.bfloat16)
+    values = cosine(tall * freq, grid_len)
+    right_ref[:, :half] = values.astype(jnp.bfloat16)
+    right_ref[:, grid_len : grid_len + half] = (sign * values).astype(jnp.bfloat16)
     turns = jnp.where(freq == 0, tall * half, tall * freq + (grid_len - grid_len // 4))
-    right_ref[:, half:] = cosine(turns, grid_len).astype(jnp.bfloat16)
+    values = cosine(turns, grid_len)
+    right_ref[:, half:grid_len] = values.astype(jnp.bfloat16)
+    right_ref[:, grid_len + half :] = (sign * values).astype(jnp.bfloat16)
 
 
 def plane_kernel(
@@ -265,13 +271,15 @@
     held_ref,
     sem,
 ):
-    chunks, rows, chunk = value_ref.shape
+    rows, _, count = value_ref.shape
+    chunk = min(out_ref.shape[1], count)
+    chunks = count // chunk
     grid_len = out_ref.shape[1]
     half = grid_len // 2
     sticks, lanes = message_ref.shape[1:]
     spots = 2 * bands
-    height = math.gcd(grid_len, P_BLOCK)
-    blocks = grid_len // height
+    height = math.gcd(half, P_BLOCK)
+    blocks = half // height
     group = math.gcd(bands, BAND_GROUP)
     select = (iota((rows + bands, lanes), 0) == iota((rows + bands, lanes), 1)).astype(
         jnp.bfloat16
@@ -282,7 +290,10 @@
         picked = dot_last(
             select, message_ref[pl.ds(index * pieces, pieces)].reshape(chunk, lanes)
         )
-        value_ref[index] = picked[:rows]
+        for row in range(rows):
+            value_ref[row, :, pl.ds(index * chunk, chunk)] = jnp.broadcast_to(
+                picked[row : row + 1], (PACK, chunk)
+            ).astype(jnp.bfloat16)
         return jnp.maximum(peak, jnp.max(picked[rows:], 1, keepdims=True))
 
     peak = loop(chunks, turn, jnp.zeros((bands, 1), jnp.float32))
@@ -296,12 +307,7 @@
         parts = []
         for band in range(group):
             at = plane * spots + first_band + band
-            real, imag = (
-                jnp.broadcast_to(value_ref[index, pl.ds(spot, 1), :], (PACK, chunk)).astype(
-                    jnp.bfloat16
-                )[None]
-                for spot in (at, at + bands)
-            )
+            real, imag = value_ref[at, :, lane][None], value_ref[at + bands, :, lane][None]
             parts.append((cos_table * real - sin_table * imag).reshape(height, chunk))
             parts.append((sin_table * real + cos_table * imag).reshape(height, chunk))
         return dot(jnp.concatenate(parts, 0), right_ref[pl.ds(index * chunk, chunk), :])
@@ -318,7 +324,7 @@
                         0,
                         chunks,
                         lambda at, so_far: so_far + stick_sums(at, plane, block, first_band),
-                        jnp.zeros((2 * group * height, grid_len), jnp.float32),
+                        jnp.zeros((2 * group * height, 2 * grid_len), jnp.float32),
                     )
                 )
         return found
@@ -326,15 +332,15 @@
     def add_squares(step, found, sums):
         first_band = step % groups * group
         result = []
-        for plane in range(own_planes):
-            with_cos, with_sin, mixed = sums[plane]
+        for place, (with_cos, with_sin, mixed) in enumerate(sums):
+            plane, left = place // 2, place % 2 * grid_len
             for band in range(group):
                 top = 2 * band * height
-                a = found[plane][top : top + height, :half]
-                d = found[plane][top : top + height, half:]
+                a = found[plane][top : top + height, left : left + half]
+                d = found[plane][top : top + height, left + half : left + grid_len]
                 top += height
-                c = found[plane][top : top + height, :half]
-                b = found[plane][top : top + height, half:]
+                c = found[plane][top : top + height, left : left + half]
+                b = found[plane][top : top + height, left + half : left + grid_len]
                 weight = weight_ref[pl.ds(first_band + band, 1), :half]
                 with_cos += weight * (a * a + c * c)
                 with_sin += weight * (b * b + d * d)
@@ -342,41 +348,52 @@
             result.append((with_cos, with_sin, mixed))
         return result
 
-    def copy_out(plane, block):
-        where = (plane, pl.ds(block * height, height))
+    def copy_out(place, block):
+        where = (place // 2, pl.ds(place % 2 * half + block * height, height))
         return pltpu.make_async_copy(
-            held_ref.at[where], out_ref.at[where], sem.at[plane * blocks + block]
+            held_ref.at[where], out_ref.at[where], sem.at[place * blocks + block]
         )
 
     def finish(block, sums):
         lane = iota((height, half), 1)
-        row = pl.ds(block * height, height)
-        for plane, (with_cos, with_sin, mixed) in enumerate(sums):
+        for place, (with_cos, with_sin, mixed) in enumerate(sums):
             both, mixed = with_cos + with_sin, mixed + mixed
             ahead = jnp.where(lane == 0, with_cos, both + mixed)
             back = jnp.where(lane == 0, with_sin, both - mixed)
-            held_ref[plane, row, :half] = ahead
-            held_ref[plane, row, half:] = jnp.take_along_axis(
+            row = pl.ds(place % 2 * half + block * height, height)
+            held_ref[place // 2, row, :half] = ahead
+            held_ref[place // 2, row, half:] = jnp.take_along_axis(
                 back, jnp.where(lane == 0, 0, half - lane), axis=1
             )
-            copy_out(plane, block).start()
+            copy_out(place, block).start()
 
     zero = jnp.zeros((height, half), jnp.float32)
-    empty = [(zero, zero, zero)] * own_planes
+    empty = [(zero, zero, zero)] * (2 * own_planes)
     groups = bands // group
-
-    def one_block(block, carry):
-        def one_group(index, sums):
-            step = block * groups + index
-            return add_squares(step, group_sums(step), sums)
-
-        finish(block, loop(groups, one_group, empty))
-        return carry
-
-    lax.fori_loop(0, blocks, one_block, 0)
-    for plane in range(own_planes):
+    if blocks * groups > 32:
+
+        def one_block(block, carry):
+            def one_group(index, sums):
+                step = block * groups + index
+                return add_squares(step, group_sums(step), sums)
+
+            finish(block, lax.fori_loop(0, groups, one_group, empty))
+            return carry
+
+        lax.fori_loop(0, blocks, one_block, 0)
+    else:
+        sums, ahead = empty, group_sums(0)
+        for step in range(blocks * groups):
+            found = ahead
+            if step + 1 < blocks * groups:
+                ahead = group_sums(step + 1)
+            sums = add_squares(step, found, sums)
+            if (step + 1) % groups == 0:
+                finish(step // groups, sums)
+                sums = empty
+    for place in range(2 * own_planes):
         for block in range(blocks):
-            copy_out(plane, block).wait()
+            copy_out(place, block).wait()
 
 
 def shards(coeffs, rotation_matrix, stick_length, stick_column, plane_index, occupation):
@@ -392,7 +409,7 @@
     lanes = -(-(rows + bands) // LANES) * LANES
     vmem = pl.BlockSpec(memory_space=pltpu.VMEM)
     hbm = pl.BlockSpec(memory_space=pltpu.HBM)
-    table_bytes = 6 * grid_len * stick_count
+    table_bytes = 8 * grid_len * stick_count
     message_bytes = 2 * stick_count * lanes
 
     messages = pl.pallas_call(
@@ -427,8 +444,8 @@
     left, right = pl.pallas_call(
         functools.partial(table_kernel, grid_len),
         out_shape=(
-            jax.ShapeDtypeStruct((2, grid_len, stick_count), jnp.bfloat16),
-            jax.ShapeDtypeStruct((stick_count, grid_len), jnp.bfloat16),
+            jax.ShapeDtypeStruct((2, grid_len // 2, stick_count), jnp.bfloat16),
+            jax.ShapeDtypeStruct((stick_count, 2 * grid_len), jnp.bfloat16),
         ),
         in_specs=[hbm],
         out_specs=(vmem, vmem),
@@ -441,16 +458,15 @@
         ),
         name="stick_tables",
     )(pltpu.with_memory_space_constraint(stick_column.reshape(1, stick_count), pltpu.HBM))
-    chunk = min(grid_len, stick_count)
     norm_factor = 1.0 / float(bands * stick_count * grid_len)
-    blocks = own_planes * (grid_len // math.gcd(grid_len, P_BLOCK))
+    blocks = 2 * own_planes * (grid_len // 2 // math.gcd(grid_len // 2, P_BLOCK))
     return pl.pallas_call(
         functools.partial(plane_kernel, bands, own_planes, norm_factor),
         out_shape=jax.ShapeDtypeStruct((own_planes, grid_len, grid_len), jnp.float32),
         in_specs=[vmem] * 3,
         out_specs=hbm,
         scratch_shapes=[
-            pltpu.VMEM((stick_count // chunk, rows, chunk), jnp.float32),
+            pltpu.VMEM((rows, PACK, stick_count), jnp.bfloat16),
             pltpu.VMEM((bands, LANES), jnp.float32),
             pltpu.VMEM((own_planes, grid_len, grid_len), jnp.float32),
             pltpu.SemaphoreType.DMA((blocks,)),

time: 20.7 us -> 19.8 us (0.957)
  Pallas kernels: 7.34 us -> 6.16 us
  waiting for transfers between devices: 5.85 us -> 6.14 us
    pallas_call x1, Pallas kernels: 3.55 us -> 2.66 us  [shards(): pl.pallas_call(functools.partial(plane_kernel, bands, own_planes, norm_fa...]
    all_to_all x1, waiting for transfers between devices: 5.85 us -> 6.14 us  [shards(): lax.all_to_all(messages, ('band', 'pw'), split_axis=0, concat_axis=0, til...]
    pallas_call x1, Pallas kernels: 1.42 us -> 1.13 us  [shards(): pl.pallas_call(functools.partial(table_kernel, grid_len), out_shape=(jax....]
  transfers between devices with their start and end apart: 1 -> 1, of which waited for: 1 -> 1; matrix products, arithmetic and copies ran while one was open for 0% -> 0% of each run, Pallas kernels for 7% -> 6%
where the time goes in v11:
time: 19.8 us; the launch traced here: 19.6 us
  starting transfers between devices  7.3 us (37%)
  Pallas kernels  6.16 us (31%)
  waiting for transfers between devices  6.14 us (31%)
    all_to_all x1, starting transfers between devices, shards(): lax.all_to_all(messages, ('band', 'pw'), split_axis=0, concat_axis=0, til...  7.3 us
    all_to_all x1, waiting for transfers between devices, shards(): lax.all_to_all(messages, ('band', 'pw'), split_axis=0, concat_axis=0, til...  6.14 us
    pallas_call x1, Pallas kernels, shards(): pl.pallas_call(functools.partial(plane_kernel, bands, own_planes, norm_fa...  2.66 us
    pallas_call x1, Pallas kernels, shards(): pl.pallas_call(stick_kernel, out_shape=jax.ShapeDtypeStruct((devices, sti...  2.37 us
    pallas_call x1, Pallas kernels, shards(): pl.pallas_call(functools.partial(table_kernel, grid_len), out_shape=(jax....  1.13 us
  transfers between devices with their start and end apart: 1, of which 1 were waited for; matrix products, arithmetic and copies ran while one was open for 0% of the time, Pallas kernels for 6%

profile of v11, /device:TPU:0, one launch (start us, length us, event | category | flops | bytes accessed | tf_op | source)
XLA Modules:
  0.0 19.6 jit_solution(7931933804986984432)
XLA Ops:
  0.0 2.4 %stick_values.1 = bf16[32,8,128]{2,1,0:T(8,128)(2,1)} custom-call(s32[256]{0:T(256)} %length_hbm.1, s32[16]{0:T(128)} %plane_hbm.1, s32[2]{0:T(128)} %occupation_hbm.1, bf16[2,8,64]{2,1,0:T(8,128)(2,1)} %bitcast.4, bf16[1024,256]{1,0:T(8,128)(2,1)} %bitcast.3), custom_call_target="tpu_custom_call" | custom-call | tf_op jit(solution)/shard_map/stick_values/pallas_call | solution.py:415
  2.4 7.3 %all-to-all-start = ((bf16[32,8,128]{2,1,0:T(8,128)(2,1)}), bf16[32,8,128]{2,1,0:T(8,128)(2,1)S(1)}, u32[]{:S(2)}, u32[]{:S(2)}) async-start(bf16[32,8,128]{2,1,0:T(8,128)(2,1)} %stick_values.1), calls=%async_computation | async-start | bytes 131072 | tf_op jit(solution)/shard_map/all_to_all | solution.py:443
  9.7 1.1 %stick_tables.1 = (bf16[2,128,256]{2,1,0:T(8,128)(2,1)S(1)}, bf16[256,512]{1,0:T(8,128)(2,1)S(1)}) custom-call(s32[1,256]{1,0:T(1,128)} %bitcast.5), custom_call_target="tpu_custom_call" | custom-call | flops 5242880 | bytes 786432 | tf_op jit(solution)/shard_map/stick_tables/pallas_call | solution.py:444
  10.8 6.1 %all-to-all-done.message_ref = bf16[32,8,128]{2,1,0:T(8,128)(2,1)S(1)} async-done(((bf16[32,8,128]{2,1,0:T(8,128)(2,1)}), bf16[32,8,128]{2,1,0:T(8,128)(2,1)S(1)}, u32[]{:S(2)}, u32[]{:S(2)}) %all-to-all-start) | async-done | bytes 65568 | tf_op jit(solution)/shard_map/all_to_all | solution.py:443
  17.0 2.7 %plane_density.1 = f32[2,256,256]{2,1,0:T(8,128)} custom-call(bf16[32,8,128]{2,1,0:T(8,128)(2,1)S(1)} %all-to-all-done.message_ref, bf16[2,128,256]{2,1,0:T(8,128)(2,1)S(1)} %get-tuple-element.7.left_ref, bf16[256,512]{1,0:T(8,128)(2,1)S(1)} %get-tuple-element.8.right_ref), custom_call_target="tpu_custom_call" | custom-call | tf_op jit(solution)/shard_map/plane_density/pallas_call | solution.py:463
Async XLA Ops:
  2.4 14.6 %all-to-all-start = ((bf16[32,8,128]{2,1,0:T(8,128)(2,1)}), bf16[32,8,128]{2,1,0:T(8,128)(2,1)S(1)}, u32[]{:S(2)}, u32[]{:S(2)}) async-start(bf16[32,8,128]{2,1,0:T(8,128)(2,1)} %stick_values.1), calls=%async_computation | async-start | bytes 131072 | tf_op jit(solution)/shard_map/all_to_all | solution.py:443

commit v12 on v11

--- a/solution.py
+++ b/solution.py
@@ -13,6 +13,7 @@
 P_BLOCK = 32
 BAND_GROUP = 8
 GROUP_LANES = 256
+GATHER_LIMIT = 1 << 22
 COEFF_COPIES = 1
 MIB = 1024 * 1024
 
@@ -223,16 +224,9 @@
             return carry
 
         lax.fori_loop(0, pw_count // group_pw, one_group, 0)
-    copies = [
-        pltpu.make_async_copy(
-            message_ref, out_hbm.at[pl.ds(band * pw_count, pw_count)], sems.at[band]
-        )
-        for band in range(out_hbm.shape[0] // pw_count)
-    ]
-    for copy in copies:
-        copy.start()
-    for copy in copies:
-        copy.wait()
+    copy = pltpu.make_async_copy(message_ref, out_hbm, sems.at[0])
+    copy.start()
+    copy.wait()
 
 
 def table_kernel(grid_len, column_hbm, left_ref, right_ref, column_ref, sem):
@@ -262,15 +256,22 @@
     bands,
     own_planes,
     norm_factor,
-    message_ref,
+    gathered_ref,
     left_ref,
     right_ref,
     out_ref,
+    message_ref,
+    message_sem,
     value_ref,
     weight_ref,
     held_ref,
     sem,
 ):
+    place = lax.axis_index("pw") if gathered_ref.shape[1] > 1 else 0
+    copy = pltpu.make_async_copy(
+        gathered_ref.at[:, place], message_ref, message_sem
+    )
+    copy.start()
     rows, _, count = value_ref.shape
     chunk = min(out_ref.shape[1], count)
     chunks = count // chunk
@@ -296,6 +297,7 @@
             ).astype(jnp.bfloat16)
         return jnp.maximum(peak, jnp.max(picked[rows:], 1, keepdims=True))
 
+    copy.wait()
     peak = loop(chunks, turn, jnp.zeros((bands, 1), jnp.float32))
     weight_ref[...] = jnp.broadcast_to(peak * norm_factor, weight_ref.shape)
 
@@ -414,7 +416,7 @@
 
     messages = pl.pallas_call(
         stick_kernel,
-        out_shape=jax.ShapeDtypeStruct((devices, sticks, lanes), jnp.bfloat16),
+        out_shape=jax.ShapeDtypeStruct((pw_count, sticks, lanes), jnp.bfloat16),
         in_specs=[hbm] * 5,
         out_specs=hbm,
         scratch_shapes=[
@@ -440,7 +442,16 @@
             )
         )
     )
-    arrived = lax.all_to_all(messages, ("band", "pw"), split_axis=0, concat_axis=0, tiled=True)
+    if devices * pw_count * sticks * lanes <= GATHER_LIMIT:
+        arrived = lax.all_gather(messages, ("band", "pw"), axis=0)
+    else:
+        arrived = lax.all_to_all(
+            jnp.concatenate([messages] * band_count, 0),
+            ("band", "pw"),
+            split_axis=0,
+            concat_axis=0,
+            tiled=True,
+        )[:, None]
     left, right = pl.pallas_call(
         functools.partial(table_kernel, grid_len),
         out_shape=(
@@ -463,9 +474,11 @@
     return pl.pallas_call(
         functools.partial(plane_kernel, bands, own_planes, norm_factor),
         out_shape=jax.ShapeDtypeStruct((own_planes, grid_len, grid_len), jnp.float32),
-        in_specs=[vmem] * 3,
+        in_specs=[hbm, vmem, vmem],
         out_specs=hbm,
         scratch_shapes=[
+            pltpu.VMEM((devices, sticks, lanes), jnp.bfloat16),
+            pltpu.SemaphoreType.DMA,
             pltpu.VMEM((rows, PACK, stick_count), jnp.bfloat16),
             pltpu.VMEM((bands, LANES), jnp.float32),
             pltpu.VMEM((own_planes, grid_len, grid_len), jnp.float32),
@@ -473,7 +486,7 @@
         ],
         compiler_params=room(table_bytes, message_bytes),
         name="plane_density",
-    )(arrived, left, right)
+    )(pltpu.with_memory_space_constraint(arrived, pltpu.HBM), left, right)
 
 
 def solution(mesh):

time: 19.8 us -> 84 us (4.24)
  blocking collectives: 0 us -> 77.4 us
  starting transfers between devices: 7.3 us -> 0 us
  waiting for transfers between devices: 6.14 us -> 0 us
    all_gather x0 -> x1, blocking collectives: none -> 77.4 us  [shards(): arrived = lax.all_gather(messages, ('band', 'pw'), axis=0)]
    all_to_all x1 -> x0, starting transfers between devices: 7.3 us -> none  [shards(): lax.all_to_all(messages, ('band', 'pw'), split_axis=0, concat_axis=0, til...]
    all_to_all x1 -> x0, waiting for transfers between devices: 6.14 us -> none  [shards(): lax.all_to_all(messages, ('band', 'pw'), split_axis=0, concat_axis=0, til...]
    pallas_call x1, Pallas kernels: 2.66 us -> 3.53 us  [shards(): pl.pallas_call(functools.partial(plane_kernel, bands, own_planes, norm_fa...]
  transfers between devices with their start and end apart: 1 -> 0, of which waited for: 1 -> 0; matrix products, arithmetic and copies ran while one was open for 0% -> 0% of each run, Pallas kernels for 6% -> 0%
where the time goes in v12:
time: 84 us; the launch traced here: 83.8 us
  blocking collectives  77.4 us (92%)
  Pallas kernels  6.42 us (8%)
    all_gather x1, blocking collectives, shards(): arrived = lax.all_gather(messages, ('band', 'pw'), axis=0)  77.4 us
    pallas_call x1, Pallas kernels, shards(): pl.pallas_call(functools.partial(plane_kernel, bands, own_planes, norm_fa...  3.53 us
    pallas_call x1, Pallas kernels, shards(): pl.pallas_call(stick_kernel, out_shape=jax.ShapeDtypeStruct((pw_count, st...  1.76 us

profile of v12, /device:TPU:0, one launch (start us, length us, event | category | flops | bytes accessed | tf_op | source)
XLA Modules:
  0.0 83.8 jit_solution(7954612775797435432)
XLA Ops:
  0.0 1.8 %stick_values.1 = bf16[8,8,128]{2,1,0:T(8,128)(2,1)S(1)} custom-call(s32[256]{0:T(256)} %length_hbm.1, s32[16]{0:T(128)} %plane_hbm.1, s32[2]{0:T(128)} %occupation_hbm.1, bf16[2,8,64]{2,1,0:T(8,128)(2,1)} %bitcast.6, bf16[1024,256]{1,0:T(8,128)(2,1)} %bitcast.5), custom_call_target="tpu_custom_call" | custom-call | tf_op jit(solution)/shard_map/stick_values/pallas_call | solution.py:417
  1.8 1.1 %stick_tables.1 = (bf16[2,128,256]{2,1,0:T(8,128)(2,1)S(1)}, bf16[256,512]{1,0:T(8,128)(2,1)S(1)}) custom-call(s32[1,256]{1,0:T(1,128)} %bitcast.7), custom_call_target="tpu_custom_call" | custom-call | flops 5242880 | bytes 786432 | tf_op jit(solution)/shard_map/stick_tables/pallas_call | solution.py:455
  2.9 77.4 %all-gather = bf16[256,8,128]{2,1,0:T(8,128)(2,1)} all-gather(bf16[8,8,128]{2,1,0:T(8,128)(2,1)S(1)} %stick_values.1), channel_id=2, replica_groups=mesh['band'=4,'pw'=8] {'band','pw'}, dimensions={0}, use_global_device_ids=true | all-gather | bytes 540672 | tf_op jit(solution)/shard_map/all_gather | solution.py:446
  80.3 3.5 %plane_density.1 = f32[2,256,256]{2,1,0:T(8,128)} custom-call(bf16[32,8,8,128]{3,2,1,0:T(8,128)(2,1)} %bitcast.4, bf16[2,128,256]{2,1,0:T(8,128)(2,1)S(1)} %get-tuple-element.7.left_ref, bf16[256,512]{1,0:T(8,128)(2,1)S(1)} %get-tuple-element.8.right_ref), custom_call_target="tpu_custom_call" | custom-call | tf_op jit(solution)/shard_map/plane_density/pallas_call | solution.py:474

commit v13 on v11

--- a/solution.py
+++ b/solution.py
@@ -67,6 +67,13 @@
 
 def room(*sizes):
     return pltpu.CompilerParams(vmem_limit_bytes=min(56 * MIB, 16 * MIB + 2 * sum(sizes)))
+
+
+def lane_groups(sticks, spots, bands, lanes):
+    groups = 1
+    while 2 * groups * spots + bands <= lanes and sticks % (2 * groups) == 0 and sticks > 4 * groups:
+        groups *= 2
+    return groups
 
 
 def spread(scalars, index, shape):
@@ -121,6 +128,7 @@
 
     group_lanes = GROUP_LANES // (own_planes * 2 * out_count) * (own_planes * 2 * out_count)
     spots = own_planes * 2 * out_count
+    side = lane_groups(sticks, spots, out_count, lanes)
     group_pw = group_lanes // spots
 
     wide = in_count * sticks
@@ -148,7 +156,7 @@
     shape = (sticks, lanes)
     occupied = jnp.zeros(shape, jnp.int32)
     for own_band in range(own_bands):
-        lane = spots + band_index * own_bands + own_band
+        lane = side * spots + band_index * own_bands + own_band
         occupied = jnp.where(iota(shape, 1) == lane, occupation_ref[own_band], occupied)
     occupied = occupied.astype(jnp.float32)
 
@@ -199,11 +207,17 @@
         for place in range(group_pw):
             first = place * spots
             tile = first // lanes * lanes
-            piece = values[:, tile : tile + lanes]
-            if first > tile:
-                piece = pltpu.roll(piece, lanes - (first - tile), 1)
-            piece = jnp.where(iota((sticks, lanes), 1) < spots, piece, occupied)
-            message_ref[first_pw + place] = piece.astype(message_ref.dtype)
+            part = values[:, tile : tile + lanes]
+            message = occupied
+            for index in reversed(range(side)):
+                shift = (index * spots - (first - tile)) % lanes
+                piece = pltpu.roll(part, shift, 1) if shift else part
+                if index:
+                    piece = pltpu.roll(piece, sticks - index * (sticks // side), 0)
+                message = jnp.where(
+                    iota((sticks, lanes), 1) < (index + 1) * spots, piece, message
+                )
+            message_ref[first_pw + place] = message[: sticks // side].astype(message_ref.dtype)
 
     if group_pw == pw_count:
         form = forms(0)
@@ -235,13 +249,33 @@
         copy.wait()
 
 
-def table_kernel(grid_len, column_hbm, left_ref, right_ref, column_ref, sem):
+def reorder(columns, grid_len, chunk, sticks, side):
+    count = columns.shape[1]
+    shape = (chunk, chunk)
+    to, rows = iota(shape, 1), sticks // side
+    index, rest = lax.div(to, chunk // side), lax.rem(to, chunk // side)
+    source = lax.div(rest, rows) * sticks + index * rows + lax.rem(rest, rows)
+    order = (iota(shape, 0) == source).astype(jnp.bfloat16)
+    shape = (8, count)
+    columns = jnp.broadcast_to(columns, shape)
+    halves = jnp.where(iota(shape, 0) == 0, cut(columns, grid_len), wrap(columns, grid_len))
+    halves = halves.astype(jnp.float32).astype(jnp.bfloat16)
+    ordered = [
+        dot(halves[:, first : first + chunk], order) for first in range(0, count, chunk)
+    ]
+    ordered = jnp.concatenate(ordered, 1).astype(jnp.int32)
+    return ordered[:1] * grid_len + ordered[1:2]
+
+
+def table_kernel(grid_len, chunk, sticks, side, column_hbm, left_ref, right_ref, column_ref, sem):
     copy = pltpu.make_async_copy(column_hbm, column_ref, sem)
     copy.start()
     copy.wait()
     count = column_ref.shape[1]
     half = grid_len // 2
     columns = column_ref[...]
+    if side > 1:
+        columns = reorder(columns, grid_len, chunk, sticks, side)
     turns = iota((half, count), 0) * cut(columns, grid_len)
     left_ref[0] = cosine(turns, grid_len).astype(jnp.bfloat16)
     left_ref[1] = sine(turns, grid_len).astype(jnp.bfloat16)
@@ -262,12 +296,12 @@
     bands,
     own_planes,
     norm_factor,
+    sticks,
     message_ref,
     left_ref,
     right_ref,
     out_ref,
     value_ref,
-    weight_ref,
     held_ref,
     sem,
 ):
@@ -276,28 +310,43 @@
     chunks = count // chunk
     grid_len = out_ref.shape[1]
     half = grid_len // 2
-    sticks, lanes = message_ref.shape[1:]
+    message_rows, lanes = message_ref.shape[1:]
+    side = sticks // message_rows
     spots = 2 * bands
     height = math.gcd(half, P_BLOCK)
     blocks = half // height
     group = math.gcd(bands, BAND_GROUP)
-    select = (iota((rows + bands, lanes), 0) == iota((rows + bands, lanes), 1)).astype(
-        jnp.bfloat16
-    )
-
-    def turn(index, peak):
+    shape = (side * rows + bands, lanes)
+    select = (iota(shape, 0) == iota(shape, 1)).astype(jnp.bfloat16)
+
+    def turn(index):
         pieces = chunk // sticks
-        picked = dot_last(
-            select, message_ref[pl.ds(index * pieces, pieces)].reshape(chunk, lanes)
-        )
+        message = message_ref[pl.ds(index * pieces, pieces)]
+        return dot_last(select, message.reshape(pieces * message_rows, lanes))
+
+    def occupations(picked):
+        return jnp.max(picked[side * rows :], 1, keepdims=True)
+
+    def keep(index, picked, scale):
+        width = chunk // side
         for row in range(rows):
-            value_ref[row, :, pl.ds(index * chunk, chunk)] = jnp.broadcast_to(
-                picked[row : row + 1], (PACK, chunk)
-            ).astype(jnp.bfloat16)
-        return jnp.maximum(peak, jnp.max(picked[rows:], 1, keepdims=True))
-
-    peak = loop(chunks, turn, jnp.zeros((bands, 1), jnp.float32))
-    weight_ref[...] = jnp.broadcast_to(peak * norm_factor, weight_ref.shape)
+            for place in range(side):
+                piece = picked[place * rows + row : place * rows + row + 1]
+                piece = piece * scale[row % bands : row % bands + 1]
+                value_ref[row, :, pl.ds(index * chunk + place * width, width)] = (
+                    jnp.broadcast_to(piece, (PACK, width)).astype(jnp.bfloat16)
+                )
+
+    picked = turn(0)
+    found = occupations(picked)
+    for index in range(1, chunks):
+        found = jnp.maximum(found, occupations(turn(index)))
+    peak = jnp.max(found, 0, keepdims=True)
+    scale = jnp.where(found == peak, 1.0, jnp.sqrt(found / jnp.maximum(peak, 1.0)))
+    keep(0, picked, scale)
+    for index in range(1, chunks):
+        keep(index, turn(index), scale)
+    factor = peak * norm_factor
 
     def stick_sums(index, plane, block, first_band):
         lane = pl.ds(index * chunk, chunk)
@@ -329,8 +378,7 @@
                 )
         return found
 
-    def add_squares(step, found, sums):
-        first_band = step % groups * group
+    def add_squares(found, sums):
         result = []
         for place, (with_cos, with_sin, mixed) in enumerate(sums):
             plane, left = place // 2, place % 2 * grid_len
@@ -341,10 +389,9 @@
                 top += height
                 c = found[plane][top : top + height, left : left + half]
                 b = found[plane][top : top + height, left + half : left + grid_len]
-                weight = weight_ref[pl.ds(first_band + band, 1), :half]
-                with_cos += weight * (a * a + c * c)
-                with_sin += weight * (b * b + d * d)
-                mixed += weight * (c * d - a * b)
+                with_cos += a * a + c * c
+                with_sin += b * b + d * d
+                mixed += c * d - a * b
             result.append((with_cos, with_sin, mixed))
         return result
 
@@ -361,9 +408,9 @@
             ahead = jnp.where(lane == 0, with_cos, both + mixed)
             back = jnp.where(lane == 0, with_sin, both - mixed)
             row = pl.ds(place % 2 * half + block * height, height)
-            held_ref[place // 2, row, :half] = ahead
+            held_ref[place // 2, row, :half] = ahead * factor
             held_ref[place // 2, row, half:] = jnp.take_along_axis(
-                back, jnp.where(lane == 0, 0, half - lane), axis=1
+                back * factor, jnp.where(lane == 0, 0, half - lane), axis=1
             )
             copy_out(place, block).start()
 
@@ -375,7 +422,7 @@
         def one_block(block, carry):
             def one_group(index, sums):
                 step = block * groups + index
-                return add_squares(step, group_sums(step), sums)
+                return add_squares(group_sums(step), sums)
 
             finish(block, lax.fori_loop(0, groups, one_group, empty))
             return carry
@@ -387,7 +434,7 @@
             found = ahead
             if step + 1 < blocks * groups:
                 ahead = group_sums(step + 1)
-            sums = add_squares(step, found, sums)
+            sums = add_squares(found, sums)
             if (step + 1) % groups == 0:
                 finish(step // groups, sums)
                 sums = empty
@@ -407,6 +454,8 @@
     spots = 2 * bands
     rows = own_planes * spots
     lanes = -(-(rows + bands) // LANES) * LANES
+    side = lane_groups(sticks, rows, bands, lanes)
+    message_rows = sticks // side
     vmem = pl.BlockSpec(memory_space=pltpu.VMEM)
     hbm = pl.BlockSpec(memory_space=pltpu.HBM)
     table_bytes = 8 * grid_len * stick_count
@@ -414,7 +463,7 @@
 
     messages = pl.pallas_call(
         stick_kernel,
-        out_shape=jax.ShapeDtypeStruct((devices, sticks, lanes), jnp.bfloat16),
+        out_shape=jax.ShapeDtypeStruct((devices, message_rows, lanes), jnp.bfloat16),
         in_specs=[hbm] * 5,
         out_specs=hbm,
         scratch_shapes=[
@@ -423,7 +472,7 @@
             pltpu.SMEM(occupation.shape, jnp.int32),
             pltpu.VMEM((2, bands, in_count), jnp.bfloat16),
             pltpu.VMEM((2 * in_count * sticks, grid_len), jnp.bfloat16),
-            pltpu.VMEM((pw_count, sticks, lanes), jnp.bfloat16),
+            pltpu.VMEM((pw_count, message_rows, lanes), jnp.bfloat16),
             pltpu.SemaphoreType.DMA((max(4 + COEFF_COPIES, band_count),)),
         ],
         compiler_params=room(2 * message_bytes),
@@ -442,7 +491,7 @@
     )
     arrived = lax.all_to_all(messages, ("band", "pw"), split_axis=0, concat_axis=0, tiled=True)
     left, right = pl.pallas_call(
-        functools.partial(table_kernel, grid_len),
+        functools.partial(table_kernel, grid_len, min(grid_len, stick_count), sticks, side),
         out_shape=(
             jax.ShapeDtypeStruct((2, grid_len // 2, stick_count), jnp.bfloat16),
             jax.ShapeDtypeStruct((stick_count, 2 * grid_len), jnp.bfloat16),
@@ -461,13 +510,12 @@
     norm_factor = 1.0 / float(bands * stick_count * grid_len)
     blocks = 2 * own_planes * (grid_len // 2 // math.gcd(grid_len // 2, P_BLOCK))
     return pl.pallas_call(
-        functools.partial(plane_kernel, bands, own_planes, norm_factor),
+        functools.partial(plane_kernel, bands, own_planes, norm_factor, sticks),
         out_shape=jax.ShapeDtypeStruct((own_planes, grid_len, grid_len), jnp.float32),
         in_specs=[vmem] * 3,
         out_specs=hbm,
         scratch_shapes=[
             pltpu.VMEM((rows, PACK, stick_count), jnp.bfloat16),
-            pltpu.VMEM((bands, LANES), jnp.float32),
             pltpu.VMEM((own_planes, grid_len, grid_len), jnp.float32),
             pltpu.SemaphoreType.DMA((blocks,)),
         ],

time: 19.8 us -> 19.6 us (0.990)
  waiting for transfers between devices: 6.14 us -> 5.89 us
    all_to_all x1, waiting for transfers between devices: 6.14 us -> 5.89 us  [shards(): lax.all_to_all(messages, ('band', 'pw'), split_axis=0, concat_axis=0, til...]
  transfers between devices with their start and end apart: 1 -> 1, of which waited for: 1 -> 1; matrix products, arithmetic and copies ran while one was open for 0% -> 0% of each run, Pallas kernels for 6% -> 7%
where the time goes in v13:
time: 19.6 us; the launch traced here: 19.4 us
  starting transfers between devices  7.3 us (37%)
  Pallas kernels  6.23 us (32%)
  waiting for transfers between devices  5.89 us (30%)
    all_to_all x1, starting transfers between devices, shards(): lax.all_to_all(messages, ('band', 'pw'), split_axis=0, concat_axis=0, til...  7.3 us
    all_to_all x1, waiting for transfers between devices, shards(): lax.all_to_all(messages, ('band', 'pw'), split_axis=0, concat_axis=0, til...  5.89 us
    pallas_call x1, Pallas kernels, shards(): pl.pallas_call(functools.partial(plane_kernel, bands, own_planes, norm_fa...  2.57 us
    pallas_call x1, Pallas kernels, shards(): pl.pallas_call(stick_kernel, out_shape=jax.ShapeDtypeStruct((devices, mes...  2.36 us
    pallas_call x1, Pallas kernels, shards(): pl.pallas_call(functools.partial(table_kernel, grid_len, min(grid_len, st...  1.29 us
  transfers between devices with their start and end apart: 1, of which 1 were waited for; matrix products, arithmetic and copies ran while one was open for 0% of the time, Pallas kernels for 7%

profile of v13, /device:TPU:0, one launch (start us, length us, event | category | flops | bytes accessed | tf_op | source)
XLA Modules:
  0.0 19.4 jit_solution(16731714837798995028)
XLA Ops:
  0.0 2.4 %stick_values.1 = bf16[32,4,128]{2,1,0:T(4,128)(2,1)} custom-call(s32[256]{0:T(256)} %length_hbm.1, s32[16]{0:T(128)} %plane_hbm.1, s32[2]{0:T(128)} %occupation_hbm.1, bf16[2,8,64]{2,1,0:T(8,128)(2,1)} %bitcast.4, bf16[1024,256]{1,0:T(8,128)(2,1)} %bitcast.3), custom_call_target="tpu_custom_call" | custom-call | tf_op jit(solution)/shard_map/stick_values/pallas_call | solution.py:464
  2.4 7.3 %all-to-all-start = ((bf16[32,4,128]{2,1,0:T(4,128)(2,1)}), bf16[32,4,128]{2,1,0:T(4,128)(2,1)S(1)}, u32[]{:S(2)}, u32[]{:S(2)}) async-start(bf16[32,4,128]{2,1,0:T(4,128)(2,1)} %stick_values.1), calls=%async_computation | async-start | bytes 65536 | tf_op jit(solution)/shard_map/all_to_all | solution.py:492
  9.7 1.3 %stick_tables.1 = (bf16[2,128,256]{2,1,0:T(8,128)(2,1)S(1)}, bf16[256,512]{1,0:T(8,128)(2,1)S(1)}) custom-call(s32[1,256]{1,0:T(1,128)} %bitcast.5), custom_call_target="tpu_custom_call" | custom-call | flops 5242880 | bytes 786432 | tf_op jit(solution)/shard_map/stick_tables/pallas_call | solution.py:493
  11.0 5.9 %all-to-all-done.message_ref = bf16[32,4,128]{2,1,0:T(4,128)(2,1)S(1)} async-done(((bf16[32,4,128]{2,1,0:T(4,128)(2,1)}), bf16[32,4,128]{2,1,0:T(4,128)(2,1)S(1)}, u32[]{:S(2)}, u32[]{:S(2)}) %all-to-all-start) | async-done | bytes 32800 | tf_op jit(solution)/shard_map/all_to_all | solution.py:492
  16.9 2.6 %plane_density.1 = f32[2,256,256]{2,1,0:T(8,128)} custom-call(bf16[32,4,128]{2,1,0:T(4,128)(2,1)S(1)} %all-to-all-done.message_ref, bf16[2,128,256]{2,1,0:T(8,128)(2,1)S(1)} %get-tuple-element.7.left_ref, bf16[256,512]{1,0:T(8,128)(2,1)S(1)} %get-tuple-element.8.right_ref), custom_call_target="tpu_custom_call" | custom-call | tf_op jit(solution)/shard_map/plane_density/pallas_call | solution.py:512
Async XLA Ops:
  2.4 14.5 %all-to-all-start = ((bf16[32,4,128]{2,1,0:T(4,128)(2,1)}), bf16[32,4,128]{2,1,0:T(4,128)(2,1)S(1)}, u32[]{:S(2)}, u32[]{:S(2)}) async-start(bf16[32,4,128]{2,1,0:T(4,128)(2,1)} %stick_values.1), calls=%async_computation | async-start | bytes 65536 | tf_op jit(solution)/shard_map/all_to_all | solution.py:492

commit v14 on v13

--- a/solution.py
+++ b/solution.py
@@ -13,7 +13,7 @@
 P_BLOCK = 32
 BAND_GROUP = 8
 GROUP_LANES = 256
-COEFF_COPIES = 1
+COEFF_COPIES = 4
 MIB = 1024 * 1024
 
 
@@ -105,10 +105,10 @@
         for index, (source, target) in enumerate(
             (
                 (rotation_hbm, rotation_ref),
-                *((coeff_hbm.at[rows], coeff_ref.at[rows]) for rows in pieces),
                 (plane_hbm, plane_ref),
                 (length_hbm, length_ref),
                 (occupation_hbm, occupation_ref),
+                *((coeff_hbm.at[rows], coeff_ref.at[rows]) for rows in pieces),
             )
         )
     ]
@@ -148,7 +148,7 @@
         rows[1, band] = jnp.concatenate([imag, real], 1)
     rotation = jnp.concatenate([rows[key] for key in sorted(rows)], 0).astype(jnp.bfloat16)
 
-    for copy in copies[1 + COEFF_COPIES :]:
+    for copy in copies[1:4]:
         copy.wait()
     lengths = [length_ref[first_stick + place] for place in range(sticks)]
     row_lengths = spread(lengths, iota((sticks, grid_len), 0), (sticks, grid_len))
@@ -221,10 +221,9 @@
 
     if group_pw == pw_count:
         form = forms(0)
-    rotated = jnp.zeros((row_count, grid_len), jnp.float32)
-    for index, where in enumerate(pieces):
-        copies[1 + index].wait()
-        rotated += dot(rotation[:, index * piece : (index + 1) * piece], coeff_ref[where])
+    for copy in copies[4:]:
+        copy.wait()
+    rotated = dot(rotation, coeff_ref[...])
     rotated = rotated.reshape(row_count // sticks, sticks, grid_len)
     rotated = jnp.where(live[None], rotated, 0.0).reshape(row_count, grid_len)
     rotated = rotated.astype(jnp.bfloat16)

time: 19.6 us -> 19.7 us (level)
  no operation moved by 1% of the time
where the time goes in v14:
time: 19.7 us; the launch traced here: 19.5 us
  starting transfers between devices  7.3 us (37%)
  Pallas kernels  6.25 us (32%)
  waiting for transfers between devices  5.89 us (30%)
    all_to_all x1, starting transfers between devices, shards(): lax.all_to_all(messages, ('band', 'pw'), split_axis=0, concat_axis=0, til...  7.3 us
    all_to_all x1, waiting for transfers between devices, shards(): lax.all_to_all(messages, ('band', 'pw'), split_axis=0, concat_axis=0, til...  5.89 us
    pallas_call x1, Pallas kernels, shards(): pl.pallas_call(functools.partial(plane_kernel, bands, own_planes, norm_fa...  2.56 us
    pallas_call x1, Pallas kernels, shards(): pl.pallas_call(stick_kernel, out_shape=jax.ShapeDtypeStruct((devices, mes...  2.4 us
    pallas_call x1, Pallas kernels, shards(): pl.pallas_call(functools.partial(table_kernel, grid_len, min(grid_len, st...  1.29 us
  transfers between devices with their start and end apart: 1, of which 1 were waited for; matrix products, arithmetic and copies ran while one was open for 0% of the time, Pallas kernels for 7%

profile of v14, /device:TPU:0, one launch (start us, length us, event | category | flops | bytes accessed | tf_op | source)
XLA Modules:
  0.0 19.5 jit_solution(15982295630249609761)
XLA Ops:
  0.0 2.4 %stick_values.1 = bf16[32,4,128]{2,1,0:T(4,128)(2,1)} custom-call(s32[256]{0:T(256)} %length_hbm.1, s32[16]{0:T(128)} %plane_hbm.1, s32[2]{0:T(128)} %occupation_hbm.1, bf16[2,8,64]{2,1,0:T(8,128)(2,1)} %bitcast.4, bf16[1024,256]{1,0:T(8,128)(2,1)} %bitcast.3), custom_call_target="tpu_custom_call" | custom-call | tf_op jit(solution)/shard_map/stick_values/pallas_call | solution.py:463
  2.4 7.3 %all-to-all-start = ((bf16[32,4,128]{2,1,0:T(4,128)(2,1)}), bf16[32,4,128]{2,1,0:T(4,128)(2,1)S(1)}, u32[]{:S(2)}, u32[]{:S(2)}) async-start(bf16[32,4,128]{2,1,0:T(4,128)(2,1)} %stick_values.1), calls=%async_computation | async-start | bytes 65536 | tf_op jit(solution)/shard_map/all_to_all | solution.py:491
  9.7 1.3 %stick_tables.1 = (bf16[2,128,256]{2,1,0:T(8,128)(2,1)S(1)}, bf16[256,512]{1,0:T(8,128)(2,1)S(1)}) custom-call(s32[1,256]{1,0:T(1,128)} %bitcast.5), custom_call_target="tpu_custom_call" | custom-call | flops 5242880 | bytes 786432 | tf_op jit(solution)/shard_map/stick_tables/pallas_call | solution.py:492
  11.0 5.9 %all-to-all-done.message_ref = bf16[32,4,128]{2,1,0:T(4,128)(2,1)S(1)} async-done(((bf16[32,4,128]{2,1,0:T(4,128)(2,1)}), bf16[32,4,128]{2,1,0:T(4,128)(2,1)S(1)}, u32[]{:S(2)}, u32[]{:S(2)}) %all-to-all-start) | async-done | bytes 32800 | tf_op jit(solution)/shard_map/all_to_all | solution.py:491
  16.9 2.6 %plane_density.1 = f32[2,256,256]{2,1,0:T(8,128)} custom-call(bf16[32,4,128]{2,1,0:T(4,128)(2,1)S(1)} %all-to-all-done.message_ref, bf16[2,128,256]{2,1,0:T(8,128)(2,1)S(1)} %get-tuple-element.7.left_ref, bf16[256,512]{1,0:T(8,128)(2,1)S(1)} %get-tuple-element.8.right_ref), custom_call_target="tpu_custom_call" | custom-call | tf_op jit(solution)/shard_map/plane_density/pallas_call | solution.py:511
Async XLA Ops:
  2.4 14.5 %all-to-all-start = ((bf16[32,4,128]{2,1,0:T(4,128)(2,1)}), bf16[32,4,128]{2,1,0:T(4,128)(2,1)S(1)}, u32[]{:S(2)}, u32[]{:S(2)}) async-start(bf16[32,4,128]{2,1,0:T(4,128)(2,1)} %stick_values.1), calls=%async_computation | async-start | bytes 65536 | tf_op jit(solution)/shard_map/all_to_all | solution.py:491

commit v15 on v14

--- a/solution.py
+++ b/solution.py
@@ -10,7 +10,7 @@
 
 LANES = 128
 PACK = 16
-P_BLOCK = 32
+P_BLOCK = 64
 BAND_GROUP = 8
 GROUP_LANES = 256
 COEFF_COPIES = 4
@@ -67,6 +67,10 @@
 
 def room(*sizes):
     return pltpu.CompilerParams(vmem_limit_bytes=min(56 * MIB, 16 * MIB + 2 * sum(sizes)))
+
+
+def row_block(grid_len, stick_count):
+    return math.gcd(grid_len // 2, P_BLOCK if stick_count <= grid_len else P_BLOCK // 2)
 
 
 def lane_groups(sticks, spots, bands, lanes):
@@ -148,8 +152,9 @@
         rows[1, band] = jnp.concatenate([imag, real], 1)
     rotation = jnp.concatenate([rows[key] for key in sorted(rows)], 0).astype(jnp.bfloat16)
 
-    for copy in copies[1:4]:
+    for copy in copies[1:]:
         copy.wait()
+    rotated = dot(rotation, coeff_ref[...])
     lengths = [length_ref[first_stick + place] for place in range(sticks)]
     row_lengths = spread(lengths, iota((sticks, grid_len), 0), (sticks, grid_len))
     live = iota((sticks, grid_len), 1) < row_lengths
@@ -221,9 +226,6 @@
 
     if group_pw == pw_count:
         form = forms(0)
-    for copy in copies[4:]:
-        copy.wait()
-    rotated = dot(rotation, coeff_ref[...])
     rotated = rotated.reshape(row_count // sticks, sticks, grid_len)
     rotated = jnp.where(live[None], rotated, 0.0).reshape(row_count, grid_len)
     rotated = rotated.astype(jnp.bfloat16)
@@ -312,7 +314,7 @@
     message_rows, lanes = message_ref.shape[1:]
     side = sticks // message_rows
     spots = 2 * bands
-    height = math.gcd(half, P_BLOCK)
+    height = row_block(grid_len, count)
     blocks = half // height
     group = math.gcd(bands, BAND_GROUP)
     shape = (side * rows + bands, lanes)
@@ -507,7 +509,7 @@
         name="stick_tables",
     )(pltpu.with_memory_space_constraint(stick_column.reshape(1, stick_count), pltpu.HBM))
     norm_factor = 1.0 / float(bands * stick_count * grid_len)
-    blocks = 2 * own_planes * (grid_len // 2 // math.gcd(grid_len // 2, P_BLOCK))
+    blocks = 2 * own_planes * (grid_len // 2 // row_block(grid_len, stick_count))
     return pl.pallas_call(
         functools.partial(plane_kernel, bands, own_planes, norm_factor, sticks),
         out_shape=jax.ShapeDtypeStruct((own_planes, grid_len, grid_len), jnp.float32),

time: 19.7 us -> 19.7 us (level)
  no operation moved by 1% of the time
where the time goes in v15:
time: 19.7 us; the launch traced here: 19.5 us
  starting transfers between devices  7.3 us (37%)
  Pallas kernels  6.27 us (32%)
  waiting for transfers between devices  5.89 us (30%)
    all_to_all x1, starting transfers between devices, shards(): lax.all_to_all(messages, ('band', 'pw'), split_axis=0, concat_axis=0, til...  7.3 us
    all_to_all x1, waiting for transfers between devices, shards(): lax.all_to_all(messages, ('band', 'pw'), split_axis=0, concat_axis=0, til...  5.89 us
    pallas_call x1, Pallas kernels, shards(): pl.pallas_call(functools.partial(plane_kernel, bands, own_planes, norm_fa...  2.62 us
    pallas_call x1, Pallas kernels, shards(): pl.pallas_call(stick_kernel, out_shape=jax.ShapeDtypeStruct((devices, mes...  2.37 us
    pallas_call x1, Pallas kernels, shards(): pl.pallas_call(functools.partial(table_kernel, grid_len, min(grid_len, st...  1.29 us
  transfers between devices with their start and end apart: 1, of which 1 were waited for; matrix products, arithmetic and copies ran while one was open for 0% of the time, Pallas kernels for 7%

profile of v15, /device:TPU:0, one launch (start us, length us, event | category | flops | bytes accessed | tf_op | source)
XLA Modules:
  0.0 19.5 jit_solution(11366947215603447552)
XLA Ops:
  0.0 2.4 %stick_values.1 = bf16[32,4,128]{2,1,0:T(4,128)(2,1)} custom-call(s32[256]{0:T(256)} %length_hbm.1, s32[16]{0:T(128)} %plane_hbm.1, s32[2]{0:T(128)} %occupation_hbm.1, bf16[2,8,64]{2,1,0:T(8,128)(2,1)} %bitcast.4, bf16[1024,256]{1,0:T(8,128)(2,1)} %bitcast.3), custom_call_target="tpu_custom_call" | custom-call | tf_op jit(solution)/shard_map/stick_values/pallas_call | solution.py:465
  2.4 7.3 %all-to-all-start = ((bf16[32,4,128]{2,1,0:T(4,128)(2,1)}), bf16[32,4,128]{2,1,0:T(4,128)(2,1)S(1)}, u32[]{:S(2)}, u32[]{:S(2)}) async-start(bf16[32,4,128]{2,1,0:T(4,128)(2,1)} %stick_values.1), calls=%async_computation | async-start | bytes 65536 | tf_op jit(solution)/shard_map/all_to_all | solution.py:493
  9.7 1.3 %stick_tables.1 = (bf16[2,128,256]{2,1,0:T(8,128)(2,1)S(1)}, bf16[256,512]{1,0:T(8,128)(2,1)S(1)}) custom-call(s32[1,256]{1,0:T(1,128)} %bitcast.5), custom_call_target="tpu_custom_call" | custom-call | flops 5242880 | bytes 786432 | tf_op jit(solution)/shard_map/stick_tables/pallas_call | solution.py:494
  11.0 5.9 %all-to-all-done.message_ref = bf16[32,4,128]{2,1,0:T(4,128)(2,1)S(1)} async-done(((bf16[32,4,128]{2,1,0:T(4,128)(2,1)}), bf16[32,4,128]{2,1,0:T(4,128)(2,1)S(1)}, u32[]{:S(2)}, u32[]{:S(2)}) %all-to-all-start) | async-done | bytes 32800 | tf_op jit(solution)/shard_map/all_to_all | solution.py:493
  16.9 2.6 %plane_density.1 = f32[2,256,256]{2,1,0:T(8,128)} custom-call(bf16[32,4,128]{2,1,0:T(4,128)(2,1)S(1)} %all-to-all-done.message_ref, bf16[2,128,256]{2,1,0:T(8,128)(2,1)S(1)} %get-tuple-element.7.left_ref, bf16[256,512]{1,0:T(8,128)(2,1)S(1)} %get-tuple-element.8.right_ref), custom_call_target="tpu_custom_call" | custom-call | tf_op jit(solution)/shard_map/plane_density/pallas_call | solution.py:513
Async XLA Ops:
  2.4 14.5 %all-to-all-start = ((bf16[32,4,128]{2,1,0:T(4,128)(2,1)}), bf16[32,4,128]{2,1,0:T(4,128)(2,1)S(1)}, u32[]{:S(2)}, u32[]{:S(2)}) async-start(bf16[32,4,128]{2,1,0:T(4,128)(2,1)} %stick_values.1), calls=%async_computation | async-start | bytes 65536 | tf_op jit(solution)/shard_map/all_to_all | solution.py:493

commit v16 on v15

--- a/solution.py
+++ b/solution.py
@@ -10,7 +10,7 @@
 
 LANES = 128
 PACK = 16
-P_BLOCK = 64
+P_BLOCK = 32
 BAND_GROUP = 8
 GROUP_LANES = 256
 COEFF_COPIES = 4
@@ -222,7 +222,7 @@
                 message = jnp.where(
                     iota((sticks, lanes), 1) < (index + 1) * spots, piece, message
                 )
-            message_ref[first_pw + place] = message[: sticks // side].astype(message_ref.dtype)
+            message_ref[pw_count - 1 - first_pw - place] = message[: sticks // side].astype(message_ref.dtype)
 
     if group_pw == pw_count:
         form = forms(0)
@@ -255,14 +255,15 @@
     shape = (chunk, chunk)
     to, rows = iota(shape, 1), sticks // side
     index, rest = lax.div(to, chunk // side), lax.rem(to, chunk // side)
-    source = lax.div(rest, rows) * sticks + index * rows + lax.rem(rest, rows)
+    device = chunk // sticks - 1 - lax.div(rest, rows)
+    source = device * sticks + index * rows + lax.rem(rest, rows)
     order = (iota(shape, 0) == source).astype(jnp.bfloat16)
     shape = (8, count)
     columns = jnp.broadcast_to(columns, shape)
     halves = jnp.where(iota(shape, 0) == 0, cut(columns, grid_len), wrap(columns, grid_len))
     halves = halves.astype(jnp.float32).astype(jnp.bfloat16)
     ordered = [
-        dot(halves[:, first : first + chunk], order) for first in range(0, count, chunk)
+        dot(halves[:, first : first + chunk], order) for first in range(0, count, chunk)[::-1]
     ]
     ordered = jnp.concatenate(ordered, 1).astype(jnp.int32)
     return ordered[:1] * grid_len + ordered[1:2]
@@ -275,8 +276,7 @@
     count = column_ref.shape[1]
     half = grid_len // 2
     columns = column_ref[...]
-    if side > 1:
-        columns = reorder(columns, grid_len, chunk, sticks, side)
+    columns = reorder(columns, grid_len, chunk, sticks, side)
     turns = iota((half, count), 0) * cut(columns, grid_len)
     left_ref[0] = cosine(turns, grid_len).astype(jnp.bfloat16)
     left_ref[1] = sine(turns, grid_len).astype(jnp.bfloat16)
@@ -490,7 +490,14 @@
             )
         )
     )
-    arrived = lax.all_to_all(messages, ("band", "pw"), split_axis=0, concat_axis=0, tiled=True)
+    arrived = lax.all_to_all(
+        messages,
+        ("band", "pw"),
+        split_axis=0,
+        concat_axis=0,
+        axis_index_groups=[list(range(devices))[::-1]],
+        tiled=True,
+    )
     left, right = pl.pallas_call(
         functools.partial(table_kernel, grid_len, min(grid_len, stick_count), sticks, side),
         out_shape=(

time: 19.7 us -> 19.7 us (level)
  no operation moved by 1% of the time
where the time goes in v16:
time: 19.7 us; the launch traced here: 19.5 us
  starting transfers between devices  7.3 us (37%)
  Pallas kernels  6.23 us (32%)
  waiting for transfers between devices  5.98 us (30%)
    all_to_all x1, starting transfers between devices, shards(): lax.all_to_all(messages, ('band', 'pw'), split_axis=0, concat_axis=0, axi...  7.3 us
    all_to_all x1, waiting for transfers between devices, shards(): lax.all_to_all(messages, ('band', 'pw'), split_axis=0, concat_axis=0, axi...  5.98 us
    pallas_call x1, Pallas kernels, shards(): pl.pallas_call(functools.partial(plane_kernel, bands, own_planes, norm_fa...  2.57 us
    pallas_call x1, Pallas kernels, shards(): pl.pallas_call(stick_kernel, out_shape=jax.ShapeDtypeStruct((devices, mes...  2.37 us
    pallas_call x1, Pallas kernels, shards(): pl.pallas_call(functools.partial(table_kernel, grid_len, min(grid_len, st...  1.29 us
  transfers between devices with their start and end apart: 1, of which 1 were waited for; matrix products, arithmetic and copies ran while one was open for 0% of the time, Pallas kernels for 7%

profile of v16, /device:TPU:0, one launch (start us, length us, event | category | flops | bytes accessed | tf_op | source)
XLA Modules:
  0.0 19.5 jit_solution(4466330626728739418)
XLA Ops:
  0.0 2.4 %stick_values.1 = bf16[32,4,128]{2,1,0:T(4,128)(2,1)} custom-call(s32[256]{0:T(256)} %length_hbm.1, s32[16]{0:T(128)} %plane_hbm.1, s32[2]{0:T(128)} %occupation_hbm.1, bf16[2,8,64]{2,1,0:T(8,128)(2,1)} %bitcast.4, bf16[1024,256]{1,0:T(8,128)(2,1)} %bitcast.3), custom_call_target="tpu_custom_call" | custom-call | tf_op jit(solution)/shard_map/stick_values/pallas_call | solution.py:465
  2.4 7.3 %all-to-all-start = ((bf16[32,4,128]{2,1,0:T(4,128)(2,1)}), bf16[32,4,128]{2,1,0:T(4,128)(2,1)S(1)}, u32[]{:S(2)}, u32[]{:S(2)}) async-start(bf16[32,4,128]{2,1,0:T(4,128)(2,1)} %stick_values.1), calls=%async_computation | async-start | bytes 65536 | tf_op jit(solution)/shard_map/all_to_all | solution.py:493
  9.7 1.3 %stick_tables.1 = (bf16[2,128,256]{2,1,0:T(8,128)(2,1)S(1)}, bf16[256,512]{1,0:T(8,128)(2,1)S(1)}) custom-call(s32[1,256]{1,0:T(1,128)} %bitcast.5), custom_call_target="tpu_custom_call" | custom-call | flops 5242880 | bytes 786432 | tf_op jit(solution)/shard_map/stick_tables/pallas_call | solution.py:501
  11.0 6.0 %all-to-all-done.message_ref = bf16[32,4,128]{2,1,0:T(4,128)(2,1)S(1)} async-done(((bf16[32,4,128]{2,1,0:T(4,128)(2,1)}), bf16[32,4,128]{2,1,0:T(4,128)(2,1)S(1)}, u32[]{:S(2)}, u32[]{:S(2)}) %all-to-all-start) | async-done | bytes 32800 | tf_op jit(solution)/shard_map/all_to_all | solution.py:493
  17.0 2.6 %plane_density.1 = f32[2,256,256]{2,1,0:T(8,128)} custom-call(bf16[32,4,128]{2,1,0:T(4,128)(2,1)S(1)} %all-to-all-done.message_ref, bf16[2,128,256]{2,1,0:T(8,128)(2,1)S(1)} %get-tuple-element.7.left_ref, bf16[256,512]{1,0:T(8,128)(2,1)S(1)} %get-tuple-element.8.right_ref), custom_call_target="tpu_custom_call" | custom-call | tf_op jit(solution)/shard_map/plane_density/pallas_call | solution.py:520
Async XLA Ops:
  2.4 14.6 %all-to-all-start = ((bf16[32,4,128]{2,1,0:T(4,128)(2,1)}), bf16[32,4,128]{2,1,0:T(4,128)(2,1)S(1)}, u32[]{:S(2)}, u32[]{:S(2)}) async-start(bf16[32,4,128]{2,1,0:T(4,128)(2,1)} %stick_values.1), calls=%async_computation | async-start | bytes 65536 | tf_op jit(solution)/shard_map/all_to_all | solution.py:493

commit v17 on v15

--- a/solution.py
+++ b/solution.py
@@ -10,7 +10,7 @@
 
 LANES = 128
 PACK = 16
-P_BLOCK = 64
+P_BLOCK = 16
 BAND_GROUP = 8
 GROUP_LANES = 256
 COEFF_COPIES = 4
@@ -69,8 +69,8 @@
     return pltpu.CompilerParams(vmem_limit_bytes=min(56 * MIB, 16 * MIB + 2 * sum(sizes)))
 
 
-def row_block(grid_len, stick_count):
-    return math.gcd(grid_len // 2, P_BLOCK if stick_count <= grid_len else P_BLOCK // 2)
+def row_block(grid_len):
+    return math.gcd(grid_len // 2, P_BLOCK)
 
 
 def lane_groups(sticks, spots, bands, lanes):
@@ -238,16 +238,11 @@
             return carry
 
         lax.fori_loop(0, pw_count // group_pw, one_group, 0)
-    copies = [
-        pltpu.make_async_copy(
-            message_ref, out_hbm.at[pl.ds(band * pw_count, pw_count)], sems.at[band]
-        )
-        for band in range(out_hbm.shape[0] // pw_count)
-    ]
-    for copy in copies:
-        copy.start()
-    for copy in copies:
-        copy.wait()
+    for band in range(1, out_hbm.shape[0] // pw_count):
+        message_ref[band * pw_count : (band + 1) * pw_count] = message_ref[:pw_count]
+    copy = pltpu.make_async_copy(message_ref, out_hbm, sems.at[0])
+    copy.start()
+    copy.wait()
 
 
 def reorder(columns, grid_len, chunk, sticks, side):
@@ -314,7 +309,7 @@
     message_rows, lanes = message_ref.shape[1:]
     side = sticks // message_rows
     spots = 2 * bands
-    height = row_block(grid_len, count)
+    height = row_block(grid_len)
     blocks = half // height
     group = math.gcd(bands, BAND_GROUP)
     shape = (side * rows + bands, lanes)
@@ -349,47 +344,42 @@
         keep(index, turn(index), scale)
     factor = peak * norm_factor
 
-    def stick_sums(index, plane, block, first_band):
+    def stick_sums(index, block, first_band):
         lane = pl.ds(index * chunk, chunk)
         row = pl.ds(block * height, height)
         cos_table = left_ref[0, row, lane].reshape(height // PACK, PACK, chunk)
         sin_table = left_ref[1, row, lane].reshape(height // PACK, PACK, chunk)
         parts = []
-        for band in range(group):
-            at = plane * spots + first_band + band
-            real, imag = value_ref[at, :, lane][None], value_ref[at + bands, :, lane][None]
-            parts.append((cos_table * real - sin_table * imag).reshape(height, chunk))
-            parts.append((sin_table * real + cos_table * imag).reshape(height, chunk))
+        for plane in range(own_planes):
+            for band in range(group):
+                at = plane * spots + first_band + band
+                real, imag = value_ref[at, :, lane][None], value_ref[at + bands, :, lane][None]
+                parts.append((cos_table * real - sin_table * imag).reshape(height, chunk))
+                parts.append((sin_table * real + cos_table * imag).reshape(height, chunk))
         return dot(jnp.concatenate(parts, 0), right_ref[pl.ds(index * chunk, chunk), :])
 
     def group_sums(step):
         first_band, block = step % groups * group, step // groups
-        found = []
-        for plane in range(own_planes):
-            if chunks == 1:
-                found.append(stick_sums(0, plane, block, first_band))
-            else:
-                found.append(
-                    lax.fori_loop(
-                        0,
-                        chunks,
-                        lambda at, so_far: so_far + stick_sums(at, plane, block, first_band),
-                        jnp.zeros((2 * group * height, 2 * grid_len), jnp.float32),
-                    )
-                )
-        return found
+        if chunks == 1:
+            return stick_sums(0, block, first_band)
+        return lax.fori_loop(
+            0,
+            chunks,
+            lambda at, so_far: so_far + stick_sums(at, block, first_band),
+            jnp.zeros((2 * own_planes * group * height, 2 * grid_len), jnp.float32),
+        )
 
     def add_squares(found, sums):
         result = []
         for place, (with_cos, with_sin, mixed) in enumerate(sums):
             plane, left = place // 2, place % 2 * grid_len
             for band in range(group):
-                top = 2 * band * height
-                a = found[plane][top : top + height, left : left + half]
-                d = found[plane][top : top + height, left + half : left + grid_len]
+                top = 2 * (plane * group + band) * height
+                a = found[top : top + height, left : left + half]
+                d = found[top : top + height, left + half : left + grid_len]
                 top += height
-                c = found[plane][top : top + height, left : left + half]
-                b = found[plane][top : top + height, left + half : left + grid_len]
+                c = found[top : top + height, left : left + half]
+                b = found[top : top + height, left + half : left + grid_len]
                 with_cos += a * a + c * c
                 with_sin += b * b + d * d
                 mixed += c * d - a * b
@@ -418,7 +408,7 @@
     zero = jnp.zeros((height, half), jnp.float32)
     empty = [(zero, zero, zero)] * (2 * own_planes)
     groups = bands // group
-    if blocks * groups > 32:
+    if blocks * groups > 16:
 
         def one_block(block, carry):
             def one_group(index, sums):
@@ -473,7 +463,7 @@
             pltpu.SMEM(occupation.shape, jnp.int32),
             pltpu.VMEM((2, bands, in_count), jnp.bfloat16),
             pltpu.VMEM((2 * in_count * sticks, grid_len), jnp.bfloat16),
-            pltpu.VMEM((pw_count, message_rows, lanes), jnp.bfloat16),
+            pltpu.VMEM((devices, message_rows, lanes), jnp.bfloat16),
             pltpu.SemaphoreType.DMA((max(4 + COEFF_COPIES, band_count),)),
         ],
         compiler_params=room(2 * message_bytes),
@@ -509,7 +499,7 @@
         name="stick_tables",
     )(pltpu.with_memory_space_constraint(stick_column.reshape(1, stick_count), pltpu.HBM))
     norm_factor = 1.0 / float(bands * stick_count * grid_len)
-    blocks = 2 * own_planes * (grid_len // 2 // row_block(grid_len, stick_count))
+    blocks = 2 * own_planes * (grid_len // 2 // row_block(grid_len))
     return pl.pallas_call(
         functools.partial(plane_kernel, bands, own_planes, norm_factor, sticks),
         out_shape=jax.ShapeDtypeStruct((own_planes, grid_len, grid_len), jnp.float32),

time: 19.7 us -> 19.6 us (level)
  no operation moved by 1% of the time
where the time goes in v17:
time: 19.6 us; the launch traced here: 19.4 us
  starting transfers between devices  7.3 us (37%)
  Pallas kernels  6.21 us (32%)
  waiting for transfers between devices  5.89 us (30%)
    all_to_all x1, starting transfers between devices, shards(): lax.all_to_all(messages, ('band', 'pw'), split_axis=0, concat_axis=0, til...  7.3 us
    all_to_all x1, waiting for transfers between devices, shards(): lax.all_to_all(messages, ('band', 'pw'), split_axis=0, concat_axis=0, til...  5.89 us
    pallas_call x1, Pallas kernels, shards(): pl.pallas_call(functools.partial(plane_kernel, bands, own_planes, norm_fa...  2.54 us
    pallas_call x1, Pallas kernels, shards(): pl.pallas_call(stick_kernel, out_shape=jax.ShapeDtypeStruct((devices, mes...  2.38 us
    pallas_call x1, Pallas kernels, shards(): pl.pallas_call(functools.partial(table_kernel, grid_len, min(grid_len, st...  1.29 us
  transfers between devices with their start and end apart: 1, of which 1 were waited for; matrix products, arithmetic and copies ran while one was open for 0% of the time, Pallas kernels for 7%

profile of v17, /device:TPU:0, one launch (start us, length us, event | category | flops | bytes accessed | tf_op | source)
XLA Modules:
  0.0 19.4 jit_solution(12243669149148504974)
XLA Ops:
  0.0 2.4 %stick_values.1 = bf16[32,4,128]{2,1,0:T(4,128)(2,1)} custom-call(s32[256]{0:T(256)} %length_hbm.1, s32[16]{0:T(128)} %plane_hbm.1, s32[2]{0:T(128)} %occupation_hbm.1, bf16[2,8,64]{2,1,0:T(8,128)(2,1)} %bitcast.4, bf16[1024,256]{1,0:T(8,128)(2,1)} %bitcast.3), custom_call_target="tpu_custom_call" | custom-call | tf_op jit(solution)/shard_map/stick_values/pallas_call | solution.py:455
  2.4 7.3 %all-to-all-start = ((bf16[32,4,128]{2,1,0:T(4,128)(2,1)}), bf16[32,4,128]{2,1,0:T(4,128)(2,1)S(1)}, u32[]{:S(2)}, u32[]{:S(2)}) async-start(bf16[32,4,128]{2,1,0:T(4,128)(2,1)} %stick_values.1), calls=%async_computation | async-start | bytes 65536 | tf_op jit(solution)/shard_map/all_to_all | solution.py:483
  9.7 1.3 %stick_tables.1 = (bf16[2,128,256]{2,1,0:T(8,128)(2,1)S(1)}, bf16[256,512]{1,0:T(8,128)(2,1)S(1)}) custom-call(s32[1,256]{1,0:T(1,128)} %bitcast.5), custom_call_target="tpu_custom_call" | custom-call | flops 5242880 | bytes 786432 | tf_op jit(solution)/shard_map/stick_tables/pallas_call | solution.py:484
  11.0 5.9 %all-to-all-done.message_ref = bf16[32,4,128]{2,1,0:T(4,128)(2,1)S(1)} async-done(((bf16[32,4,128]{2,1,0:T(4,128)(2,1)}), bf16[32,4,128]{2,1,0:T(4,128)(2,1)S(1)}, u32[]{:S(2)}, u32[]{:S(2)}) %all-to-all-start) | async-done | bytes 32800 | tf_op jit(solution)/shard_map/all_to_all | solution.py:483
  16.9 2.5 %plane_density.1 = f32[2,256,256]{2,1,0:T(8,128)} custom-call(bf16[32,4,128]{2,1,0:T(4,128)(2,1)S(1)} %all-to-all-done.message_ref, bf16[2,128,256]{2,1,0:T(8,128)(2,1)S(1)} %get-tuple-element.7.left_ref, bf16[256,512]{1,0:T(8,128)(2,1)S(1)} %get-tuple-element.8.right_ref), custom_call_target="tpu_custom_call" | custom-call | tf_op jit(solution)/shard_map/plane_density/pallas_call | solution.py:503
Async XLA Ops:
  2.4 14.5 %all-to-all-start = ((bf16[32,4,128]{2,1,0:T(4,128)(2,1)}), bf16[32,4,128]{2,1,0:T(4,128)(2,1)S(1)}, u32[]{:S(2)}, u32[]{:S(2)}) async-start(bf16[32,4,128]{2,1,0:T(4,128)(2,1)} %stick_values.1), calls=%async_computation | async-start | bytes 65536 | tf_op jit(solution)/shard_map/all_to_all | solution.py:483

commit v18 on v17

--- a/solution.py
+++ b/solution.py
@@ -222,7 +222,7 @@
                 message = jnp.where(
                     iota((sticks, lanes), 1) < (index + 1) * spots, piece, message
                 )
-            message_ref[first_pw + place] = message[: sticks // side].astype(message_ref.dtype)
+            message_ref[wrap(pw_count - first_pw - place, pw_count)] = message[: sticks // side].astype(message_ref.dtype)
 
     if group_pw == pw_count:
         form = forms(0)
@@ -250,14 +250,15 @@
     shape = (chunk, chunk)
     to, rows = iota(shape, 1), sticks // side
     index, rest = lax.div(to, chunk // side), lax.rem(to, chunk // side)
-    source = lax.div(rest, rows) * sticks + index * rows + lax.rem(rest, rows)
+    device = chunk // sticks - 1 - lax.div(rest, rows)
+    source = device * sticks + index * rows + lax.rem(rest, rows)
     order = (iota(shape, 0) == source).astype(jnp.bfloat16)
     shape = (8, count)
-    columns = jnp.broadcast_to(columns, shape)
+    columns = pltpu.roll(jnp.broadcast_to(columns, shape), count - sticks, 1)
     halves = jnp.where(iota(shape, 0) == 0, cut(columns, grid_len), wrap(columns, grid_len))
     halves = halves.astype(jnp.float32).astype(jnp.bfloat16)
     ordered = [
-        dot(halves[:, first : first + chunk], order) for first in range(0, count, chunk)
+        dot(halves[:, first : first + chunk], order) for first in range(0, count, chunk)[::-1]
     ]
     ordered = jnp.concatenate(ordered, 1).astype(jnp.int32)
     return ordered[:1] * grid_len + ordered[1:2]
@@ -270,8 +271,7 @@
     count = column_ref.shape[1]
     half = grid_len // 2
     columns = column_ref[...]
-    if side > 1:
-        columns = reorder(columns, grid_len, chunk, sticks, side)
+    columns = reorder(columns, grid_len, chunk, sticks, side)
     turns = iota((half, count), 0) * cut(columns, grid_len)
     left_ref[0] = cosine(turns, grid_len).astype(jnp.bfloat16)
     left_ref[1] = sine(turns, grid_len).astype(jnp.bfloat16)
@@ -480,7 +480,14 @@
             )
         )
     )
-    arrived = lax.all_to_all(messages, ("band", "pw"), split_axis=0, concat_axis=0, tiled=True)
+    arrived = lax.all_to_all(
+        messages,
+        ("band", "pw"),
+        split_axis=0,
+        concat_axis=0,
+        axis_index_groups=[[0, *range(devices - 1, 0, -1)]],
+        tiled=True,
+    )
     left, right = pl.pallas_call(
         functools.partial(table_kernel, grid_len, min(grid_len, stick_count), sticks, side),
         out_shape=(

time: 19.6 us -> 19.7 us (level)
  no operation moved by 1% of the time
where the time goes in v18:
time: 19.7 us; the launch traced here: 19.5 us
  starting transfers between devices  7.3 us (37%)
  Pallas kernels  6.24 us (32%)
  waiting for transfers between devices  5.95 us (30%)
    all_to_all x1, starting transfers between devices, shards(): lax.all_to_all(messages, ('band', 'pw'), split_axis=0, concat_axis=0, axi...  7.3 us
    all_to_all x1, waiting for transfers between devices, shards(): lax.all_to_all(messages, ('band', 'pw'), split_axis=0, concat_axis=0, axi...  5.95 us
    pallas_call x1, Pallas kernels, shards(): pl.pallas_call(functools.partial(plane_kernel, bands, own_planes, norm_fa...  2.54 us
    pallas_call x1, Pallas kernels, shards(): pl.pallas_call(stick_kernel, out_shape=jax.ShapeDtypeStruct((devices, mes...  2.38 us
    pallas_call x1, Pallas kernels, shards(): pl.pallas_call(functools.partial(table_kernel, grid_len, min(grid_len, st...  1.32 us
  transfers between devices with their start and end apart: 1, of which 1 were waited for; matrix products, arithmetic and copies ran while one was open for 0% of the time, Pallas kernels for 7%

profile of v18, /device:TPU:0, one launch (start us, length us, event | category | flops | bytes accessed | tf_op | source)
XLA Modules:
  0.0 19.5 jit_solution(14924790342842238411)
XLA Ops:
  0.0 2.4 %stick_values.1 = bf16[32,4,128]{2,1,0:T(4,128)(2,1)} custom-call(s32[256]{0:T(256)} %length_hbm.1, s32[16]{0:T(128)} %plane_hbm.1, s32[2]{0:T(128)} %occupation_hbm.1, bf16[2,8,64]{2,1,0:T(8,128)(2,1)} %bitcast.4, bf16[1024,256]{1,0:T(8,128)(2,1)} %bitcast.3), custom_call_target="tpu_custom_call" | custom-call | tf_op jit(solution)/shard_map/stick_values/pallas_call | solution.py:455
  2.4 7.3 %all-to-all-start = ((bf16[32,4,128]{2,1,0:T(4,128)(2,1)}), bf16[32,4,128]{2,1,0:T(4,128)(2,1)S(1)}, u32[]{:S(2)}, u32[]{:S(2)}) async-start(bf16[32,4,128]{2,1,0:T(4,128)(2,1)} %stick_values.1), calls=%async_computation | async-start | bytes 65536 | tf_op jit(solution)/shard_map/all_to_all | solution.py:483
  9.7 1.3 %stick_tables.1 = (bf16[2,128,256]{2,1,0:T(8,128)(2,1)S(1)}, bf16[256,512]{1,0:T(8,128)(2,1)S(1)}) custom-call(s32[1,256]{1,0:T(1,128)} %bitcast.5), custom_call_target="tpu_custom_call" | custom-call | flops 5242880 | bytes 786432 | tf_op jit(solution)/shard_map/stick_tables/pallas_call | solution.py:491
  11.0 6.0 %all-to-all-done.message_ref = bf16[32,4,128]{2,1,0:T(4,128)(2,1)S(1)} async-done(((bf16[32,4,128]{2,1,0:T(4,128)(2,1)}), bf16[32,4,128]{2,1,0:T(4,128)(2,1)S(1)}, u32[]{:S(2)}, u32[]{:S(2)}) %all-to-all-start) | async-done | bytes 32800 | tf_op jit(solution)/shard_map/all_to_all | solution.py:483
  17.0 2.5 %plane_density.1 = f32[2,256,256]{2,1,0:T(8,128)} custom-call(bf16[32,4,128]{2,1,0:T(4,128)(2,1)S(1)} %all-to-all-done.message_ref, bf16[2,128,256]{2,1,0:T(8,128)(2,1)S(1)} %get-tuple-element.7.left_ref, bf16[256,512]{1,0:T(8,128)(2,1)S(1)} %get-tuple-element.8.right_ref), custom_call_target="tpu_custom_call" | custom-call | tf_op jit(solution)/shard_map/plane_density/pallas_call | solution.py:510
Async XLA Ops:
  2.4 14.6 %all-to-all-start = ((bf16[32,4,128]{2,1,0:T(4,128)(2,1)}), bf16[32,4,128]{2,1,0:T(4,128)(2,1)S(1)}, u32[]{:S(2)}, u32[]{:S(2)}) async-start(bf16[32,4,128]{2,1,0:T(4,128)(2,1)} %stick_values.1), calls=%async_computation | async-start | bytes 65536 | tf_op jit(solution)/shard_map/all_to_all | solution.py:483

commit v19 on v17

--- a/solution.py
+++ b/solution.py
@@ -238,11 +238,16 @@
             return carry
 
         lax.fori_loop(0, pw_count // group_pw, one_group, 0)
-    for band in range(1, out_hbm.shape[0] // pw_count):
-        message_ref[band * pw_count : (band + 1) * pw_count] = message_ref[:pw_count]
-    copy = pltpu.make_async_copy(message_ref, out_hbm, sems.at[0])
-    copy.start()
-    copy.wait()
+    copies = [
+        pltpu.make_async_copy(
+            message_ref, out_hbm.at[pl.ds(band * pw_count, pw_count)], sems.at[band]
+        )
+        for band in range(out_hbm.shape[0] // pw_count)
+    ]
+    for copy in copies:
+        copy.start()
+    for copy in copies:
+        copy.wait()
 
 
 def reorder(columns, grid_len, chunk, sticks, side):
@@ -463,7 +468,7 @@
             pltpu.SMEM(occupation.shape, jnp.int32),
             pltpu.VMEM((2, bands, in_count), jnp.bfloat16),
             pltpu.VMEM((2 * in_count * sticks, grid_len), jnp.bfloat16),
-            pltpu.VMEM((devices, message_rows, lanes), jnp.bfloat16),
+            pltpu.VMEM((pw_count, message_rows, lanes), jnp.bfloat16),
             pltpu.SemaphoreType.DMA((max(4 + COEFF_COPIES, band_count),)),
         ],
         compiler_params=room(2 * message_bytes),

time: 19.6 us -> 19.6 us (level)
  no operation moved by 1% of the time
where the time goes in v19:
time: 19.6 us; the launch traced here: 19.4 us
  starting transfers between devices  7.3 us (37%)
  Pallas kernels  6.19 us (32%)
  waiting for transfers between devices  5.89 us (30%)
    all_to_all x1, starting transfers between devices, shards(): lax.all_to_all(messages, ('band', 'pw'), split_axis=0, concat_axis=0, til...  7.3 us
    all_to_all x1, waiting for transfers between devices, shards(): lax.all_to_all(messages, ('band', 'pw'), split_axis=0, concat_axis=0, til...  5.89 us
    pallas_call x1, Pallas kernels, shards(): pl.pallas_call(functools.partial(plane_kernel, bands, own_planes, norm_fa...  2.54 us
    pallas_call x1, Pallas kernels, shards(): pl.pallas_call(stick_kernel, out_shape=jax.ShapeDtypeStruct((devices, mes...  2.37 us
    pallas_call x1, Pallas kernels, shards(): pl.pallas_call(functools.partial(table_kernel, grid_len, min(grid_len, st...  1.29 us
  transfers between devices with their start and end apart: 1, of which 1 were waited for; matrix products, arithmetic and copies ran while one was open for 0% of the time, Pallas kernels for 7%

profile of v19, /device:TPU:0, one launch (start us, length us, event | category | flops | bytes accessed | tf_op | source)
XLA Modules:
  0.0 19.4 jit_solution(11732548644814689025)
XLA Ops:
  0.0 2.4 %stick_values.1 = bf16[32,4,128]{2,1,0:T(4,128)(2,1)} custom-call(s32[256]{0:T(256)} %length_hbm.1, s32[16]{0:T(128)} %plane_hbm.1, s32[2]{0:T(128)} %occupation_hbm.1, bf16[2,8,64]{2,1,0:T(8,128)(2,1)} %bitcast.4, bf16[1024,256]{1,0:T(8,128)(2,1)} %bitcast.3), custom_call_target="tpu_custom_call" | custom-call | tf_op jit(solution)/shard_map/stick_values/pallas_call | solution.py:460
  2.4 7.3 %all-to-all-start = ((bf16[32,4,128]{2,1,0:T(4,128)(2,1)}), bf16[32,4,128]{2,1,0:T(4,128)(2,1)S(1)}, u32[]{:S(2)}, u32[]{:S(2)}) async-start(bf16[32,4,128]{2,1,0:T(4,128)(2,1)} %stick_values.1), calls=%async_computation | async-start | bytes 65536 | tf_op jit(solution)/shard_map/all_to_all | solution.py:488
  9.7 1.3 %stick_tables.1 = (bf16[2,128,256]{2,1,0:T(8,128)(2,1)S(1)}, bf16[256,512]{1,0:T(8,128)(2,1)S(1)}) custom-call(s32[1,256]{1,0:T(1,128)} %bitcast.5), custom_call_target="tpu_custom_call" | custom-call | flops 5242880 | bytes 786432 | tf_op jit(solution)/shard_map/stick_tables/pallas_call | solution.py:489
  11.0 5.9 %all-to-all-done.message_ref = bf16[32,4,128]{2,1,0:T(4,128)(2,1)S(1)} async-done(((bf16[32,4,128]{2,1,0:T(4,128)(2,1)}), bf16[32,4,128]{2,1,0:T(4,128)(2,1)S(1)}, u32[]{:S(2)}, u32[]{:S(2)}) %all-to-all-start) | async-done | bytes 32800 | tf_op jit(solution)/shard_map/all_to_all | solution.py:488
  16.9 2.5 %plane_density.1 = f32[2,256,256]{2,1,0:T(8,128)} custom-call(bf16[32,4,128]{2,1,0:T(4,128)(2,1)S(1)} %all-to-all-done.message_ref, bf16[2,128,256]{2,1,0:T(8,128)(2,1)S(1)} %get-tuple-element.7.left_ref, bf16[256,512]{1,0:T(8,128)(2,1)S(1)} %get-tuple-element.8.right_ref), custom_call_target="tpu_custom_call" | custom-call | tf_op jit(solution)/shard_map/plane_density/pallas_call | solution.py:508
Async XLA Ops:
  2.4 14.5 %all-to-all-start = ((bf16[32,4,128]{2,1,0:T(4,128)(2,1)}), bf16[32,4,128]{2,1,0:T(4,128)(2,1)S(1)}, u32[]{:S(2)}, u32[]{:S(2)}) async-start(bf16[32,4,128]{2,1,0:T(4,128)(2,1)} %stick_values.1), calls=%async_computation | async-start | bytes 65536 | tf_op jit(solution)/shard_map/all_to_all | solution.py:488
